TPU v7x, 256 devices: a whole 4x4x8 slice. The times are simulated.
256 devices in a mesh: cand: 128 (over x, z, y_lo, core), tok: 2 (over y_hi).
Axes of the slice: x: 4, y: 4 (y_hi: 2, y_lo: 2; y = y_hi * 2 + y_lo), z: 8, core: 2. Of those that a mesh axis runs over, the one named last changes fastest.
Arguments:
- embeddings: bfloat16 [128, 512, 1024], P('cand', 'tok')
- lengths: int32 [128], replicated, may hold values from 64 to 512, as said below
Outputs:
- utility: float32 [128, 24], P('cand')
Inputs may be any that keep to these rules, and one draw needn't show every extreme that they name: The first lengths[c] token rows of candidate c are its tokens; the others are padding. Some candidate has all 512 slots valid.
All inputs are finite; a program needn't handle non-finite values.
Results may differ from a plain program's by a relative error of at most 0.0003.
Values may be sent and summed in bfloat16 or wider, within the bound.
No kernel may reach another device: no remote copies, remote signals or barrier semaphores. Data moves between devices by JAX's collectives and lax.ppermute only.
A program may use at most 64 MiB of HBM per device.

v0:
```python
import jax
import jax.numpy as jnp
from jax import lax
from jax.sharding import PartitionSpec as P

STEPS = 12


def passed_along(value, axis, steps):
    count = lax.axis_size(axis)
    pairs = [(source, (source + steps) % count) for source in range(count)]
    return lax.ppermute(value, axis, pairs)


def normalize(emb):
    values = emb.astype(jnp.float32)
    factor = lax.rsqrt(jnp.sum(values * values, axis=-1, keepdims=True) + 1e-06)
    return (values * factor).astype(jnp.bfloat16)


def on_device(embeddings, lengths):
    normed_half = normalize(embeddings)
    per_dev = normed_half.shape[0]
    half_rows = normed_half.shape[1]
    cand_count = lax.axis_size("cand")
    device = lax.axis_index("cand")
    tok_index = lax.axis_index("tok")
    half_pos = tok_index * half_rows + jnp.arange(half_rows, dtype=jnp.int32)
    full_pos = jnp.arange(half_rows * lax.axis_size("tok"), dtype=jnp.int32)
    own_len = lax.dynamic_slice_in_dim(lengths, device * per_dev, per_dev, 0)
    own_lenf = own_len.astype(jnp.float32)
    own_full = lax.all_gather(normed_half, "tok", axis=1, tiled=True)
    own_valid = full_pos[None, :] < own_len[:, None]
    current = normed_half
    forward_list = []
    backward_list = []
    for offset in range(1, STEPS + 1):
        current = passed_along(current, "cand", -1)
        partner = jnp.remainder(device + offset, cand_count)
        peer_len = lax.dynamic_slice_in_dim(lengths, partner * per_dev, per_dev, 0)
        peer_lenf = peer_len.astype(jnp.float32)
        peer_valid = half_pos[None, :] < peer_len[:, None]
        sims = jnp.einsum("ale,bme->ablm", own_full, current, preferred_element_type=jnp.float32)
        row_part = jnp.max(jnp.where(peer_valid[None, :, None, :], sims, -3.0), axis=3)
        colbest = jnp.max(jnp.where(own_valid[:, None, :, None], sims, -3.0), axis=2)
        recall_part = jnp.sum(jnp.where(peer_valid[None, :, :], colbest, 0.0), axis=2)
        rowbest = lax.pmax(row_part, "tok")
        recall_sum = lax.psum(recall_part, "tok")
        precision = (
            jnp.sum(jnp.where(own_valid[:, None, :], rowbest, 0.0), axis=2) / own_lenf[:, None]
        )
        recall = recall_sum / peer_lenf[None, :]
        scores = 0.5 * (precision + recall)
        forward_list.append(scores)
        arrived = passed_along(scores, "cand", offset)
        backward_list.append(arrived.T)
    forward = jnp.stack(forward_list, axis=1).reshape(per_dev, STEPS * per_dev)
    backward = jnp.stack(backward_list, axis=1).reshape(per_dev, STEPS * per_dev)
    return jnp.concatenate([forward, backward], axis=1)


def solution(mesh):
    in_specs = (P("cand", "tok", None), P())
    out_specs = P("cand", None)
    return jax.shard_map(
        on_device, mesh=mesh, in_specs=in_specs, out_specs=out_specs, check_vma=False
    )
```

profile of v0, /device:TPU:4, one launch (start us, length us, event | category | flops | bytes accessed | tf_op | source)
XLA Modules:
  0.0 269.0 jit_solution(8647242641543110872)
XLA Ops:
  8.0 6.4 %collective-permute-start = (bf16[1,256,1024]{2,1,0:T(8,128)(2,1)S(1)}, bf16[1,256,1024]{2,1,0:T(8,128)(2,1)S(1)}, u32[]{:S(2)}, u32[]{:S(2)}) collective-permute-start(bf16[1,256,1024]{2,1,0:T(8,128)(2,1)S(1)} %fusion.1), channel_id=1, source_target_pairs={{0,254},{2,0},{4,2},{6,4},{8,6},{10,8},{12,10},{14,12},{16,14},{18... | collective-permute-start | bytes 1572872 | tf_op jit(solution)/shard_map/ppermute | solution.py:12
  14.4 6.7 %collective-permute-done = bf16[1,256,1024]{2,1,0:T(8,128)(2,1)S(1)} collective-permute-done((bf16[1,256,1024]{2,1,0:T(8,128)(2,1)S(1)}, bf16[1,256,1024]{2,1,0:T(8,128)(2,1)S(1)}, u32[]{:S(2)}, u32[]{:S(2)}) %collective-permute-start) | collective-permute-done | bytes 524320 | tf_op jit(solution)/shard_map/ppermute | solution.py:12
  21.1 4.9 %collective-permute-start.1 = (bf16[1,256,1024]{2,1,0:T(8,128)(2,1)S(1)}, bf16[1,256,1024]{2,1,0:T(8,128)(2,1)S(1)}, u32[]{:S(2)}, u32[]{:S(2)}) collective-permute-start(bf16[1,256,1024]{2,1,0:T(8,128)(2,1)S(1)} %collective-permute-done), channel_id=1, source_target_pairs={{0,254},{2,0},{4,2},{6,4},{8,6},{10,8},{12,10},{14,12},{16,14},{18... | collective-permute-start | bytes 1572872 | tf_op jit(solution)/shard_map/ppermute | solution.py:12
  26.0 6.7 %collective-permute-done.1 = bf16[1,256,1024]{2,1,0:T(8,128)(2,1)S(1)} collective-permute-done((bf16[1,256,1024]{2,1,0:T(8,128)(2,1)S(1)}, bf16[1,256,1024]{2,1,0:T(8,128)(2,1)S(1)}, u32[]{:S(2)}, u32[]{:S(2)}) %collective-permute-start.1) | collective-permute-done | bytes 524320 | tf_op jit(solution)/shard_map/ppermute | solution.py:12
  32.7 4.9 %collective-permute-start.2 = (bf16[1,256,1024]{2,1,0:T(8,128)(2,1)S(1)}, bf16[1,256,1024]{2,1,0:T(8,128)(2,1)S(1)}, u32[]{:S(2)}, u32[]{:S(2)}) collective-permute-start(bf16[1,256,1024]{2,1,0:T(8,128)(2,1)S(1)} %collective-permute-done.1), channel_id=1, source_target_pairs={{0,254},{2,0},{4,2},{6,4},{8,6},{10,8},{12,10},{14,12},{16,14},{18... | collective-permute-start | bytes 1572872 | tf_op jit(solution)/shard_map/ppermute | solution.py:12
  37.6 6.7 %collective-permute-done.2 = bf16[1,256,1024]{2,1,0:T(8,128)(2,1)S(1)} collective-permute-done((bf16[1,256,1024]{2,1,0:T(8,128)(2,1)S(1)}, bf16[1,256,1024]{2,1,0:T(8,128)(2,1)S(1)}, u32[]{:S(2)}, u32[]{:S(2)}) %collective-permute-start.2) | collective-permute-done | bytes 524320 | tf_op jit(solution)/shard_map/ppermute | solution.py:12
  44.3 4.9 %collective-permute-start.3 = (bf16[1,256,1024]{2,1,0:T(8,128)(2,1)S(1)}, bf16[1,256,1024]{2,1,0:T(8,128)(2,1)S(1)}, u32[]{:S(2)}, u32[]{:S(2)}) collective-permute-start(bf16[1,256,1024]{2,1,0:T(8,128)(2,1)S(1)} %collective-permute-done.2), channel_id=1, source_target_pairs={{0,254},{2,0},{4,2},{6,4},{8,6},{10,8},{12,10},{14,12},{16,14},{18... | collective-permute-start | bytes 1572872 | tf_op jit(solution)/shard_map/ppermute | solution.py:12
  49.2 6.7 %collective-permute-done.3 = bf16[1,256,1024]{2,1,0:T(8,128)(2,1)S(1)} collective-permute-done((bf16[1,256,1024]{2,1,0:T(8,128)(2,1)S(1)}, bf16[1,256,1024]{2,1,0:T(8,128)(2,1)S(1)}, u32[]{:S(2)}, u32[]{:S(2)}) %collective-permute-start.3) | collective-permute-done | bytes 524320 | tf_op jit(solution)/shard_map/ppermute | solution.py:12
  55.9 4.9 %collective-permute-start.4 = (bf16[1,256,1024]{2,1,0:T(8,128)(2,1)S(1)}, bf16[1,256,1024]{2,1,0:T(8,128)(2,1)S(1)}, u32[]{:S(2)}, u32[]{:S(2)}) collective-permute-start(bf16[1,256,1024]{2,1,0:T(8,128)(2,1)S(1)} %collective-permute-done.3), channel_id=1, source_target_pairs={{0,254},{2,0},{4,2},{6,4},{8,6},{10,8},{12,10},{14,12},{16,14},{18... | collective-permute-start | bytes 1572872 | tf_op jit(solution)/shard_map/ppermute | solution.py:12
  60.8 6.7 %collective-permute-done.4 = bf16[1,256,1024]{2,1,0:T(8,128)(2,1)S(1)} collective-permute-done((bf16[1,256,1024]{2,1,0:T(8,128)(2,1)S(1)}, bf16[1,256,1024]{2,1,0:T(8,128)(2,1)S(1)}, u32[]{:S(2)}, u32[]{:S(2)}) %collective-permute-start.4) | collective-permute-done | bytes 524320 | tf_op jit(solution)/shard_map/ppermute | solution.py:12
  67.5 4.9 %collective-permute-start.5 = (bf16[1,256,1024]{2,1,0:T(8,128)(2,1)S(1)}, bf16[1,256,1024]{2,1,0:T(8,128)(2,1)}, u32[]{:S(2)}, u32[]{:S(2)}) collective-permute-start(bf16[1,256,1024]{2,1,0:T(8,128)(2,1)S(1)} %collective-permute-done.4), channel_id=1, source_target_pairs={{0,254},{2,0},{4,2},{6,4},{8,6},{10,8},{12,10},{14,12},{16,14},{18... | collective-permute-start | bytes 1572872 | tf_op jit(solution)/shard_map/ppermute | solution.py:12
  79.2 5.0 %collective-permute-start.6 = (bf16[1,256,1024]{2,1,0:T(8,128)(2,1)}, bf16[1,256,1024]{2,1,0:T(8,128)(2,1)S(1)}, u32[]{:S(2)}, u32[]{:S(2)}) collective-permute-start(bf16[1,256,1024]{2,1,0:T(8,128)(2,1)} %collective-permute-done.5), channel_id=1, source_target_pairs={{0,254},{2,0},{4,2},{6,4},{8,6},{10,8},{12,10},{14,12},{16,14},{18... | collective-permute-start | bytes 1572872 | tf_op jit(solution)/shard_map/ppermute | solution.py:12
  102.8 5.1 %collective-permute-start.8 = (bf16[1,256,1024]{2,1,0:T(8,128)(2,1)}, bf16[1,256,1024]{2,1,0:T(8,128)(2,1)}, u32[]{:S(2)}, u32[]{:S(2)}) collective-permute-start(bf16[1,256,1024]{2,1,0:T(8,128)(2,1)} %collective-permute-done.7), channel_id=1, source_target_pairs={{0,254},{2,0},{4,2},{6,4},{8,6},{10,8},{12,10},{14,12},{16,14},{18... | collective-permute-start | bytes 1572872 | tf_op jit(solution)/shard_map/ppermute | solution.py:12
  110.8 4.2 %collective-permute-done.8 = bf16[1,256,1024]{2,1,0:T(8,128)(2,1)} collective-permute-done((bf16[1,256,1024]{2,1,0:T(8,128)(2,1)}, bf16[1,256,1024]{2,1,0:T(8,128)(2,1)}, u32[]{:S(2)}, u32[]{:S(2)}) %collective-permute-start.8) | collective-permute-done | bytes 524320 | tf_op jit(solution)/shard_map/ppermute | solution.py:12
  114.9 4.9 %collective-permute-start.9 = (bf16[1,256,1024]{2,1,0:T(8,128)(2,1)}, bf16[1,256,1024]{2,1,0:T(8,128)(2,1)S(1)}, u32[]{:S(2)}, u32[]{:S(2)}) collective-permute-start(bf16[1,256,1024]{2,1,0:T(8,128)(2,1)} %collective-permute-done.8), channel_id=1, source_target_pairs={{0,254},{2,0},{4,2},{6,4},{8,6},{10,8},{12,10},{14,12},{16,14},{18... | collective-permute-start | bytes 1572872 | tf_op jit(solution)/shard_map/ppermute | solution.py:12
  122.3 4.5 %collective-permute-done.9 = bf16[1,256,1024]{2,1,0:T(8,128)(2,1)S(1)} collective-permute-done((bf16[1,256,1024]{2,1,0:T(8,128)(2,1)}, bf16[1,256,1024]{2,1,0:T(8,128)(2,1)S(1)}, u32[]{:S(2)}, u32[]{:S(2)}) %collective-permute-start.9) | collective-permute-done | bytes 524320 | tf_op jit(solution)/shard_map/ppermute | solution.py:12
  126.9 4.8 %collective-permute-start.10 = (bf16[1,256,1024]{2,1,0:T(8,128)(2,1)S(1)}, bf16[1,256,1024]{2,1,0:T(8,128)(2,1)S(1)}, u32[]{:S(2)}, u32[]{:S(2)}) collective-permute-start(bf16[1,256,1024]{2,1,0:T(8,128)(2,1)S(1)} %collective-permute-done.9), channel_id=1, source_target_pairs={{0,254},{2,0},{4,2},{6,4},{8,6},{10,8},{12,10},{14,12},{16,14},{18... | collective-permute-start | bytes 1572872 | tf_op jit(solution)/shard_map/ppermute | solution.py:12
  138.4 4.9 %collective-permute-start.11 = (bf16[1,256,1024]{2,1,0:T(8,128)(2,1)S(1)}, bf16[1,256,1024]{2,1,0:T(8,128)(2,1)S(1)}, u32[]{:S(2)}, u32[]{:S(2)}) collective-permute-start(bf16[1,256,1024]{2,1,0:T(8,128)(2,1)S(1)} %collective-permute-done.10), channel_id=1, source_target_pairs={{0,254},{2,0},{4,2},{6,4},{8,6},{10,8},{12,10},{14,12},{16,14},{18... | collective-permute-start | bytes 1572872 | tf_op jit(solution)/shard_map/ppermute | solution.py:12
  153.0 11.2 %all-reduce.1 = (f32[1,1,512]{2,1,0:T(1,128)S(1)}, f32[1,1,512]{2,1,0:T(1,128)S(1)}, f32[1,1,512]{2,1,0:T(1,128)S(1)}, f32[1,1,512]{2,1,0:T(1,128)S(1)}, f32[1,1...) all-reduce(f32[1,1,512]{2,1,0:T(1,128)S(1)} %bitcast.229, ...), channel_id=1, replica_groups=mesh['cand'=128,'tok'=2] {'tok'}, use_global_device_ids=true, to_apply=%region_2.3 | all-reduce | flops 6144 | bytes 49152 | tf_op jit(solution)/shard_map/pmax | solution.py:47
  173.6 7.2 %all-reduce = (f32[1,1]{1,0:T(1,128)}, f32[1,1]{1,0:T(1,128)}, f32[1,1]{1,0:T(1,128)}, f32[1,1]{1,0:T(1,128)}, f32[1,1]{1,0:T(1,128)}, /*index=5*/f32[1,1]{1,0:T...) all-reduce(f32[1,1]{1,0:T(1,128)} %bitcast.8, ...), channel_id=1, replica_groups=mesh['cand'=128,'tok'=2] {'tok'}, use_global_device_ids=true, to_apply=%region_6.7 | all-reduce | flops 12 | bytes 96 | tf_op jit(solution)/shard_map/psum | solution.py:48
  212.2 9.5 %collective-permute-start.19 = (f32[1,1]{1,0:T(1,128)}, f32[1,1]{1,0:T(1,128)}, u32[]{:S(2)}, u32[]{:S(2)}) collective-permute-start(f32[1,1]{1,0:T(1,128)} %mul.61), channel_id=1, source_target_pairs={{0,16},{2,18},{4,20},{6,22},{8,24},{10,26},{12,28},{14,30},{16,32}... | collective-permute-start | bytes 20 | tf_op jit(solution)/shard_map/ppermute | solution.py:12
  224.8 21.8 %collective-permute-start.22 = (f32[1,1]{1,0:T(1,128)}, f32[1,1]{1,0:T(1,128)}, u32[]{:S(2)}, u32[]{:S(2)}) collective-permute-start(f32[1,1]{1,0:T(1,128)} %mul.64), channel_id=1, source_target_pairs={{0,22},{2,24},{4,26},{6,28},{8,30},{10,32},{12,34},{14,36},{16,38}... | collective-permute-start | bytes 20 | tf_op jit(solution)/shard_map/ppermute | solution.py:12
  248.2 5.8 %collective-permute-done.23 = f32[1,1]{1,0:T(1,128)} collective-permute-done((f32[1,1]{1,0:T(1,128)}, f32[1,1]{1,0:T(1,128)}, u32[]{:S(2)}, u32[]{:S(2)}) %collective-permute-start.23) | collective-permute-done | bytes 36 | tf_op jit(solution)/shard_map/ppermute | solution.py:12
  254.0 7.5 %stack.55 = f32[1,12,1]{1,2,0:T(1,128)S(1)} concatenate(f32[1,1,1]{1,2,0:T(1,128)} %bitcast.112, f32[1,1,1]{1,2,0:T(1,128)} %bitcast.114, f32[1,1,1]{1,2,0:T(1,128)} %bitcast.116, f32[1,1,1]{1,2,0:T(1,128)} %bitcast.118, f32[1,1,1]{1,2,0:T(1,128)} %bitcast.120, f32[1,1,1]{1,2,0:T(1,128)} %bitcast.122, f32[1,1,1]{1,2,0:T(1,128)} %bitcast.124, f32[1,1,1]{1,2,0:T(1,128)} %bitcast.126, ...), dimensions={1} | concatenate | bytes 96 | tf_op jit(solution)/shard_map/stack | solution.py:58
  (82 shorter events, 70.9 us)
Async XLA Ops:
  6.5 101.5 %all-gather.2.cloned.1.call-start = ((), (), s32[]{:S(2)}) async-start(), calls=%async_computation | async-start | bytes 1572864 | tf_op jit(solution)/shard_map/all_gather | solution.py:32
  8.0 13.1 %collective-permute-start = (bf16[1,256,1024]{2,1,0:T(8,128)(2,1)S(1)}, bf16[1,256,1024]{2,1,0:T(8,128)(2,1)S(1)}, u32[]{:S(2)}, u32[]{:S(2)}) collective-permute-start(bf16[1,256,1024]{2,1,0:T(8,128)(2,1)S(1)} %fusion.1), channel_id=1, source_target_pairs={{0,254},{2,0},{4,2},{6,4},{8,6},{10,8},{12,10},{14,12},{16,14},{18... | collective-permute-start | bytes 1572872 | tf_op jit(solution)/shard_map/ppermute | solution.py:12
  21.1 11.6 %collective-permute-start.1 = (bf16[1,256,1024]{2,1,0:T(8,128)(2,1)S(1)}, bf16[1,256,1024]{2,1,0:T(8,128)(2,1)S(1)}, u32[]{:S(2)}, u32[]{:S(2)}) collective-permute-start(bf16[1,256,1024]{2,1,0:T(8,128)(2,1)S(1)} %collective-permute-done), channel_id=1, source_target_pairs={{0,254},{2,0},{4,2},{6,4},{8,6},{10,8},{12,10},{14,12},{16,14},{18... | collective-permute-start | bytes 1572872 | tf_op jit(solution)/shard_map/ppermute | solution.py:12
  32.7 11.6 %collective-permute-start.2 = (bf16[1,256,1024]{2,1,0:T(8,128)(2,1)S(1)}, bf16[1,256,1024]{2,1,0:T(8,128)(2,1)S(1)}, u32[]{:S(2)}, u32[]{:S(2)}) collective-permute-start(bf16[1,256,1024]{2,1,0:T(8,128)(2,1)S(1)} %collective-permute-done.1), channel_id=1, source_target_pairs={{0,254},{2,0},{4,2},{6,4},{8,6},{10,8},{12,10},{14,12},{16,14},{18... | collective-permute-start | bytes 1572872 | tf_op jit(solution)/shard_map/ppermute | solution.py:12
  44.3 11.6 %collective-permute-start.3 = (bf16[1,256,1024]{2,1,0:T(8,128)(2,1)S(1)}, bf16[1,256,1024]{2,1,0:T(8,128)(2,1)S(1)}, u32[]{:S(2)}, u32[]{:S(2)}) collective-permute-start(bf16[1,256,1024]{2,1,0:T(8,128)(2,1)S(1)} %collective-permute-done.2), channel_id=1, source_target_pairs={{0,254},{2,0},{4,2},{6,4},{8,6},{10,8},{12,10},{14,12},{16,14},{18... | collective-permute-start | bytes 1572872 | tf_op jit(solution)/shard_map/ppermute | solution.py:12
  55.9 11.6 %collective-permute-start.4 = (bf16[1,256,1024]{2,1,0:T(8,128)(2,1)S(1)}, bf16[1,256,1024]{2,1,0:T(8,128)(2,1)S(1)}, u32[]{:S(2)}, u32[]{:S(2)}) collective-permute-start(bf16[1,256,1024]{2,1,0:T(8,128)(2,1)S(1)} %collective-permute-done.3), channel_id=1, source_target_pairs={{0,254},{2,0},{4,2},{6,4},{8,6},{10,8},{12,10},{14,12},{16,14},{18... | collective-permute-start | bytes 1572872 | tf_op jit(solution)/shard_map/ppermute | solution.py:12
  67.5 11.6 %collective-permute-start.5 = (bf16[1,256,1024]{2,1,0:T(8,128)(2,1)S(1)}, bf16[1,256,1024]{2,1,0:T(8,128)(2,1)}, u32[]{:S(2)}, u32[]{:S(2)}) collective-permute-start(bf16[1,256,1024]{2,1,0:T(8,128)(2,1)S(1)} %collective-permute-done.4), channel_id=1, source_target_pairs={{0,254},{2,0},{4,2},{6,4},{8,6},{10,8},{12,10},{14,12},{16,14},{18... | collective-permute-start | bytes 1572872 | tf_op jit(solution)/shard_map/ppermute | solution.py:12
  79.2 16.3 %collective-permute-start.6 = (bf16[1,256,1024]{2,1,0:T(8,128)(2,1)}, bf16[1,256,1024]{2,1,0:T(8,128)(2,1)S(1)}, u32[]{:S(2)}, u32[]{:S(2)}) collective-permute-start(bf16[1,256,1024]{2,1,0:T(8,128)(2,1)} %collective-permute-done.5), channel_id=1, source_target_pairs={{0,254},{2,0},{4,2},{6,4},{8,6},{10,8},{12,10},{14,12},{16,14},{18... | collective-permute-start | bytes 1572872 | tf_op jit(solution)/shard_map/ppermute | solution.py:12
  102.8 12.1 %collective-permute-start.8 = (bf16[1,256,1024]{2,1,0:T(8,128)(2,1)}, bf16[1,256,1024]{2,1,0:T(8,128)(2,1)}, u32[]{:S(2)}, u32[]{:S(2)}) collective-permute-start(bf16[1,256,1024]{2,1,0:T(8,128)(2,1)} %collective-permute-done.7), channel_id=1, source_target_pairs={{0,254},{2,0},{4,2},{6,4},{8,6},{10,8},{12,10},{14,12},{16,14},{18... | collective-permute-start | bytes 1572872 | tf_op jit(solution)/shard_map/ppermute | solution.py:12
  114.9 11.9 %collective-permute-start.9 = (bf16[1,256,1024]{2,1,0:T(8,128)(2,1)}, bf16[1,256,1024]{2,1,0:T(8,128)(2,1)S(1)}, u32[]{:S(2)}, u32[]{:S(2)}) collective-permute-start(bf16[1,256,1024]{2,1,0:T(8,128)(2,1)} %collective-permute-done.8), channel_id=1, source_target_pairs={{0,254},{2,0},{4,2},{6,4},{8,6},{10,8},{12,10},{14,12},{16,14},{18... | collective-permute-start | bytes 1572872 | tf_op jit(solution)/shard_map/ppermute | solution.py:12
  126.9 11.5 %collective-permute-start.10 = (bf16[1,256,1024]{2,1,0:T(8,128)(2,1)S(1)}, bf16[1,256,1024]{2,1,0:T(8,128)(2,1)S(1)}, u32[]{:S(2)}, u32[]{:S(2)}) collective-permute-start(bf16[1,256,1024]{2,1,0:T(8,128)(2,1)S(1)} %collective-permute-done.9), channel_id=1, source_target_pairs={{0,254},{2,0},{4,2},{6,4},{8,6},{10,8},{12,10},{14,12},{16,14},{18... | collective-permute-start | bytes 1572872 | tf_op jit(solution)/shard_map/ppermute | solution.py:12
  138.4 11.6 %collective-permute-start.11 = (bf16[1,256,1024]{2,1,0:T(8,128)(2,1)S(1)}, bf16[1,256,1024]{2,1,0:T(8,128)(2,1)S(1)}, u32[]{:S(2)}, u32[]{:S(2)}) collective-permute-start(bf16[1,256,1024]{2,1,0:T(8,128)(2,1)S(1)} %collective-permute-done.10), channel_id=1, source_target_pairs={{0,254},{2,0},{4,2},{6,4},{8,6},{10,8},{12,10},{14,12},{16,14},{18... | collective-permute-start | bytes 1572872 | tf_op jit(solution)/shard_map/ppermute | solution.py:12
  181.5 26.8 %collective-permute-start.12 = (f32[1,1]{1,0:T(1,128)}, f32[1,1]{1,0:T(1,128)}, u32[]{:S(2)}, u32[]{:S(2)}) collective-permute-start(f32[1,1]{1,0:T(1,128)} %mul.54), channel_id=1, source_target_pairs={{0,2},{2,4},{4,6},{6,8},{8,10},{10,12},{12,14},{14,16},{16,18},{18... | collective-permute-start | bytes 20 | tf_op jit(solution)/shard_map/ppermute | solution.py:12
  183.7 26.0 %collective-permute-start.13 = (f32[1,1]{1,0:T(1,128)}, f32[1,1]{1,0:T(1,128)}, u32[]{:S(2)}, u32[]{:S(2)}) collective-permute-start(f32[1,1]{1,0:T(1,128)} %mul.55), channel_id=1, source_target_pairs={{0,4},{2,6},{4,8},{6,10},{8,12},{10,14},{12,16},{14,18},{16,20},{1... | collective-permute-start | bytes 20 | tf_op jit(solution)/shard_map/ppermute | solution.py:12
  187.6 24.6 %collective-permute-start.14 = (f32[1,1]{1,0:T(1,128)}, f32[1,1]{1,0:T(1,128)}, u32[]{:S(2)}, u32[]{:S(2)}) collective-permute-start(f32[1,1]{1,0:T(1,128)} %mul.56), channel_id=1, source_target_pairs={{0,6},{2,8},{4,10},{6,12},{8,14},{10,16},{12,18},{14,20},{16,22},{... | collective-permute-start | bytes 20 | tf_op jit(solution)/shard_map/ppermute | solution.py:12
  190.3 31.4 %collective-permute-start.15 = (f32[1,1]{1,0:T(1,128)}, f32[1,1]{1,0:T(1,128)}, u32[]{:S(2)}, u32[]{:S(2)}) collective-permute-start(f32[1,1]{1,0:T(1,128)} %mul.57), channel_id=1, source_target_pairs={{0,8},{2,10},{4,12},{6,14},{8,16},{10,18},{12,20},{14,22},{16,24},... | collective-permute-start | bytes 20 | tf_op jit(solution)/shard_map/ppermute | solution.py:12
  194.1 28.9 %collective-permute-start.16 = (f32[1,1]{1,0:T(1,128)}, f32[1,1]{1,0:T(1,128)}, u32[]{:S(2)}, u32[]{:S(2)}) collective-permute-start(f32[1,1]{1,0:T(1,128)} %mul.58), channel_id=1, source_target_pairs={{0,10},{2,12},{4,14},{6,16},{8,18},{10,20},{12,22},{14,24},{16,26}... | collective-permute-start | bytes 20 | tf_op jit(solution)/shard_map/ppermute | solution.py:12
  208.3 16.5 %collective-permute-start.17 = (f32[1,1]{1,0:T(1,128)}, f32[1,1]{1,0:T(1,128)}, u32[]{:S(2)}, u32[]{:S(2)}) collective-permute-start(f32[1,1]{1,0:T(1,128)} %mul.59), channel_id=1, source_target_pairs={{0,12},{2,14},{4,16},{6,18},{8,20},{10,22},{12,24},{14,26},{16,28}... | collective-permute-start | bytes 20 | tf_op jit(solution)/shard_map/ppermute | solution.py:12
  209.7 36.9 %collective-permute-start.18 = (f32[1,1]{1,0:T(1,128)}, f32[1,1]{1,0:T(1,128)}, u32[]{:S(2)}, u32[]{:S(2)}) collective-permute-start(f32[1,1]{1,0:T(1,128)} %mul.60), channel_id=1, source_target_pairs={{0,14},{2,16},{4,18},{6,20},{8,22},{10,24},{12,26},{14,28},{16,30}... | collective-permute-start | bytes 20 | tf_op jit(solution)/shard_map/ppermute | solution.py:12
  212.2 36.0 %collective-permute-start.19 = (f32[1,1]{1,0:T(1,128)}, f32[1,1]{1,0:T(1,128)}, u32[]{:S(2)}, u32[]{:S(2)}) collective-permute-start(f32[1,1]{1,0:T(1,128)} %mul.61), channel_id=1, source_target_pairs={{0,16},{2,18},{4,20},{6,22},{8,24},{10,26},{12,28},{14,30},{16,32}... | collective-permute-start | bytes 20 | tf_op jit(solution)/shard_map/ppermute | solution.py:12
  221.7 26.5 %collective-permute-start.20 = (f32[1,1]{1,0:T(1,128)}, f32[1,1]{1,0:T(1,128)}, u32[]{:S(2)}, u32[]{:S(2)}) collective-permute-start(f32[1,1]{1,0:T(1,128)} %mul.62), channel_id=1, source_target_pairs={{0,18},{2,20},{4,22},{6,24},{8,26},{10,28},{12,30},{14,32},{16,34}... | collective-permute-start | bytes 20 | tf_op jit(solution)/shard_map/ppermute | solution.py:12
  223.0 25.2 %collective-permute-start.21 = (f32[1,1]{1,0:T(1,128)}, f32[1,1]{1,0:T(1,128)}, u32[]{:S(2)}, u32[]{:S(2)}) collective-permute-start(f32[1,1]{1,0:T(1,128)} %mul.63), channel_id=1, source_target_pairs={{0,20},{2,22},{4,24},{6,26},{8,28},{10,30},{12,32},{14,34},{16,36}... | collective-permute-start | bytes 20 | tf_op jit(solution)/shard_map/ppermute | solution.py:12
  224.8 23.3 %collective-permute-start.22 = (f32[1,1]{1,0:T(1,128)}, f32[1,1]{1,0:T(1,128)}, u32[]{:S(2)}, u32[]{:S(2)}) collective-permute-start(f32[1,1]{1,0:T(1,128)} %mul.64), channel_id=1, source_target_pairs={{0,22},{2,24},{4,26},{6,28},{8,30},{10,32},{12,34},{14,36},{16,38}... | collective-permute-start | bytes 20 | tf_op jit(solution)/shard_map/ppermute | solution.py:12
  246.6 7.4 %collective-permute-start.23 = (f32[1,1]{1,0:T(1,128)}, f32[1,1]{1,0:T(1,128)}, u32[]{:S(2)}, u32[]{:S(2)}) collective-permute-start(f32[1,1]{1,0:T(1,128)} %mul.65), channel_id=1, source_target_pairs={{0,24},{2,26},{4,28},{6,30},{8,32},{10,34},{12,36},{14,38},{16,40}... | collective-permute-start | bytes 20 | tf_op jit(solution)/shard_map/ppermute | solution.py:12
  (5 other events, 75.5 us)
Sparse Core Ops, SparseCore 0:
  72.6 35.3 all-gather.1
where the time goes:
time: 270 us; the launch traced here: 269 us
  starting transfers between devices  103 us (38%)
  waiting for transfers between devices  60.4 us (22%)
  between operations  37.1 us (14%)
  other arithmetic  30 us (11%)
  blocking collectives  18.4 us (7%)
  matrix products  11.5 us (4%)
  local copies, waits for them, and re-layouts  9 us (3%)
    ppermute x24, starting transfers between devices, passed_along(): return lax.ppermute(value, axis, pairs)  103 us
    ppermute x24, waiting for transfers between devices, passed_along(): return lax.ppermute(value, axis, pairs)  60.3 us
    reduce_sum x7, other arithmetic, on_device(): jnp.sum(jnp.where(peer_valid[None, :, :], colbest, 0.0), axis=2)  12.1 us
    dot_general x12, matrix products, on_device(): jnp.einsum('ale,bme->ablm', own_full, current, preferred_element_type=jnp...  11.5 us
    pmax x1, blocking collectives, on_device(): rowbest = lax.pmax(row_part, 'tok')  11.2 us
    reduce_sum x6, other arithmetic, on_device(): jnp.sum(jnp.where(own_valid[:, None, :], rowbest, 0.0), axis=2)  7.67 us
    lt x12, other arithmetic, on_device(): peer_valid = half_pos[None, :] < peer_len[:, None]  7.59 us
    another operation x1, local copies, waits for them, and re-layouts, on_device(): jnp.stack(backward_list, axis=1).reshape(per_dev, STEPS * per_dev)  7.52 us
  transfers between devices with their start and end apart: 25, of which 13 were waited for; matrix products, arithmetic and copies ran while one was open for 11% of the time, Pallas kernels for 0%

commit v1 on v0

v1 whole, which is shorter than its diff:
```python
import functools

import jax
import jax.numpy as jnp
from jax import lax
from jax.experimental import pallas as pl
from jax.experimental.pallas import tpu as pltpu
from jax.sharding import PartitionSpec as P

STEPS = 12
AXES = ("cand", "tok")
GROUP = 4
REACH = STEPS // GROUP
LOW = -4.0
VMEM = 48 * 1024 * 1024


def place(flat):
    return flat // 8, (flat // 4) % 2, (flat // 2) % 2, flat % 2


def flat(group, y_lo, core, y_hi, groups):
    return (((group % groups) * 2 + y_lo) * 2 + core) * 2 + y_hi


def send(value, move):
    count = lax.axis_size(AXES)
    groups = count // 8
    pairs = [(i, flat(*move(*place(i)), groups)) for i in range(count)]
    return lax.ppermute(value, AXES, pairs)


def along(steps):
    return lambda g, l, c, h: (g + steps, l, c, h)


def within(dl, dc, dh):
    return lambda g, l, c, h: (g, l ^ dl, c ^ dc, h ^ dh)


def ring(g, l, c, h):
    y = (2 * h + l + (1 if c == 0 else -1)) % 4
    return (g, y % 2, c, y // 2)


def normalize_kernel(emb_ref, out_ref):
    values = emb_ref[0].astype(jnp.float32)
    factor = lax.rsqrt(jnp.sum(values * values, axis=-1, keepdims=True) + 1e-06)
    out_ref[...] = (values * factor).astype(jnp.bfloat16)


def normalize(emb):
    _, rows, width = emb.shape
    step = rows // 2
    return pl.pallas_call(
        normalize_kernel,
        grid=(rows // step,),
        in_specs=[pl.BlockSpec((1, step, width), lambda i: (0, i, 0))],
        out_specs=pl.BlockSpec((step, width), lambda i: (i, 0)),
        out_shape=jax.ShapeDtypeStruct((rows, width), jnp.bfloat16),
        name="normalize",
    )(emb)


def slot(ids, k, e):
    y_lo, core, y_hi = ids
    source = core ^ e
    y = (2 * y_hi + y_lo + jnp.where(source == 0, 4 - k, k)) % 4
    return 2 * (y % 2) + source, y // 2


def scan_kernel(n_x, n_a, dists, ids_ref, len_ref, *refs):
    xs, items = refs[:n_x], refs[n_x : n_x + n_a]
    msg_ref = refs[n_x + n_a]
    xbuf, abuf, racc, sems = refs[n_x + n_a + 1 :]
    group, y_lo, core, y_hi = (ids_ref[i] for i in range(4))
    cands = len_ref.shape[0]
    rows = xbuf.shape[0] // n_x
    copies = []
    for i, ref in enumerate(xs):
        copies.append(
            pltpu.make_async_copy(ref, xbuf.at[pl.ds(i * rows, rows)], sems.at[i])
        )
    for i, ref in enumerate(items):
        copies.append(pltpu.make_async_copy(ref, abuf.at[i], sems.at[n_x + i]))
    for copy in copies:
        copy.start()
    racc[...] = jnp.full(racc.shape, LOW, jnp.float32)
    lane = lax.broadcasted_iota(jnp.int32, (1, rows), 1)
    sub = lax.broadcasted_iota(jnp.int32, (rows, 1), 0)
    lane128 = lax.broadcasted_iota(jnp.int32, (1, 128), 1)
    own = 2 * y_lo + core
    x_valid = []
    for dist in dists:
        length = len_ref[(GROUP * (group + dist) + own) % cands]
        x_valid.append(length - rows * y_hi)
    for copy in copies[:n_x]:
        copy.wait()
    for a in range(n_a):
        copies[n_x + a].wait()

    @pl.loop(0, n_a)
    def _(a):
        cand, half = slot((y_lo, core, y_hi), a // 2, a % 2)
        a_valid = len_ref[GROUP * group + cand] - rows * half
        for i in range(n_x):
            sims = lax.dot_general(
                xbuf[i * rows : (i + 1) * rows, :],
                abuf[a],
                (((1,), (1,)), ((), ())),
                preferred_element_type=jnp.float32,
            )
            best = jnp.max(jnp.where(lane < a_valid, sims, LOW), axis=1, keepdims=True)
            racc[i] = jnp.where(lane128 == a, best, racc[i])
            col = jnp.max(jnp.where(sub < x_valid[i], sims, LOW), axis=0, keepdims=True)
            msg_ref[i, pl.ds(a, 1), :] = col

    for i in range(n_x):
        turned = racc[i].T
        paired = jnp.maximum(turned[0:4], turned[4:8])
        paired = jnp.where(lane < x_valid[i], paired, 0.0)
        msg_ref[i, 8:16, :] = jnp.concatenate([paired, jnp.zeros_like(paired)], axis=0)


def scan(ids, lengths, xs, dists, items):
    n_x, n_a = len(xs), len(items)
    rows, width = xs[0].shape
    flops = 2 * n_x * n_a * rows * rows * width
    return pl.pallas_call(
        functools.partial(scan_kernel, n_x, n_a, dists),
        in_specs=[pl.BlockSpec(memory_space=pltpu.SMEM)] * 2
        + [pl.BlockSpec(memory_space=pl.ANY)] * (n_x + n_a),
        out_specs=pl.BlockSpec(memory_space=pltpu.VMEM),
        out_shape=jax.ShapeDtypeStruct((n_x, 16, rows), jnp.float32),
        scratch_shapes=[
            pltpu.VMEM((n_x * rows, width), jnp.bfloat16),
            pltpu.VMEM((n_a, rows, width), jnp.bfloat16),
            pltpu.VMEM((n_x, rows, 128), jnp.float32),
            pltpu.SemaphoreType.DMA((n_x + n_a,)),
        ],
        compiler_params=pltpu.CompilerParams(vmem_limit_bytes=VMEM),
        cost_estimate=pl.CostEstimate(
            flops=flops, bytes_accessed=2 * (n_x + n_a) * rows * width, transcendentals=0
        ),
        name="scan",
    )(ids, lengths, *xs, *items)


def score_kernel(dists, ids_ref, len_ref, own_ref, got_ref, out_ref):
    group, y_lo, core, y_hi = (ids_ref[i] for i in range(4))
    cands = len_ref.shape[0]
    n_x, _, rows = own_ref.shape
    lane = lax.broadcasted_iota(jnp.int32, (8, rows), 1)
    sub = lax.broadcasted_iota(jnp.int32, (8, 1), 0)
    lane128 = lax.broadcasted_iota(jnp.int32, (8, 128), 1)
    valid = jnp.zeros((8, 1), jnp.int32)
    a_len = jnp.ones((8, 1), jnp.int32)
    for a in range(8):
        cand, half = slot((y_lo, core, y_hi), a // 2, a % 2)
        length = len_ref[GROUP * group + cand]
        valid = jnp.where(sub == a, length - rows * half, valid)
        a_len = jnp.where(sub == a, length, a_len)
    a_len = a_len.astype(jnp.float32)
    tile = jnp.zeros((8, 128), jnp.float32)
    for i, dist in enumerate(dists):
        x_len = len_ref[(GROUP * (group + dist) + 2 * y_lo + core) % cands]
        x_len = jnp.full((8, 1), x_len, jnp.int32).astype(jnp.float32)
        own, got = own_ref[i], got_ref[i]
        col = jnp.maximum(own[0:8], jnp.concatenate([got[4:8], got[0:4]], axis=0))
        col = jnp.sum(jnp.where(lane < valid, col, 0.0), axis=1, keepdims=True)
        recall = col + jnp.concatenate([col[4:8], col[0:4]], axis=0)
        precision = jnp.sum(own[8:16] + got[8:16], axis=1, keepdims=True)
        score = 0.5 * (precision / x_len + recall / a_len)
        tile = jnp.where(lane128 == dist, score, tile)
    out_ref[...] = tile


def score(ids, lengths, own, got, dists):
    return pl.pallas_call(
        functools.partial(score_kernel, dists),
        in_specs=[pl.BlockSpec(memory_space=pltpu.SMEM)] * 2
        + [pl.BlockSpec(memory_space=pltpu.VMEM)] * 2,
        out_specs=pl.BlockSpec(memory_space=pltpu.VMEM),
        out_shape=jax.ShapeDtypeStruct((8, 128), jnp.float32),
        name="score",
    )(ids, lengths, own, got)


def place_kernel(ids_ref, *refs):
    near, early, late = refs[0], refs[1:5], refs[5:9]
    back = refs[9:12]
    out_ref = refs[12]
    y_lo, core = ids_ref[1], ids_ref[2]
    own = 2 * y_lo + core
    sub = lax.broadcasted_iota(jnp.int32, (8, 128), 0)
    lane = lax.broadcasted_iota(jnp.int32, (8, 128), 1)
    other = 2 * (y_lo ^ (sub // 2)) + (core ^ (sub % 2))
    total = jnp.zeros((8, 128), jnp.float32)

    def add(total, values, steps, base, used):
        use = (steps >= 1) & (steps <= STEPS) & (lane == base + steps - 1) & (sub < 4) & used
        return total + jnp.where(use, values, 0.0)

    own_group = near[:, 0:1]
    total = add(total, own_group, other - own, 0, sub < 4)
    total = add(total, own_group, own - other, STEPS, sub < 4)
    for a in range(4):
        for dist in range(1, REACH + 1):
            tile = (early if dist < REACH else late)[a]
            total = add(total, tile[:, dist : dist + 1], GROUP * dist + other - own, 0, sub == a)
    for dist in range(1, REACH + 1):
        tile = back[dist - 1]
        total = add(
            total, tile[:, dist : dist + 1], GROUP * dist + own - other, STEPS, sub < 4
        )
    out_ref[...] = jnp.sum(total, axis=0, keepdims=True)[:, : 2 * STEPS]


def placed(ids, near, early, late, back):
    return pl.pallas_call(
        place_kernel,
        in_specs=[pl.BlockSpec(memory_space=pltpu.SMEM)]
        + [pl.BlockSpec(memory_space=pltpu.VMEM)] * 12,
        out_specs=pl.BlockSpec(memory_space=pltpu.VMEM),
        out_shape=jax.ShapeDtypeStruct((1, 2 * STEPS), jnp.float32),
        name="placed",
    )(ids, near, *early, *late, *back)


def on_device(embeddings, lengths):
    device = lax.axis_index("cand")
    ids = jnp.stack(
        [device // 4, (device // 2) % 2, device % 2, lax.axis_index("tok")]
    ).astype(jnp.int32)
    own = normalize(embeddings)
    peer = own
    peers = []
    for _ in range(REACH):
        peer = send(peer, along(-1))
        peers.append(peer)
    items = []
    piece = own
    for k in range(4):
        items += [piece, send(piece, within(0, 1, 0))]
        if k < 3:
            piece = send(piece, ring)
    first = scan(ids, lengths, [own, *peers[:-1]], tuple(range(REACH)), items)
    got = send(first, within(0, 0, 1))
    tile = score(ids, lengths, first, got, tuple(range(REACH)))
    early = [tile] + [send(tile, within(a // 2, a % 2, 0)) for a in range(1, 4)]
    back = [send(tile, along(dist)) for dist in range(1, REACH)]
    last = scan(ids, lengths, [peers[-1]], (REACH,), items)
    got = send(last, within(0, 0, 1))
    tile3 = score(ids, lengths, last, got, (REACH,))
    late = [tile3] + [send(tile3, within(a // 2, a % 2, 0)) for a in range(1, 4)]
    back.append(send(tile3, along(REACH)))
    return placed(ids, tile, early, late, back)


def solution(mesh):
    in_specs = (P("cand", "tok", None), P())
    out_specs = P("cand", None)
    return jax.shard_map(
        on_device, mesh=mesh, in_specs=in_specs, out_specs=out_specs, check_vma=False
    )
```

time: 270 us -> 99.4 us (0.37)
  the two profiles are of different devices: /device:TPU:4 before, /device:TPU:16 now
where the time goes in v1:
time: 99.4 us; the launch traced here: 99 us
  waiting for transfers between devices  37.1 us (37%)
  starting transfers between devices  36.2 us (36%)
  Pallas kernels  19.6 us (20%)
  local copies, waits for them, and re-layouts  5.78 us (6%)
    ppermute x21, waiting for transfers between devices, send(): return lax.ppermute(value, AXES, pairs)  37.1 us
    ppermute x21, starting transfers between devices, send(): return lax.ppermute(value, AXES, pairs)  36.2 us
    pallas_call x2, Pallas kernels, scan(): pl.pallas_call(functools.partial(scan_kernel, n_x, n_a, dists), in_specs=...  13 us
    unnamed x38, local copies, waits for them, and re-layouts  5.78 us
    pallas_call x2, Pallas kernels, score(): pl.pallas_call(functools.partial(score_kernel, dists), in_specs=[pl.Block...  3.22 us
  transfers between devices with their start and end apart: 21, of which 7 were waited for; matrix products, arithmetic and copies ran while one was open for 0% of the time, Pallas kernels for 16%

profile of v1, /device:TPU:16, one launch (start us, length us, event | category | flops | bytes accessed | tf_op | source)
XLA Modules:
  0.0 99.0 jit_solution(14952361567310166518)
XLA Ops:
  0.0 1.9 %normalize.1.refs_0_.refs_3_.refs_1_ = bf16[256,1024]{1,0:T(8,128)(2,1)} custom-call(bf16[1,256,1024]{2,1,0:T(8,128)(2,1)} %emb_ref.1), custom_call_target="tpu_custom_call" | custom-call | tf_op jit(solution)/shard_map/normalize/pallas_call | solution.py:55
  1.9 1.3 %collective-permute-start.3 = (bf16[256,1024]{1,0:T(8,128)(2,1)}, bf16[256,1024]{1,0:T(8,128)(2,1)S(1)}, u32[]{:S(2)}, u32[]{:S(2)}) collective-permute-start(bf16[256,1024]{1,0:T(8,128)(2,1)} %normalize.1.refs_0_.refs_3_.refs_1_), channel_id=1, source_target_pairs={{0,4},{1,5},{2,7},{3,6},{4,1},{5,0},{6,2},{7,3},{8,12},{9,13},{10,... | collective-permute-start | bytes 1572872 | tf_op jit(solution)/shard_map/ppermute | solution.py:30
  3.2 8.1 %collective-permute-done.3.refs_5_.refs_3_ = bf16[256,1024]{1,0:T(8,128)(2,1)S(1)} collective-permute-done((bf16[256,1024]{1,0:T(8,128)(2,1)}, bf16[256,1024]{1,0:T(8,128)(2,1)S(1)}, u32[]{:S(2)}, u32[]{:S(2)}) %collective-permute-start.3) | collective-permute-done | bytes 524320 | tf_op jit(solution)/shard_map/ppermute | solution.py:30
  11.3 1.3 %collective-permute-start.5 = (bf16[256,1024]{1,0:T(8,128)(2,1)S(1)}, bf16[256,1024]{1,0:T(8,128)(2,1)S(1)}, u32[]{:S(2)}, u32[]{:S(2)}) collective-permute-start(bf16[256,1024]{1,0:T(8,128)(2,1)S(1)} %collective-permute-done.3.refs_5_.refs_3_), channel_id=1, source_target_pairs={{0,4},{1,5},{2,7},{3,6},{4,1},{5,0},{6,2},{7,3},{8,12},{9,13},{10,... | collective-permute-start | bytes 1572872 | tf_op jit(solution)/shard_map/ppermute | solution.py:30
  12.6 8.1 %collective-permute-start = (bf16[256,1024]{1,0:T(8,128)(2,1)}, bf16[256,1024]{1,0:T(8,128)(2,1)S(1)}, u32[]{:S(2)}, u32[]{:S(2)}) collective-permute-start(bf16[256,1024]{1,0:T(8,128)(2,1)} %normalize.1.refs_0_.refs_3_.refs_1_), channel_id=1, source_target_pairs={{0,248},{1,249},{2,250},{3,251},{4,252},{5,253},{6,254},{7,255},{8... | collective-permute-start | bytes 1572872 | tf_op jit(solution)/shard_map/ppermute | solution.py:30
  20.7 1.8 %collective-permute-start.7 = (bf16[256,1024]{1,0:T(8,128)(2,1)S(1)}, bf16[256,1024]{1,0:T(8,128)(2,1)S(1)}, u32[]{:S(2)}, u32[]{:S(2)}) collective-permute-start(bf16[256,1024]{1,0:T(8,128)(2,1)S(1)} %collective-permute-done.5.refs_7_.refs_5_), channel_id=1, source_target_pairs={{0,4},{1,5},{2,7},{3,6},{4,1},{5,0},{6,2},{7,3},{8,12},{9,13},{10,... | collective-permute-start | bytes 1572872 | tf_op jit(solution)/shard_map/ppermute | solution.py:30
  22.5 7.7 %collective-permute-done.refs_1_ = bf16[256,1024]{1,0:T(8,128)(2,1)S(1)} collective-permute-done((bf16[256,1024]{1,0:T(8,128)(2,1)}, bf16[256,1024]{1,0:T(8,128)(2,1)S(1)}, u32[]{:S(2)}, u32[]{:S(2)}) %collective-permute-start) | collective-permute-done | bytes 524320 | tf_op jit(solution)/shard_map/ppermute | solution.py:30
  30.2 5.7 %collective-permute-start.1 = (bf16[256,1024]{1,0:T(8,128)(2,1)S(1)}, bf16[256,1024]{1,0:T(8,128)(2,1)}, u32[]{:S(2)}, u32[]{:S(2)}) collective-permute-start(bf16[256,1024]{1,0:T(8,128)(2,1)S(1)} %collective-permute-done.refs_1_), channel_id=1, source_target_pairs={{0,248},{1,249},{2,250},{3,251},{4,252},{5,253},{6,254},{7,255},{8... | collective-permute-start | bytes 1572872 | tf_op jit(solution)/shard_map/ppermute | solution.py:30
  37.7 6.5 %collective-permute-done.1.refs_2_ = bf16[256,1024]{1,0:T(8,128)(2,1)} collective-permute-done((bf16[256,1024]{1,0:T(8,128)(2,1)S(1)}, bf16[256,1024]{1,0:T(8,128)(2,1)}, u32[]{:S(2)}, u32[]{:S(2)}) %collective-permute-start.1) | collective-permute-done | bytes 524320 | tf_op jit(solution)/shard_map/ppermute | solution.py:30
  44.2 5.9 %collective-permute-start.13 = (bf16[256,1024]{1,0:T(8,128)(2,1)}, bf16[256,1024]{1,0:T(8,128)(2,1)}, u32[]{:S(2)}, u32[]{:S(2)}) collective-permute-start(bf16[256,1024]{1,0:T(8,128)(2,1)} %collective-permute-done.1.refs_2_), channel_id=1, source_target_pairs={{0,248},{1,249},{2,250},{3,251},{4,252},{5,253},{6,254},{7,255},{8... | collective-permute-start | bytes 1572872 | tf_op jit(solution)/shard_map/ppermute | solution.py:30
  50.7 1.0 %copy-done = bf16[256,1024]{1,0:T(8,128)(2,1)S(1)} copy-done((bf16[256,1024]{1,0:T(8,128)(2,1)S(1)}, bf16[256,1024]{1,0:T(8,128)(2,1)}, u32[]{:S(2)}) %copy-start) | copy-done | bytes 524312
  51.8 1.0 %copy-done.7 = bf16[256,1024]{1,0:T(8,128)(2,1)S(1)} copy-done((bf16[256,1024]{1,0:T(8,128)(2,1)S(1)}, bf16[256,1024]{1,0:T(8,128)(2,1)}, u32[]{:S(2)}) %copy-start.7) | copy-done | bytes 524312
  52.8 7.7 %scan.2.own_ref = f32[3,16,256]{2,1,0:T(8,128)S(1)} custom-call(s32[4]{0:T(128)S(1)} %pad_add_fusion.ids_ref, s32[128]{0:T(128)S(1)} %copy-done.5, bf16[256,1024]{1,0:T(8,128)(2,1)S(1)} %copy-done, bf16[256,1024]{1,0:T(8,128)(2,1)S(1)} %copy-done.7, bf16[256,1024]{1,0:T(8,128)(2,1)} %collective-permute-done.1.refs_2_, bf16[256,1024]{1,0:T(8,128)(2,1)S(1)} %copy-done, ...), custom_call_target="tpu_custom_call" | custom-call | flops 3221225472 | bytes 5767168 | tf_op jit(solution)/shard_map/scan/pallas_call | solution.py:129
  60.6 6.9 %collective-permute-start.9 = (f32[3,16,256]{2,1,0:T(8,128)S(1)}, f32[3,16,256]{2,1,0:T(8,128)S(1)}, u32[]{:S(2)}, u32[]{:S(2)}) collective-permute-start(f32[3,16,256]{2,1,0:T(8,128)S(1)} %scan.2.own_ref), channel_id=1, source_target_pairs={{0,1},{1,0},{2,3},{3,2},{4,5},{5,4},{6,7},{7,6},{8,9},{9,8},{10,11... | collective-permute-start | bytes 147464 | tf_op jit(solution)/shard_map/ppermute | solution.py:30
  67.5 5.3 %scan.3.own_ref = f32[1,16,256]{2,1,0:T(8,128)S(1)} custom-call(s32[4]{0:T(128)S(1)} %pad_add_fusion.ids_ref, s32[128]{0:T(128)S(1)} %copy-done.5, bf16[256,1024]{1,0:T(8,128)(2,1)} %collective-permute-done.13.refs_0_, bf16[256,1024]{1,0:T(8,128)(2,1)S(1)} %copy-done.1, bf16[256,1024]{1,0:T(8,128)(2,1)S(1)} %collective-permute-done.2.refs_4_.refs_2_, ...), custom_call_target="tpu_custom_call" | custom-call | flops 1073741824 | bytes 4718592 | tf_op jit(solution)/shard_map/scan/pallas_call | solution.py:129
  73.3 4.9 %collective-permute-done.14.got_ref = f32[1,16,256]{2,1,0:T(8,128)S(1)} collective-permute-done((f32[1,16,256]{2,1,0:T(8,128)S(1)}, f32[1,16,256]{2,1,0:T(8,128)S(1)}, u32[]{:S(2)}, u32[]{:S(2)}) %collective-permute-start.14) | collective-permute-done | bytes 16416 | tf_op jit(solution)/shard_map/ppermute | solution.py:30
  78.8 1.6 %score.3.refs_5_ = f32[8,128]{1,0:T(8,128)} custom-call(s32[4]{0:T(128)} %copy-done.4, s32[128]{0:T(128)} %len_ref.7, f32[1,16,256]{2,1,0:T(8,128)} %copy-done.2, f32[1,16,256]{2,1,0:T(8,128)} %copy-done.9), custom_call_target="tpu_custom_call" | custom-call | tf_op jit(solution)/shard_map/score/pallas_call | solution.py:179
  80.4 1.8 %collective-permute-start.15 = (f32[8,128]{1,0:T(8,128)}, f32[8,128]{1,0:T(8,128)S(1)}, u32[]{:S(2)}, u32[]{:S(2)}) collective-permute-start(f32[8,128]{1,0:T(8,128)} %score.3.refs_5_), channel_id=1, source_target_pairs={{0,2},{1,3},{2,0},{3,1},{4,6},{5,7},{6,4},{7,5},{8,10},{9,11},{10,... | collective-permute-start | bytes 12296 | tf_op jit(solution)/shard_map/ppermute | solution.py:30
  82.8 1.7 %score.2.refs_0_.refs_1_ = f32[8,128]{1,0:T(8,128)} custom-call(s32[4]{0:T(128)} %copy-done.4, s32[128]{0:T(128)} %len_ref.7, f32[3,16,256]{2,1,0:T(8,128)} %copy-done.3, f32[3,16,256]{2,1,0:T(8,128)} %copy-done.8), custom_call_target="tpu_custom_call" | custom-call | tf_op jit(solution)/shard_map/score/pallas_call | solution.py:179
  84.5 4.8 %collective-permute-done.20.refs_11_ = f32[8,128]{1,0:T(8,128)S(1)} collective-permute-done((f32[8,128]{1,0:T(8,128)}, f32[8,128]{1,0:T(8,128)S(1)}, u32[]{:S(2)}, u32[]{:S(2)}) %collective-permute-start.20) | collective-permute-done | bytes 4128 | tf_op jit(solution)/shard_map/ppermute | solution.py:30
  89.5 1.7 %collective-permute-start.10 = (f32[8,128]{1,0:T(8,128)}, f32[8,128]{1,0:T(8,128)S(1)}, u32[]{:S(2)}, u32[]{:S(2)}) collective-permute-start(f32[8,128]{1,0:T(8,128)} %score.2.refs_0_.refs_1_), channel_id=1, source_target_pairs={{0,2},{1,3},{2,0},{3,1},{4,6},{5,7},{6,4},{7,5},{8,10},{9,11},{10,... | collective-permute-start | bytes 12296 | tf_op jit(solution)/shard_map/ppermute | solution.py:30
  91.2 1.3 %collective-permute-done.19.refs_10_ = f32[8,128]{1,0:T(8,128)S(1)} collective-permute-done((f32[8,128]{1,0:T(8,128)}, f32[8,128]{1,0:T(8,128)S(1)}, u32[]{:S(2)}, u32[]{:S(2)}) %collective-permute-start.19) | collective-permute-done | bytes 4128 | tf_op jit(solution)/shard_map/ppermute | solution.py:30
  92.5 3.9 %collective-permute-done.18.refs_9_ = f32[8,128]{1,0:T(8,128)S(1)} collective-permute-done((f32[8,128]{1,0:T(8,128)}, f32[8,128]{1,0:T(8,128)S(1)}, u32[]{:S(2)}, u32[]{:S(2)}) %collective-permute-start.18) | collective-permute-done | bytes 4128 | tf_op jit(solution)/shard_map/ppermute | solution.py:30
  97.6 1.4 %placed.1 = f32[1,24]{1,0:T(1,128)} custom-call(s32[4]{0:T(128)} %copy-done.4, f32[8,128]{1,0:T(8,128)} %score.2.refs_0_.refs_1_, f32[8,128]{1,0:T(8,128)} %score.2.refs_0_.refs_1_, f32[8,128]{1,0:T(8,128)} %copy-done.18, f32[8,128]{1,0:T(8,128)} %copy-done.17, f32[8,128]{1,0:T(8,128)} %copy-done.16, f32[8,128]{1,0:T(8,128)} %score.3.refs_5_, ...), custom_call_target="tpu_custom_call" | custom-call | tf_op jit(solution)/shard_map/placed/pallas_call | solution.py:220
  (63 shorter events, 5.6 us)
Async XLA Ops:
  1.9 9.4 %collective-permute-start.3 = (bf16[256,1024]{1,0:T(8,128)(2,1)}, bf16[256,1024]{1,0:T(8,128)(2,1)S(1)}, u32[]{:S(2)}, u32[]{:S(2)}) collective-permute-start(bf16[256,1024]{1,0:T(8,128)(2,1)} %normalize.1.refs_0_.refs_3_.refs_1_), channel_id=1, source_target_pairs={{0,4},{1,5},{2,7},{3,6},{4,1},{5,0},{6,2},{7,3},{8,12},{9,13},{10,... | collective-permute-start | bytes 1572872 | tf_op jit(solution)/shard_map/ppermute | solution.py:30
  11.3 9.3 %collective-permute-start.5 = (bf16[256,1024]{1,0:T(8,128)(2,1)S(1)}, bf16[256,1024]{1,0:T(8,128)(2,1)S(1)}, u32[]{:S(2)}, u32[]{:S(2)}) collective-permute-start(bf16[256,1024]{1,0:T(8,128)(2,1)S(1)} %collective-permute-done.3.refs_5_.refs_3_), channel_id=1, source_target_pairs={{0,4},{1,5},{2,7},{3,6},{4,1},{5,0},{6,2},{7,3},{8,12},{9,13},{10,... | collective-permute-start | bytes 1572872 | tf_op jit(solution)/shard_map/ppermute | solution.py:30
  12.6 17.6 %collective-permute-start = (bf16[256,1024]{1,0:T(8,128)(2,1)}, bf16[256,1024]{1,0:T(8,128)(2,1)S(1)}, u32[]{:S(2)}, u32[]{:S(2)}) collective-permute-start(bf16[256,1024]{1,0:T(8,128)(2,1)} %normalize.1.refs_0_.refs_3_.refs_1_), channel_id=1, source_target_pairs={{0,248},{1,249},{2,250},{3,251},{4,252},{5,253},{6,254},{7,255},{8... | collective-permute-start | bytes 1572872 | tf_op jit(solution)/shard_map/ppermute | solution.py:30
  20.7 16.5 %collective-permute-start.7 = (bf16[256,1024]{1,0:T(8,128)(2,1)S(1)}, bf16[256,1024]{1,0:T(8,128)(2,1)S(1)}, u32[]{:S(2)}, u32[]{:S(2)}) collective-permute-start(bf16[256,1024]{1,0:T(8,128)(2,1)S(1)} %collective-permute-done.5.refs_7_.refs_5_), channel_id=1, source_target_pairs={{0,4},{1,5},{2,7},{3,6},{4,1},{5,0},{6,2},{7,3},{8,12},{9,13},{10,... | collective-permute-start | bytes 1572872 | tf_op jit(solution)/shard_map/ppermute | solution.py:30
  30.2 14.0 %collective-permute-start.1 = (bf16[256,1024]{1,0:T(8,128)(2,1)S(1)}, bf16[256,1024]{1,0:T(8,128)(2,1)}, u32[]{:S(2)}, u32[]{:S(2)}) collective-permute-start(bf16[256,1024]{1,0:T(8,128)(2,1)S(1)} %collective-permute-done.refs_1_), channel_id=1, source_target_pairs={{0,248},{1,249},{2,250},{3,251},{4,252},{5,253},{6,254},{7,255},{8... | collective-permute-start | bytes 1572872 | tf_op jit(solution)/shard_map/ppermute | solution.py:30
  36.7 13.5 %collective-permute-start.2 = (bf16[256,1024]{1,0:T(8,128)(2,1)}, bf16[256,1024]{1,0:T(8,128)(2,1)S(1)}, u32[]{:S(2)}, u32[]{:S(2)}) collective-permute-start(bf16[256,1024]{1,0:T(8,128)(2,1)} %normalize.1.refs_0_.refs_3_.refs_1_), channel_id=1, source_target_pairs={{0,2},{1,3},{2,0},{3,1},{4,6},{5,7},{6,4},{7,5},{8,10},{9,11},{10,... | collective-permute-start | bytes 1572872 | tf_op jit(solution)/shard_map/ppermute | solution.py:30
  36.7 13.5 %collective-permute-start.4 = (bf16[256,1024]{1,0:T(8,128)(2,1)S(1)}, bf16[256,1024]{1,0:T(8,128)(2,1)S(1)}, u32[]{:S(2)}, u32[]{:S(2)}) collective-permute-start(bf16[256,1024]{1,0:T(8,128)(2,1)S(1)} %collective-permute-done.3.refs_5_.refs_3_), channel_id=1, source_target_pairs={{0,2},{1,3},{2,0},{3,1},{4,6},{5,7},{6,4},{7,5},{8,10},{9,11},{10,... | collective-permute-start | bytes 1572872 | tf_op jit(solution)/shard_map/ppermute | solution.py:30
  37.2 13.0 %collective-permute-start.6 = (bf16[256,1024]{1,0:T(8,128)(2,1)S(1)}, bf16[256,1024]{1,0:T(8,128)(2,1)S(1)}, u32[]{:S(2)}, u32[]{:S(2)}) collective-permute-start(bf16[256,1024]{1,0:T(8,128)(2,1)S(1)} %collective-permute-done.5.refs_7_.refs_5_), channel_id=1, source_target_pairs={{0,2},{1,3},{2,0},{3,1},{4,6},{5,7},{6,4},{7,5},{8,10},{9,11},{10,... | collective-permute-start | bytes 1572872 | tf_op jit(solution)/shard_map/ppermute | solution.py:30
  37.2 13.0 %collective-permute-start.8 = (bf16[256,1024]{1,0:T(8,128)(2,1)S(1)}, bf16[256,1024]{1,0:T(8,128)(2,1)}, u32[]{:S(2)}, u32[]{:S(2)}) collective-permute-start(bf16[256,1024]{1,0:T(8,128)(2,1)S(1)} %collective-permute-done.7.refs_9_.refs_7_), channel_id=1, source_target_pairs={{0,2},{1,3},{2,0},{3,1},{4,6},{5,7},{6,4},{7,5},{8,10},{9,11},{10,... | collective-permute-start | bytes 1572872 | tf_op jit(solution)/shard_map/ppermute | solution.py:30
  44.2 23.3 %collective-permute-start.13 = (bf16[256,1024]{1,0:T(8,128)(2,1)}, bf16[256,1024]{1,0:T(8,128)(2,1)}, u32[]{:S(2)}, u32[]{:S(2)}) collective-permute-start(bf16[256,1024]{1,0:T(8,128)(2,1)} %collective-permute-done.1.refs_2_), channel_id=1, source_target_pairs={{0,248},{1,249},{2,250},{3,251},{4,252},{5,253},{6,254},{7,255},{8... | collective-permute-start | bytes 1572872 | tf_op jit(solution)/shard_map/ppermute | solution.py:30
  50.2 17.3 %copy-start.4 = (s32[4]{0:T(128)}, s32[4]{0:T(128)S(1)}, u32[]{:S(2)}) copy-start(s32[4]{0:T(128)S(1)} %pad_add_fusion.ids_ref) | copy-start | bytes 52
  52.8 14.6 %copy-start.1 = (bf16[256,1024]{1,0:T(8,128)(2,1)S(1)}, bf16[256,1024]{1,0:T(8,128)(2,1)}, u32[]{:S(2)}) copy-start(bf16[256,1024]{1,0:T(8,128)(2,1)} %normalize.1.refs_0_.refs_3_.refs_1_) | copy-start | bytes 1572868
  60.5 12.3 %copy-start.3 = (f32[3,16,256]{2,1,0:T(8,128)}, f32[3,16,256]{2,1,0:T(8,128)S(1)}, u32[]{:S(2)}) copy-start(f32[3,16,256]{2,1,0:T(8,128)S(1)} %scan.2.own_ref) | copy-start | bytes 147460
  60.6 21.6 %collective-permute-start.9 = (f32[3,16,256]{2,1,0:T(8,128)S(1)}, f32[3,16,256]{2,1,0:T(8,128)S(1)}, u32[]{:S(2)}, u32[]{:S(2)}) collective-permute-start(f32[3,16,256]{2,1,0:T(8,128)S(1)} %scan.2.own_ref), channel_id=1, source_target_pairs={{0,1},{1,0},{2,3},{3,2},{4,5},{5,4},{6,7},{7,6},{8,9},{9,8},{10,11... | collective-permute-start | bytes 147464 | tf_op jit(solution)/shard_map/ppermute | solution.py:30
  72.8 5.3 %collective-permute-start.14 = (f32[1,16,256]{2,1,0:T(8,128)S(1)}, f32[1,16,256]{2,1,0:T(8,128)S(1)}, u32[]{:S(2)}, u32[]{:S(2)}) collective-permute-start(f32[1,16,256]{2,1,0:T(8,128)S(1)} %scan.3.own_ref), channel_id=1, source_target_pairs={{0,1},{1,0},{2,3},{3,2},{4,5},{5,4},{6,7},{7,6},{8,9},{9,8},{10,11... | collective-permute-start | bytes 49160 | tf_op jit(solution)/shard_map/ppermute | solution.py:30
  80.3 8.9 %collective-permute-start.20 = (f32[8,128]{1,0:T(8,128)}, f32[8,128]{1,0:T(8,128)S(1)}, u32[]{:S(2)}, u32[]{:S(2)}) collective-permute-start(f32[8,128]{1,0:T(8,128)} %score.3.refs_5_), channel_id=1, source_target_pairs={{0,24},{1,25},{2,26},{3,27},{4,28},{5,29},{6,30},{7,31},{8,32},{9,... | collective-permute-start | bytes 12296 | tf_op jit(solution)/shard_map/ppermute | solution.py:30
  80.3 8.9 %collective-permute-start.17 = (f32[8,128]{1,0:T(8,128)}, f32[8,128]{1,0:T(8,128)S(1)}, u32[]{:S(2)}, u32[]{:S(2)}) collective-permute-start(f32[8,128]{1,0:T(8,128)} %score.3.refs_5_), channel_id=1, source_target_pairs={{0,6},{1,7},{2,4},{3,5},{4,2},{5,3},{6,0},{7,1},{8,14},{9,15},{10,... | collective-permute-start | bytes 12296 | tf_op jit(solution)/shard_map/ppermute | solution.py:30
  80.3 9.1 %collective-permute-start.16 = (f32[8,128]{1,0:T(8,128)}, f32[8,128]{1,0:T(8,128)S(1)}, u32[]{:S(2)}, u32[]{:S(2)}) collective-permute-start(f32[8,128]{1,0:T(8,128)} %score.3.refs_5_), channel_id=1, source_target_pairs={{0,4},{1,5},{2,6},{3,7},{4,0},{5,1},{6,2},{7,3},{8,12},{9,13},{10,... | collective-permute-start | bytes 12296 | tf_op jit(solution)/shard_map/ppermute | solution.py:30
  80.4 9.1 %collective-permute-start.15 = (f32[8,128]{1,0:T(8,128)}, f32[8,128]{1,0:T(8,128)S(1)}, u32[]{:S(2)}, u32[]{:S(2)}) collective-permute-start(f32[8,128]{1,0:T(8,128)} %score.3.refs_5_), channel_id=1, source_target_pairs={{0,2},{1,3},{2,0},{3,1},{4,6},{5,7},{6,4},{7,5},{8,10},{9,11},{10,... | collective-permute-start | bytes 12296 | tf_op jit(solution)/shard_map/ppermute | solution.py:30
  84.5 8.0 %collective-permute-start.19 = (f32[8,128]{1,0:T(8,128)}, f32[8,128]{1,0:T(8,128)S(1)}, u32[]{:S(2)}, u32[]{:S(2)}) collective-permute-start(f32[8,128]{1,0:T(8,128)} %score.2.refs_0_.refs_1_), channel_id=1, source_target_pairs={{0,16},{1,17},{2,18},{3,19},{4,20},{5,21},{6,22},{7,23},{8,24},{9,... | collective-permute-start | bytes 12296 | tf_op jit(solution)/shard_map/ppermute | solution.py:30
  89.3 7.1 %collective-permute-start.18 = (f32[8,128]{1,0:T(8,128)}, f32[8,128]{1,0:T(8,128)S(1)}, u32[]{:S(2)}, u32[]{:S(2)}) collective-permute-start(f32[8,128]{1,0:T(8,128)} %score.2.refs_0_.refs_1_), channel_id=1, source_target_pairs={{0,8},{1,9},{2,10},{3,11},{4,12},{5,13},{6,14},{7,15},{8,16},{9,17... | collective-permute-start | bytes 12296 | tf_op jit(solution)/shard_map/ppermute | solution.py:30
  89.3 7.1 %collective-permute-start.12 = (f32[8,128]{1,0:T(8,128)}, f32[8,128]{1,0:T(8,128)S(1)}, u32[]{:S(2)}, u32[]{:S(2)}) collective-permute-start(f32[8,128]{1,0:T(8,128)} %score.2.refs_0_.refs_1_), channel_id=1, source_target_pairs={{0,6},{1,7},{2,4},{3,5},{4,2},{5,3},{6,0},{7,1},{8,14},{9,15},{10,... | collective-permute-start | bytes 12296 | tf_op jit(solution)/shard_map/ppermute | solution.py:30
  89.4 7.0 %collective-permute-start.11 = (f32[8,128]{1,0:T(8,128)}, f32[8,128]{1,0:T(8,128)S(1)}, u32[]{:S(2)}, u32[]{:S(2)}) collective-permute-start(f32[8,128]{1,0:T(8,128)} %score.2.refs_0_.refs_1_), channel_id=1, source_target_pairs={{0,4},{1,5},{2,6},{3,7},{4,0},{5,1},{6,2},{7,3},{8,12},{9,13},{10,... | collective-permute-start | bytes 12296 | tf_op jit(solution)/shard_map/ppermute | solution.py:30
  89.5 6.9 %collective-permute-start.10 = (f32[8,128]{1,0:T(8,128)}, f32[8,128]{1,0:T(8,128)S(1)}, u32[]{:S(2)}, u32[]{:S(2)}) collective-permute-start(f32[8,128]{1,0:T(8,128)} %score.2.refs_0_.refs_1_), channel_id=1, source_target_pairs={{0,2},{1,3},{2,0},{3,1},{4,6},{5,7},{6,4},{7,5},{8,10},{9,11},{10,... | collective-permute-start | bytes 12296 | tf_op jit(solution)/shard_map/ppermute | solution.py:30
  (16 other events, 44.8 us)

commit v2 on v0

v2 whole, which is shorter than its diff:
```python
import functools

import jax
import jax.numpy as jnp
from jax import lax
from jax.experimental import pallas as pl
from jax.experimental.pallas import tpu as pltpu
from jax.sharding import PartitionSpec as P

STEPS = 12
AXES = ("cand", "tok")
GROUP = 4
LOW = -4.0
VMEM = 48 * 1024 * 1024
IN_VMEM = pl.BlockSpec(memory_space=pltpu.VMEM)
IN_SMEM = pl.BlockSpec(memory_space=pltpu.SMEM)
X_VALID, X_LEN, A_VALID, A_LEN, Y_LO, CORE = 0, 1, 8, 16, 24, 25


def place(flat):
    return flat // 8, (flat // 4) % 2, (flat // 2) % 2, flat % 2


def flat(group, y_lo, core, y_hi, groups):
    return (((group % groups) * 2 + y_lo) * 2 + core) * 2 + y_hi


def send(value, move):
    count = lax.axis_size(AXES)
    groups = count // 8
    pairs = [(i, flat(*move(*place(i)), groups)) for i in range(count)]
    return lax.ppermute(value, AXES, pairs)


def shift(dg=0, dl=0, dc=0, dh=0):
    return lambda g, l, c, h: (g + dg, l ^ dl, c ^ dc, h ^ dh)


def ring(way):
    def move(g, l, c, h):
        y = (2 * h + l + (way if c == 0 else -way)) % 4
        return (g, y % 2, c, y // 2)

    return move


def normalize_kernel(emb_ref, out_ref):
    values = emb_ref[0].astype(jnp.float32)
    factor = lax.rsqrt(jnp.sum(values * values, axis=-1, keepdims=True) + 1e-06)
    out_ref[...] = (values * factor).astype(jnp.bfloat16)


def normalize(emb):
    _, rows, width = emb.shape
    step = rows // 2
    return pl.pallas_call(
        normalize_kernel,
        grid=(rows // step,),
        in_specs=[pl.BlockSpec((1, step, width), lambda i: (0, i, 0))],
        out_specs=pl.BlockSpec((step, width), lambda i: (i, 0)),
        out_shape=jax.ShapeDtypeStruct((rows, width), jnp.bfloat16),
        name="normalize",
    )(emb)


def plan_kernel(rows, ids_ref, len_ref, par_ref):
    group, y_lo, core, y_hi = (ids_ref[i] for i in range(4))
    cands = len_ref.shape[0]
    sub = lax.broadcasted_iota(jnp.int32, (8, 128), 0)
    lane = lax.broadcasted_iota(jnp.int32, (8, 128), 1)
    for f in range(2):
        side = core ^ f
        tile = jnp.zeros((8, 128), jnp.int32)
        for x in range(8):
            cand = GROUP * (group + 1 - x // 2) + 2 * y_lo + (side ^ (x % 2))
            length = len_ref[(cand + cands) % cands]
            tile = jnp.where((sub == x) & (lane == X_VALID), length - rows * y_hi, tile)
            tile = jnp.where((sub == x) & (lane == X_LEN), length, tile)
        for k in range(4):
            y = (2 * y_hi + y_lo + jnp.where(side == 0, 4 - k, k)) % 4
            length = len_ref[(GROUP * (group + 1) + 2 * (y % 2) + side) % cands]
            tile = jnp.where(lane == A_VALID + k, length - rows * (y // 2), tile)
            if k < 2:
                tile = jnp.where(lane == A_LEN + k, length, tile)
        tile = jnp.where(lane == Y_LO, y_lo, tile)
        tile = jnp.where(lane == CORE, side, tile)
        par_ref[8 * f : 8 * f + 8] = tile


def plan(ids, lengths, rows):
    return pl.pallas_call(
        functools.partial(plan_kernel, rows),
        in_specs=[IN_SMEM] * 2,
        out_specs=IN_VMEM,
        out_shape=jax.ShapeDtypeStruct((16, 128), jnp.int32),
        name="plan",
    )(ids, lengths)


def scan_kernel(x_ids, ks, first, last, *refs):
    n_x, n_a = len(x_ids), len(ks)
    par_ref, refs = refs[0], refs[1:]
    xs, refs = refs[:n_x], refs[n_x:]
    items, refs = refs[:n_a], refs[n_a:]
    if first:
        row_out, col_out = refs[:2]
        row_out[...] = jnp.full(row_out.shape, LOW, jnp.float32)
        col_out[...] = jnp.full(col_out.shape, LOW, jnp.float32)
        rest = refs[2:]
    else:
        row_in, col_in, row_out, col_out = refs[:4]
        row_out[...] = row_in[...]
        col_out[...] = col_in[...]
        rest = refs[4:]
    rows = xs[0].shape[0]
    lane = lax.broadcasted_iota(jnp.int32, (1, rows), 1)
    sub = lax.broadcasted_iota(jnp.int32, (rows, 1), 0)
    lane128 = lax.broadcasted_iota(jnp.int32, (1, 128), 1)
    for i, x in enumerate(x_ids):
        x_mask = sub < par_ref[x : x + 1, X_VALID : X_VALID + 1]
        for j, k in enumerate(ks):
            a_mask = lane < par_ref[0:1, A_VALID + k : A_VALID + k + 1]
            sims = lax.dot_general(
                xs[i][...],
                items[j][...],
                (((1,), (1,)), ((), ())),
                preferred_element_type=jnp.float32,
            )
            best = jnp.max(jnp.where(a_mask, sims, LOW), axis=1, keepdims=True)
            row_out[...] = jnp.where(lane128 == 8 * k + x, best, row_out[...])
            col = jnp.max(jnp.where(x_mask, sims, LOW), axis=0, keepdims=True)
            col_out[k, x : x + 1, :] = col
    if last:
        turned = row_out[...].T
        lanes = lax.broadcasted_iota(jnp.int32, (8, rows), 1)
        valid = lanes < par_ref[0:8, X_VALID : X_VALID + 1]
        sums = jnp.zeros((8, rows), jnp.float32)
        for p in range(2):
            best = jnp.maximum(turned[8 * p : 8 * p + 8], turned[8 * p + 16 : 8 * p + 24])
            total = jnp.sum(jnp.where(valid, best, 0.0), axis=1, keepdims=True)
            sums = jnp.where(lanes == p, total, sums)
        col_out[4] = sums


def scan(par, xs, x_ids, items, ks, state=None, last=False):
    n_x, n_a = len(xs), len(items)
    rows, width = xs[0].shape
    state = [] if state is None else list(state)
    return pl.pallas_call(
        functools.partial(scan_kernel, x_ids, ks, not state, last),
        in_specs=[IN_VMEM] * (1 + n_x + n_a + len(state)),
        out_specs=[IN_VMEM] * 2,
        out_shape=[
            jax.ShapeDtypeStruct((rows, 128), jnp.float32),
            jax.ShapeDtypeStruct((5, 8, rows), jnp.float32),
        ],
        compiler_params=pltpu.CompilerParams(vmem_limit_bytes=VMEM),
        cost_estimate=pl.CostEstimate(
            flops=2 * n_x * n_a * rows * rows * width,
            bytes_accessed=2 * (n_x + n_a) * rows * width,
            transcendentals=0,
        ),
        name="scan",
    )(par, *xs, *items, *state)


def score_kernel(par_ref, own_ref, over_ref, core_ref, both_ref, out_ref):
    rows = own_ref.shape[2]
    lane = lax.broadcasted_iota(jnp.int32, (8, rows), 1)
    lane128 = lax.broadcasted_iota(jnp.int32, (8, 128), 1)
    par = par_ref[...]

    def scores(par, one, two):
        x_len = par[:, X_LEN : X_LEN + 1].astype(jnp.float32)
        sums = []
        for k in range(4):
            col = jnp.maximum(one[k], two[k ^ 2])
            valid = lane < par[:, A_VALID + k : A_VALID + k + 1]
            sums.append(jnp.sum(jnp.where(valid, col, 0.0), axis=1, keepdims=True))
        precision = one[4][:, :2] + two[4][:, :2]
        tile = jnp.zeros((8, 128), jnp.float32)
        for p in range(2):
            a_len = par[:, A_LEN + p : A_LEN + p + 1].astype(jnp.float32)
            recall = (sums[p] + sums[p + 2]) / a_len
            tile = jnp.where(
                lane128 == p, 0.5 * (precision[:, p : p + 1] / x_len + recall), tile
            )
        return tile

    out_ref[0:8] = scores(par[0:8], own_ref, over_ref)
    out_ref[8:16] = scores(par[8:16], core_ref, both_ref)


def score(par, own, over, core, both):
    return pl.pallas_call(
        score_kernel,
        in_specs=[IN_VMEM] * 5,
        out_specs=IN_VMEM,
        out_shape=jax.ShapeDtypeStruct((16, 128), jnp.float32),
        name="score",
    )(par, own, over, core, both)


def put_kernel(par_ref, own_ref, same_ref, other_ref, one_ref, two_ref, out_ref):
    y_lo, core = par_ref[0:1, Y_LO : Y_LO + 1], par_ref[0:1, CORE : CORE + 1]
    sub = lax.broadcasted_iota(jnp.int32, (16, 128), 0)
    lane = lax.broadcasted_iota(jnp.int32, (16, 128), 1)
    f, d, e = sub // 8, (sub % 8) // 2, sub % 2
    own = 2 * y_lo + core
    total = jnp.zeros((16, 128), jnp.float32)

    def add(total, values, steps, base, used):
        use = used & (steps >= 1) & (steps <= STEPS) & (lane == base + steps - 1)
        return total + jnp.where(use, values, 0.0)

    for p, ref in enumerate((same_ref, other_ref)):
        values = ref[:, p : p + 1]
        x = 2 * (y_lo ^ p) + (core ^ e)
        steps = GROUP * d + own - x
        total = add(total, values, steps, STEPS, f == 0)
        total = add(total, values, -steps, 0, (f == 0) & (d == 0))
    for dist, ref in enumerate((own_ref, one_ref, two_ref), 1):
        for p in range(2):
            values = ref[:, p : p + 1]
            a = 2 * (y_lo ^ p) + (core ^ f)
            total = add(total, values, GROUP * dist + a - own, 0, (d == dist) & (e == f))
    out_ref[...] = jnp.sum(total, axis=0, keepdims=True)[:, : 2 * STEPS]


def put(par, own, same, other, one, two):
    return pl.pallas_call(
        put_kernel,
        in_specs=[IN_VMEM] * 6,
        out_specs=IN_VMEM,
        out_shape=jax.ShapeDtypeStruct((1, 2 * STEPS), jnp.float32),
        name="put",
    )(par, own, same, other, one, two)


def on_device(embeddings, lengths):
    device = lax.axis_index("cand")
    rows = embeddings.shape[1]
    ids = jnp.stack(
        [device // 4, (device // 2) % 2, device % 2, lax.axis_index("tok")]
    ).astype(jnp.int32)
    par = plan(ids, lengths, rows)
    own = normalize(embeddings)

    right = send(own, shift(dg=-1))
    left = send(own, shift(dg=1))
    over = send(own, shift(dh=1))
    own_c = send(own, shift(dc=1))
    right, left, over, own_c = lax.optimization_barrier((right, left, over, own_c))

    item1 = send(right, ring(1))
    item3 = send(right, ring(-1))
    item2 = send(over, shift(dg=-1))
    far = send(left, shift(dg=1))
    right_c = send(right, shift(dc=1))
    left_c = send(left, shift(dc=1))
    near = [right, right_c, own, own_c, left, left_c]
    state = scan(par, near, range(6), [right], [0])
    item1, item2, item3, far = lax.optimization_barrier((item1, item2, item3, far))
    far_c = send(far, shift(dc=1))
    state = scan(par, near, range(6), [item1, item2, item3], [1, 2, 3], state)
    _, message = scan(
        par, [far, far_c], [6, 7], [right, item1, item2, item3], range(4), state, True
    )

    over = send(message, shift(dh=1))
    core = send(message, shift(dc=1))
    both = send(message, shift(dc=1, dh=1))
    tile = score(par, message, over, core, both)
    same = send(tile, shift(dg=1))
    other = send(tile, shift(dg=1, dl=1))
    one = send(tile, shift(dg=-1))
    two = send(tile, shift(dg=-2))
    return put(par, tile, same, other, one, two)


def solution(mesh):
    in_specs = (P("cand", "tok", None), P())
    out_specs = P("cand", None)
    return jax.shard_map(
        on_device, mesh=mesh, in_specs=in_specs, out_specs=out_specs, check_vma=False
    )
```

time: 270 us -> 84.4 us (0.31)
  the two profiles are of different devices: /device:TPU:4 before, /device:TPU:16 now
where the time goes in v2:
time: 84.4 us; the launch traced here: 83.1 us
  waiting for transfers between devices  36.8 us (44%)
  starting transfers between devices  26.9 us (32%)
  Pallas kernels  13.9 us (16%)
  local copies, waits for them, and re-layouts  4.77 us (6%)
    ppermute x18, waiting for transfers between devices, send(): return lax.ppermute(value, AXES, pairs)  36.8 us
    ppermute x18, starting transfers between devices, send(): return lax.ppermute(value, AXES, pairs)  26.9 us
    pallas_call x3, Pallas kernels, scan(): pl.pallas_call(functools.partial(scan_kernel, x_ids, ks, not state, last)...  7.24 us
    unnamed x32, local copies, waits for them, and re-layouts  4.77 us
    pallas_call x1, Pallas kernels, normalize(): pl.pallas_call(normalize_kernel, grid=(rows // step,), in_specs=[pl.Block...  1.95 us
    pallas_call x1, Pallas kernels, score(): pl.pallas_call(score_kernel, in_specs=[IN_VMEM] * 5, out_specs=IN_VMEM, o...  1.86 us
  transfers between devices with their start and end apart: 18, of which 8 were waited for; matrix products, arithmetic and copies ran while one was open for 1% of the time, Pallas kernels for 6%

profile of v2, /device:TPU:16, one launch (start us, length us, event | category | flops | bytes accessed | tf_op | source)
XLA Modules:
  0.0 83.1 jit_solution(9695884163862987574)
XLA Ops:
  0.0 1.9 %normalize.1.refs_3_ = bf16[256,1024]{1,0:T(8,128)(2,1)} custom-call(bf16[1,256,1024]{2,1,0:T(8,128)(2,1)} %emb_ref.1), custom_call_target="tpu_custom_call" | custom-call | tf_op jit(solution)/shard_map/normalize/pallas_call | solution.py:56
  2.0 2.1 %collective-permute-start.2 = (bf16[256,1024]{1,0:T(8,128)(2,1)}, bf16[256,1024]{1,0:T(8,128)(2,1)S(1)}, u32[]{:S(2)}, u32[]{:S(2)}) collective-permute-start(bf16[256,1024]{1,0:T(8,128)(2,1)} %normalize.1.refs_3_), channel_id=1, source_target_pairs={{0,1},{1,0},{2,3},{3,2},{4,5},{5,4},{6,7},{7,6},{8,9},{9,8},{10,11... | collective-permute-start | bytes 1572872 | tf_op jit(solution)/shard_map/ppermute | solution.py:32
  4.2 6.1 %collective-permute-start = (bf16[256,1024]{1,0:T(8,128)(2,1)}, bf16[256,1024]{1,0:T(8,128)(2,1)S(1)}, u32[]{:S(2)}, u32[]{:S(2)}) collective-permute-start(bf16[256,1024]{1,0:T(8,128)(2,1)} %normalize.1.refs_3_), channel_id=1, source_target_pairs={{0,248},{1,249},{2,250},{3,251},{4,252},{5,253},{6,254},{7,255},{8... | collective-permute-start | bytes 1572872 | tf_op jit(solution)/shard_map/ppermute | solution.py:32
  10.3 7.7 %collective-permute-done.2 = bf16[256,1024]{1,0:T(8,128)(2,1)S(1)} collective-permute-done((bf16[256,1024]{1,0:T(8,128)(2,1)}, bf16[256,1024]{1,0:T(8,128)(2,1)S(1)}, u32[]{:S(2)}, u32[]{:S(2)}) %collective-permute-start.2) | collective-permute-done | bytes 524320 | tf_op jit(solution)/shard_map/ppermute | solution.py:32
  18.0 4.9 %collective-permute-done.1.refs_5_ = bf16[256,1024]{1,0:T(8,128)(2,1)S(1)} collective-permute-done((bf16[256,1024]{1,0:T(8,128)(2,1)}, bf16[256,1024]{1,0:T(8,128)(2,1)S(1)}, u32[]{:S(2)}, u32[]{:S(2)}) %collective-permute-start.1) | collective-permute-done | bytes 524320 | tf_op jit(solution)/shard_map/ppermute | solution.py:32
  22.9 5.0 %collective-permute-start.5 = (bf16[256,1024]{1,0:T(8,128)(2,1)S(1)}, bf16[256,1024]{1,0:T(8,128)(2,1)S(1)}, u32[]{:S(2)}, u32[]{:S(2)}) collective-permute-start(bf16[256,1024]{1,0:T(8,128)(2,1)S(1)} %collective-permute-done.2), channel_id=1, source_target_pairs={{0,248},{1,249},{2,250},{3,251},{4,252},{5,253},{6,254},{7,255},{8... | collective-permute-start | bytes 1572872 | tf_op jit(solution)/shard_map/ppermute | solution.py:32
  27.9 2.4 %collective-permute-start.6 = (bf16[256,1024]{1,0:T(8,128)(2,1)S(1)}, bf16[256,1024]{1,0:T(8,128)(2,1)S(1)}, u32[]{:S(2)}, u32[]{:S(2)}) collective-permute-start(bf16[256,1024]{1,0:T(8,128)(2,1)S(1)} %collective-permute-done.refs_1_.refs_7_.refs_3_), channel_id=1, source_target_pairs={{0,5},{1,4},{2,6},{3,7},{4,0},{5,1},{6,3},{7,2},{8,13},{9,12},{10,... | collective-permute-start | bytes 1572872 | tf_op jit(solution)/shard_map/ppermute | solution.py:32
  30.3 8.3 %collective-permute-done.5.refs_8_.refs_5_ = bf16[256,1024]{1,0:T(8,128)(2,1)S(1)} collective-permute-done((bf16[256,1024]{1,0:T(8,128)(2,1)S(1)}, bf16[256,1024]{1,0:T(8,128)(2,1)S(1)}, u32[]{:S(2)}, u32[]{:S(2)}) %collective-permute-start.5) | collective-permute-done | bytes 524320 | tf_op jit(solution)/shard_map/ppermute | solution.py:32
  38.7 5.6 %collective-permute-done.7.refs_1_ = bf16[256,1024]{1,0:T(8,128)(2,1)} collective-permute-done((bf16[256,1024]{1,0:T(8,128)(2,1)S(1)}, bf16[256,1024]{1,0:T(8,128)(2,1)}, u32[]{:S(2)}, u32[]{:S(2)}) %collective-permute-start.7) | collective-permute-done | bytes 524320 | tf_op jit(solution)/shard_map/ppermute | solution.py:32
  46.6 1.4 %plan.1.refs_0_.par_ref = s32[16,128]{1,0:T(8,128)} custom-call(s32[4]{0:T(128)} %pad_add_fusion.ids_ref, s32[128]{0:T(128)} %len_ref.1), custom_call_target="tpu_custom_call" | custom-call | tf_op jit(solution)/shard_map/plan/pallas_call | solution.py:91
  48.0 1.0 %copy-done = bf16[256,1024]{1,0:T(8,128)(2,1)S(1)} copy-done((bf16[256,1024]{1,0:T(8,128)(2,1)S(1)}, bf16[256,1024]{1,0:T(8,128)(2,1)}, u32[]{:S(2)}) %copy-start) | copy-done | bytes 524312
  49.7 1.1 %scan.3 = (f32[256,128]{1,0:T(8,128)S(1)}, f32[5,8,256]{2,1,0:T(8,128)S(1)}) custom-call(s32[16,128]{1,0:T(8,128)S(1)} %copy-done.2, bf16[256,1024]{1,0:T(8,128)(2,1)S(1)} %collective-permute-done.refs_1_.refs_7_.refs_3_, bf16[256,1024]{1,0:T(8,128)(2,1)S(1)} %collective-permute-done.9.refs_2_, bf16[256,1024]{1,0:T(8,128)(2,1)S(1)} %copy-done, ...), custom_call_target="tpu_custom_call" | custom-call | flops 805306368 | bytes 3670016 | tf_op jit(solution)/shard_map/scan/pallas_call | solution.py:149
  51.1 2.9 %scan.4 = (f32[256,128]{1,0:T(8,128)S(1)}, f32[5,8,256]{2,1,0:T(8,128)S(1)}) custom-call(s32[16,128]{1,0:T(8,128)S(1)} %copy-done.3, bf16[256,1024]{1,0:T(8,128)(2,1)S(1)} %collective-permute-done.refs_1_.refs_7_.refs_3_, bf16[256,1024]{1,0:T(8,128)(2,1)S(1)} %collective-permute-done.9.refs_2_, bf16[256,1024]{1,0:T(8,128)(2,1)S(1)} %copy-done.1, ...), custom_call_target="tpu_custom_call" | custom-call | flops 2415919104 | bytes 4718592 | tf_op jit(solution)/shard_map/scan/pallas_call | solution.py:149
  54.0 3.2 %scan.5 = (f32[256,128]{1,0:T(8,128)}, f32[5,8,256]{2,1,0:T(8,128)S(1)}) custom-call(s32[16,128]{1,0:T(8,128)S(1)} %copy-done.3, bf16[256,1024]{1,0:T(8,128)(2,1)} %collective-permute-done.7.refs_1_, bf16[256,1024]{1,0:T(8,128)(2,1)} %collective-permute-done.8.refs_2_, bf16[256,1024]{1,0:T(8,128)(2,1)S(1)} %collective-permute-done.refs_1_.refs_7_.refs_3_, ...), custom_call_target="tpu_custom_call" | custom-call | flops 1073741824 | bytes 3145728 | tf_op jit(solution)/shard_map/scan/pallas_call | solution.py:149
  57.2 3.3 %collective-permute-start.13 = (f32[5,8,256]{2,1,0:T(8,128)S(1)}, f32[5,8,256]{2,1,0:T(8,128)S(1)}, u32[]{:S(2)}, u32[]{:S(2)}) collective-permute-start(f32[5,8,256]{2,1,0:T(8,128)S(1)} %get-tuple-element.30.own_ref), channel_id=1, source_target_pairs={{0,3},{1,2},{2,1},{3,0},{4,7},{5,6},{6,5},{7,4},{8,11},{9,10},{10,... | collective-permute-start | bytes 122888 | tf_op jit(solution)/shard_map/ppermute | solution.py:32
  60.9 1.4 %collective-permute-done.13.both_ref = f32[5,8,256]{2,1,0:T(8,128)S(1)} collective-permute-done((f32[5,8,256]{2,1,0:T(8,128)S(1)}, f32[5,8,256]{2,1,0:T(8,128)S(1)}, u32[]{:S(2)}, u32[]{:S(2)}) %collective-permute-start.13) | collective-permute-done | bytes 40992 | tf_op jit(solution)/shard_map/ppermute | solution.py:32
  62.4 3.7 %collective-permute-done.11.over_ref = f32[5,8,256]{2,1,0:T(8,128)S(1)} collective-permute-done((f32[5,8,256]{2,1,0:T(8,128)S(1)}, f32[5,8,256]{2,1,0:T(8,128)S(1)}, u32[]{:S(2)}, u32[]{:S(2)}) %collective-permute-start.11) | collective-permute-done | bytes 40992 | tf_op jit(solution)/shard_map/ppermute | solution.py:32
  66.7 1.9 %score.1.own_ref = f32[16,128]{1,0:T(8,128)} custom-call(s32[16,128]{1,0:T(8,128)} %plan.1.refs_0_.par_ref, f32[5,8,256]{2,1,0:T(8,128)} %copy-done.4, f32[5,8,256]{2,1,0:T(8,128)} %copy-done.11, f32[5,8,256]{2,1,0:T(8,128)} %copy-done.10, f32[5,8,256]{2,1,0:T(8,128)} %copy-done.9), custom_call_target="tpu_custom_call" | custom-call | tf_op jit(solution)/shard_map/score/pallas_call | solution.py:195
  68.5 2.1 %collective-permute-start.16 = (f32[16,128]{1,0:T(8,128)}, f32[16,128]{1,0:T(8,128)S(1)}, u32[]{:S(2)}, u32[]{:S(2)}) collective-permute-start(f32[16,128]{1,0:T(8,128)} %score.1.own_ref), channel_id=1, source_target_pairs={{0,248},{1,249},{2,250},{3,251},{4,252},{5,253},{6,254},{7,255},{8... | collective-permute-start | bytes 24584 | tf_op jit(solution)/shard_map/ppermute | solution.py:32
  70.6 3.2 %collective-permute-start.15 = (f32[16,128]{1,0:T(8,128)}, f32[16,128]{1,0:T(8,128)S(1)}, u32[]{:S(2)}, u32[]{:S(2)}) collective-permute-start(f32[16,128]{1,0:T(8,128)} %score.1.own_ref), channel_id=1, source_target_pairs={{0,12},{1,13},{2,14},{3,15},{4,8},{5,9},{6,10},{7,11},{8,20},{9,21... | collective-permute-start | bytes 24584 | tf_op jit(solution)/shard_map/ppermute | solution.py:32
  73.9 2.0 %collective-permute-start.14 = (f32[16,128]{1,0:T(8,128)}, f32[16,128]{1,0:T(8,128)S(1)}, u32[]{:S(2)}, u32[]{:S(2)}) collective-permute-start(f32[16,128]{1,0:T(8,128)} %score.1.own_ref), channel_id=1, source_target_pairs={{0,8},{1,9},{2,10},{3,11},{4,12},{5,13},{6,14},{7,15},{8,16},{9,17... | collective-permute-start | bytes 24584 | tf_op jit(solution)/shard_map/ppermute | solution.py:32
  75.9 2.8 %collective-permute-done.15.other_ref = f32[16,128]{1,0:T(8,128)S(1)} collective-permute-done((f32[16,128]{1,0:T(8,128)}, f32[16,128]{1,0:T(8,128)S(1)}, u32[]{:S(2)}, u32[]{:S(2)}) %collective-permute-start.15) | collective-permute-done | bytes 8224 | tf_op jit(solution)/shard_map/ppermute | solution.py:32
  78.7 2.3 %collective-permute-done.14.same_ref = f32[16,128]{1,0:T(8,128)S(1)} collective-permute-done((f32[16,128]{1,0:T(8,128)}, f32[16,128]{1,0:T(8,128)S(1)}, u32[]{:S(2)}, u32[]{:S(2)}) %collective-permute-start.14) | collective-permute-done | bytes 8224 | tf_op jit(solution)/shard_map/ppermute | solution.py:32
  81.6 1.5 %put.1 = f32[1,24]{1,0:T(1,128)} custom-call(s32[16,128]{1,0:T(8,128)} %plan.1.refs_0_.par_ref, f32[16,128]{1,0:T(8,128)} %score.1.own_ref, f32[16,128]{1,0:T(8,128)} %copy-done.15, f32[16,128]{1,0:T(8,128)} %copy-done.14, f32[16,128]{1,0:T(8,128)} %copy-done.13, f32[16,128]{1,0:T(8,128)} %copy-done.12), custom_call_target="tpu_custom_call" | custom-call | tf_op jit(solution)/shard_map/put/pallas_call | solution.py:231
  (52 shorter events, 5.0 us)
Async XLA Ops:
  1.9 8.4 %collective-permute-start.3 = (bf16[256,1024]{1,0:T(8,128)(2,1)}, bf16[256,1024]{1,0:T(8,128)(2,1)S(1)}, u32[]{:S(2)}, u32[]{:S(2)}) collective-permute-start(bf16[256,1024]{1,0:T(8,128)(2,1)} %normalize.1.refs_3_), channel_id=1, source_target_pairs={{0,2},{1,3},{2,0},{3,1},{4,6},{5,7},{6,4},{7,5},{8,10},{9,11},{10,... | collective-permute-start | bytes 1572872 | tf_op jit(solution)/shard_map/ppermute | solution.py:32
  2.0 16.1 %collective-permute-start.2 = (bf16[256,1024]{1,0:T(8,128)(2,1)}, bf16[256,1024]{1,0:T(8,128)(2,1)S(1)}, u32[]{:S(2)}, u32[]{:S(2)}) collective-permute-start(bf16[256,1024]{1,0:T(8,128)(2,1)} %normalize.1.refs_3_), channel_id=1, source_target_pairs={{0,1},{1,0},{2,3},{3,2},{4,5},{5,4},{6,7},{7,6},{8,9},{9,8},{10,11... | collective-permute-start | bytes 1572872 | tf_op jit(solution)/shard_map/ppermute | solution.py:32
  4.0 18.9 %collective-permute-start.1 = (bf16[256,1024]{1,0:T(8,128)(2,1)}, bf16[256,1024]{1,0:T(8,128)(2,1)S(1)}, u32[]{:S(2)}, u32[]{:S(2)}) collective-permute-start(bf16[256,1024]{1,0:T(8,128)(2,1)} %normalize.1.refs_3_), channel_id=1, source_target_pairs={{0,8},{1,9},{2,10},{3,11},{4,12},{5,13},{6,14},{7,15},{8,16},{9,17... | collective-permute-start | bytes 1572872 | tf_op jit(solution)/shard_map/ppermute | solution.py:32
  4.2 18.7 %collective-permute-start = (bf16[256,1024]{1,0:T(8,128)(2,1)}, bf16[256,1024]{1,0:T(8,128)(2,1)S(1)}, u32[]{:S(2)}, u32[]{:S(2)}) collective-permute-start(bf16[256,1024]{1,0:T(8,128)(2,1)} %normalize.1.refs_3_), channel_id=1, source_target_pairs={{0,248},{1,249},{2,250},{3,251},{4,252},{5,253},{6,254},{7,255},{8... | collective-permute-start | bytes 1572872 | tf_op jit(solution)/shard_map/ppermute | solution.py:32
  22.9 15.8 %collective-permute-start.5 = (bf16[256,1024]{1,0:T(8,128)(2,1)S(1)}, bf16[256,1024]{1,0:T(8,128)(2,1)S(1)}, u32[]{:S(2)}, u32[]{:S(2)}) collective-permute-start(bf16[256,1024]{1,0:T(8,128)(2,1)S(1)} %collective-permute-done.2), channel_id=1, source_target_pairs={{0,248},{1,249},{2,250},{3,251},{4,252},{5,253},{6,254},{7,255},{8... | collective-permute-start | bytes 1572872 | tf_op jit(solution)/shard_map/ppermute | solution.py:32
  27.9 16.4 %collective-permute-start.7 = (bf16[256,1024]{1,0:T(8,128)(2,1)S(1)}, bf16[256,1024]{1,0:T(8,128)(2,1)}, u32[]{:S(2)}, u32[]{:S(2)}) collective-permute-start(bf16[256,1024]{1,0:T(8,128)(2,1)S(1)} %collective-permute-done.1.refs_5_), channel_id=1, source_target_pairs={{0,8},{1,9},{2,10},{3,11},{4,12},{5,13},{6,14},{7,15},{8,16},{9,17... | collective-permute-start | bytes 1572872 | tf_op jit(solution)/shard_map/ppermute | solution.py:32
  27.9 16.4 %collective-permute-start.6 = (bf16[256,1024]{1,0:T(8,128)(2,1)S(1)}, bf16[256,1024]{1,0:T(8,128)(2,1)S(1)}, u32[]{:S(2)}, u32[]{:S(2)}) collective-permute-start(bf16[256,1024]{1,0:T(8,128)(2,1)S(1)} %collective-permute-done.refs_1_.refs_7_.refs_3_), channel_id=1, source_target_pairs={{0,5},{1,4},{2,6},{3,7},{4,0},{5,1},{6,3},{7,2},{8,13},{9,12},{10,... | collective-permute-start | bytes 1572872 | tf_op jit(solution)/shard_map/ppermute | solution.py:32
  30.3 14.8 %collective-permute-start.4 = (bf16[256,1024]{1,0:T(8,128)(2,1)S(1)}, bf16[256,1024]{1,0:T(8,128)(2,1)S(1)}, u32[]{:S(2)}, u32[]{:S(2)}) collective-permute-start(bf16[256,1024]{1,0:T(8,128)(2,1)S(1)} %collective-permute-done.refs_1_.refs_7_.refs_3_), channel_id=1, source_target_pairs={{0,4},{1,5},{2,7},{3,6},{4,1},{5,0},{6,2},{7,3},{8,12},{9,13},{10,... | collective-permute-start | bytes 1572872 | tf_op jit(solution)/shard_map/ppermute | solution.py:32
  30.3 17.6 %collective-permute-start.10 = (bf16[256,1024]{1,0:T(8,128)(2,1)S(1)}, bf16[256,1024]{1,0:T(8,128)(2,1)S(1)}, u32[]{:S(2)}, u32[]{:S(2)}) collective-permute-start(bf16[256,1024]{1,0:T(8,128)(2,1)S(1)} %collective-permute-done.1.refs_5_), channel_id=1, source_target_pairs={{0,2},{1,3},{2,0},{3,1},{4,6},{5,7},{6,4},{7,5},{8,10},{9,11},{10,... | collective-permute-start | bytes 1572872 | tf_op jit(solution)/shard_map/ppermute | solution.py:32
  38.7 9.3 %collective-permute-start.9 = (bf16[256,1024]{1,0:T(8,128)(2,1)S(1)}, bf16[256,1024]{1,0:T(8,128)(2,1)S(1)}, u32[]{:S(2)}, u32[]{:S(2)}) collective-permute-start(bf16[256,1024]{1,0:T(8,128)(2,1)S(1)} %collective-permute-done.refs_1_.refs_7_.refs_3_), channel_id=1, source_target_pairs={{0,2},{1,3},{2,0},{3,1},{4,6},{5,7},{6,4},{7,5},{8,10},{9,11},{10,... | collective-permute-start | bytes 1572872 | tf_op jit(solution)/shard_map/ppermute | solution.py:32
  45.9 8.0 %collective-permute-start.8 = (bf16[256,1024]{1,0:T(8,128)(2,1)}, bf16[256,1024]{1,0:T(8,128)(2,1)}, u32[]{:S(2)}, u32[]{:S(2)}) collective-permute-start(bf16[256,1024]{1,0:T(8,128)(2,1)} %collective-permute-done.7.refs_1_), channel_id=1, source_target_pairs={{0,2},{1,3},{2,0},{3,1},{4,6},{5,7},{6,4},{7,5},{8,10},{9,11},{10,... | collective-permute-start | bytes 1572872 | tf_op jit(solution)/shard_map/ppermute | solution.py:32
  57.2 8.8 %copy-start.4 = (f32[5,8,256]{2,1,0:T(8,128)}, f32[5,8,256]{2,1,0:T(8,128)S(1)}, u32[]{:S(2)}) copy-start(f32[5,8,256]{2,1,0:T(8,128)S(1)} %get-tuple-element.30.own_ref) | copy-start | bytes 122884
  57.2 5.1 %collective-permute-start.13 = (f32[5,8,256]{2,1,0:T(8,128)S(1)}, f32[5,8,256]{2,1,0:T(8,128)S(1)}, u32[]{:S(2)}, u32[]{:S(2)}) collective-permute-start(f32[5,8,256]{2,1,0:T(8,128)S(1)} %get-tuple-element.30.own_ref), channel_id=1, source_target_pairs={{0,3},{1,2},{2,1},{3,0},{4,7},{5,6},{6,5},{7,4},{8,11},{9,10},{10,... | collective-permute-start | bytes 122888 | tf_op jit(solution)/shard_map/ppermute | solution.py:32
  60.5 1.8 %collective-permute-start.12 = (f32[5,8,256]{2,1,0:T(8,128)S(1)}, f32[5,8,256]{2,1,0:T(8,128)S(1)}, u32[]{:S(2)}, u32[]{:S(2)}) collective-permute-start(f32[5,8,256]{2,1,0:T(8,128)S(1)} %get-tuple-element.30.own_ref), channel_id=1, source_target_pairs={{0,2},{1,3},{2,0},{3,1},{4,6},{5,7},{6,4},{7,5},{8,10},{9,11},{10,... | collective-permute-start | bytes 122888 | tf_op jit(solution)/shard_map/ppermute | solution.py:32
  60.5 5.5 %collective-permute-start.11 = (f32[5,8,256]{2,1,0:T(8,128)S(1)}, f32[5,8,256]{2,1,0:T(8,128)S(1)}, u32[]{:S(2)}, u32[]{:S(2)}) collective-permute-start(f32[5,8,256]{2,1,0:T(8,128)S(1)} %get-tuple-element.30.own_ref), channel_id=1, source_target_pairs={{0,1},{1,0},{2,3},{3,2},{4,5},{5,4},{6,7},{7,6},{8,9},{9,8},{10,11... | collective-permute-start | bytes 122888 | tf_op jit(solution)/shard_map/ppermute | solution.py:32
  62.4 3.7 %copy-start.9 = (f32[5,8,256]{2,1,0:T(8,128)}, f32[5,8,256]{2,1,0:T(8,128)S(1)}, u32[]{:S(2)}) copy-start(f32[5,8,256]{2,1,0:T(8,128)S(1)} %collective-permute-done.13.both_ref) | copy-start | bytes 122884
  62.4 3.7 %copy-start.10 = (f32[5,8,256]{2,1,0:T(8,128)}, f32[5,8,256]{2,1,0:T(8,128)S(1)}, u32[]{:S(2)}) copy-start(f32[5,8,256]{2,1,0:T(8,128)S(1)} %collective-permute-done.12.core_ref) | copy-start | bytes 122884
  68.5 7.4 %collective-permute-start.17 = (f32[16,128]{1,0:T(8,128)}, f32[16,128]{1,0:T(8,128)S(1)}, u32[]{:S(2)}, u32[]{:S(2)}) collective-permute-start(f32[16,128]{1,0:T(8,128)} %score.1.own_ref), channel_id=1, source_target_pairs={{0,240},{1,241},{2,242},{3,243},{4,244},{5,245},{6,246},{7,247},{8... | collective-permute-start | bytes 24584 | tf_op jit(solution)/shard_map/ppermute | solution.py:32
  68.5 7.4 %collective-permute-start.16 = (f32[16,128]{1,0:T(8,128)}, f32[16,128]{1,0:T(8,128)S(1)}, u32[]{:S(2)}, u32[]{:S(2)}) collective-permute-start(f32[16,128]{1,0:T(8,128)} %score.1.own_ref), channel_id=1, source_target_pairs={{0,248},{1,249},{2,250},{3,251},{4,252},{5,253},{6,254},{7,255},{8... | collective-permute-start | bytes 24584 | tf_op jit(solution)/shard_map/ppermute | solution.py:32
  70.6 8.1 %collective-permute-start.15 = (f32[16,128]{1,0:T(8,128)}, f32[16,128]{1,0:T(8,128)S(1)}, u32[]{:S(2)}, u32[]{:S(2)}) collective-permute-start(f32[16,128]{1,0:T(8,128)} %score.1.own_ref), channel_id=1, source_target_pairs={{0,12},{1,13},{2,14},{3,15},{4,8},{5,9},{6,10},{7,11},{8,20},{9,21... | collective-permute-start | bytes 24584 | tf_op jit(solution)/shard_map/ppermute | solution.py:32
  73.9 7.2 %collective-permute-start.14 = (f32[16,128]{1,0:T(8,128)}, f32[16,128]{1,0:T(8,128)S(1)}, u32[]{:S(2)}, u32[]{:S(2)}) collective-permute-start(f32[16,128]{1,0:T(8,128)} %score.1.own_ref), channel_id=1, source_target_pairs={{0,8},{1,9},{2,10},{3,11},{4,12},{5,13},{6,14},{7,15},{8,16},{9,17... | collective-permute-start | bytes 24584 | tf_op jit(solution)/shard_map/ppermute | solution.py:32
  75.9 5.2 %copy-start.12 = (f32[16,128]{1,0:T(8,128)}, f32[16,128]{1,0:T(8,128)S(1)}, u32[]{:S(2)}) copy-start(f32[16,128]{1,0:T(8,128)S(1)} %collective-permute-done.17.two_ref) | copy-start | bytes 24580
  75.9 5.2 %copy-start.13 = (f32[16,128]{1,0:T(8,128)}, f32[16,128]{1,0:T(8,128)S(1)}, u32[]{:S(2)}) copy-start(f32[16,128]{1,0:T(8,128)S(1)} %collective-permute-done.16.one_ref) | copy-start | bytes 24580
  78.7 2.3 %copy-start.14 = (f32[16,128]{1,0:T(8,128)}, f32[16,128]{1,0:T(8,128)S(1)}, u32[]{:S(2)}) copy-start(f32[16,128]{1,0:T(8,128)S(1)} %collective-permute-done.15.other_ref) | copy-start | bytes 24580
  (10 other events, 9.4 us)

commit v3 on v2

--- a/solution.py
+++ b/solution.py
@@ -11,7 +11,8 @@
 AXES = ("cand", "tok")
 GROUP = 4
 LOW = -4.0
-VMEM = 48 * 1024 * 1024
+SMALL = pltpu.CompilerParams(vmem_limit_bytes=4 * 1024 * 1024)
+LARGE = pltpu.CompilerParams(vmem_limit_bytes=8 * 1024 * 1024)
 IN_VMEM = pl.BlockSpec(memory_space=pltpu.VMEM)
 IN_SMEM = pl.BlockSpec(memory_space=pltpu.SMEM)
 X_VALID, X_LEN, A_VALID, A_LEN, Y_LO, CORE = 0, 1, 8, 16, 24, 25
@@ -44,21 +45,38 @@
     return move
 
 
-def normalize_kernel(emb_ref, out_ref):
-    values = emb_ref[0].astype(jnp.float32)
-    factor = lax.rsqrt(jnp.sum(values * values, axis=-1, keepdims=True) + 1e-06)
-    out_ref[...] = (values * factor).astype(jnp.bfloat16)
+PARTS = 8
+
+
+def normalize_kernel(emb_ref, out_ref, buf, sems):
+    step = out_ref.shape[0] // PARTS
+    copies = [
+        pltpu.make_async_copy(
+            emb_ref.at[0, pl.ds(i * step, step)], buf.at[i], sems.at[i]
+        )
+        for i in range(PARTS)
+    ]
+    for copy in copies:
+        copy.start()
+    for i, copy in enumerate(copies):
+        copy.wait()
+        values = buf[i].astype(jnp.float32)
+        factor = lax.rsqrt(jnp.sum(values * values, axis=-1, keepdims=True) + 1e-06)
+        out_ref[i * step : (i + 1) * step, :] = (values * factor).astype(jnp.bfloat16)
 
 
 def normalize(emb):
     _, rows, width = emb.shape
-    step = rows // 2
     return pl.pallas_call(
         normalize_kernel,
-        grid=(rows // step,),
-        in_specs=[pl.BlockSpec((1, step, width), lambda i: (0, i, 0))],
-        out_specs=pl.BlockSpec((step, width), lambda i: (i, 0)),
+        in_specs=[pl.BlockSpec(memory_space=pl.ANY)],
+        out_specs=IN_VMEM,
         out_shape=jax.ShapeDtypeStruct((rows, width), jnp.bfloat16),
+        scratch_shapes=[
+            pltpu.VMEM((PARTS, rows // PARTS, width), jnp.bfloat16),
+            pltpu.SemaphoreType.DMA((PARTS,)),
+        ],
+        compiler_params=SMALL,
         name="normalize",
     )(emb)
 
@@ -85,6 +103,13 @@
         tile = jnp.where(lane == Y_LO, y_lo, tile)
         tile = jnp.where(lane == CORE, side, tile)
         par_ref[8 * f : 8 * f + 8] = tile
+        if f == 0:
+            turned = jnp.zeros((8, 128), jnp.int32)
+            for x in range(8):
+                cand = GROUP * (group + 1 - x // 2) + 2 * y_lo + (core ^ (x % 2))
+                length = len_ref[(cand + cands) % cands]
+                turned = jnp.where(lane % 8 == x, length - rows * y_hi, turned)
+            par_ref[16:24] = turned
 
 
 def plan(ids, lengths, rows):
@@ -92,7 +117,8 @@
         functools.partial(plan_kernel, rows),
         in_specs=[IN_SMEM] * 2,
         out_specs=IN_VMEM,
-        out_shape=jax.ShapeDtypeStruct((16, 128), jnp.int32),
+        out_shape=jax.ShapeDtypeStruct((24, 128), jnp.int32),
+        compiler_params=SMALL,
         name="plan",
     )(ids, lengths)
 
@@ -131,15 +157,12 @@
             col = jnp.max(jnp.where(x_mask, sims, LOW), axis=0, keepdims=True)
             col_out[k, x : x + 1, :] = col
     if last:
-        turned = row_out[...].T
-        lanes = lax.broadcasted_iota(jnp.int32, (8, rows), 1)
-        valid = lanes < par_ref[0:8, X_VALID : X_VALID + 1]
-        sums = jnp.zeros((8, rows), jnp.float32)
-        for p in range(2):
-            best = jnp.maximum(turned[8 * p : 8 * p + 8], turned[8 * p + 16 : 8 * p + 24])
-            total = jnp.sum(jnp.where(valid, best, 0.0), axis=1, keepdims=True)
-            sums = jnp.where(lanes == p, total, sums)
-        col_out[4] = sums
+        best = row_out[...]
+        best = jnp.maximum(best, pltpu.roll(best, 128 - 16, 1))
+        total = jnp.where(sub < par_ref[16:17, :], best, 0.0)
+        total = jnp.sum(total, axis=0, keepdims=True)
+        col_out[4, :, 0:128] = jnp.broadcast_to(total, (8, 128))
+        col_out[4, :, 128:256] = jnp.zeros((8, 128), jnp.float32)
 
 
 def scan(par, xs, x_ids, items, ks, state=None, last=False):
@@ -154,7 +177,7 @@
             jax.ShapeDtypeStruct((rows, 128), jnp.float32),
             jax.ShapeDtypeStruct((5, 8, rows), jnp.float32),
         ],
-        compiler_params=pltpu.CompilerParams(vmem_limit_bytes=VMEM),
+        compiler_params=LARGE,
         cost_estimate=pl.CostEstimate(
             flops=2 * n_x * n_a * rows * rows * width,
             bytes_accessed=2 * (n_x + n_a) * rows * width,
@@ -168,6 +191,7 @@
     rows = own_ref.shape[2]
     lane = lax.broadcasted_iota(jnp.int32, (8, rows), 1)
     lane128 = lax.broadcasted_iota(jnp.int32, (8, 128), 1)
+    sub128 = lax.broadcasted_iota(jnp.int32, (8, 128), 0)
     par = par_ref[...]
 
     def scores(par, one, two):
@@ -177,14 +201,14 @@
             col = jnp.maximum(one[k], two[k ^ 2])
             valid = lane < par[:, A_VALID + k : A_VALID + k + 1]
             sums.append(jnp.sum(jnp.where(valid, col, 0.0), axis=1, keepdims=True))
-        precision = one[4][:, :2] + two[4][:, :2]
+        precision = one[4][:, :128] + two[4][:, :128]
         tile = jnp.zeros((8, 128), jnp.float32)
         for p in range(2):
             a_len = par[:, A_LEN + p : A_LEN + p + 1].astype(jnp.float32)
             recall = (sums[p] + sums[p + 2]) / a_len
-            tile = jnp.where(
-                lane128 == p, 0.5 * (precision[:, p : p + 1] / x_len + recall), tile
-            )
+            mine = jnp.where(lane128 == 8 * p + sub128, precision, 0.0)
+            mine = jnp.sum(mine, axis=1, keepdims=True) / x_len
+            tile = jnp.where(lane128 == p, 0.5 * (mine + recall), tile)
         return tile
 
     out_ref[0:8] = scores(par[0:8], own_ref, over_ref)
@@ -197,6 +221,7 @@
         in_specs=[IN_VMEM] * 5,
         out_specs=IN_VMEM,
         out_shape=jax.ShapeDtypeStruct((16, 128), jnp.float32),
+        compiler_params=SMALL,
         name="score",
     )(par, own, over, core, both)
 
@@ -233,6 +258,7 @@
         in_specs=[IN_VMEM] * 6,
         out_specs=IN_VMEM,
         out_shape=jax.ShapeDtypeStruct((1, 2 * STEPS), jnp.float32),
+        compiler_params=SMALL,
         name="put",
     )(par, own, same, other, one, two)
 
@@ -246,18 +272,20 @@
     par = plan(ids, lengths, rows)
     own = normalize(embeddings)
 
+    own_c = send(own, shift(dc=1))
     right = send(own, shift(dg=-1))
     left = send(own, shift(dg=1))
     over = send(own, shift(dh=1))
-    own_c = send(own, shift(dc=1))
-    right, left, over, own_c = lax.optimization_barrier((right, left, over, own_c))
-
+    own_c, right, left, over, par = lax.optimization_barrier(
+        (own_c, right, left, over, par)
+    )
+
+    right_c = send(right, shift(dc=1))
+    left_c = send(left, shift(dc=1))
+    item3 = send(right, ring(-1))
     item1 = send(right, ring(1))
-    item3 = send(right, ring(-1))
     item2 = send(over, shift(dg=-1))
     far = send(left, shift(dg=1))
-    right_c = send(right, shift(dc=1))
-    left_c = send(left, shift(dc=1))
     near = [right, right_c, own, own_c, left, left_c]
     state = scan(par, near, range(6), [right], [0])
     item1, item2, item3, far = lax.optimization_barrier((item1, item2, item3, far))

time: 84.4 us -> 72.7 us (0.86)
  Pallas kernels: 13.9 us -> 9.53 us
  waiting for transfers between devices: 36.8 us -> 33.5 us
  local copies, waits for them, and re-layouts: 4.77 us -> 1.62 us
    ppermute x18, waiting for transfers between devices: 36.8 us -> 33.5 us  [send(): return lax.ppermute(value, AXES, pairs)]
    unnamed x32 -> x4, local copies, waits for them, and re-layouts: 4.77 us -> 1.62 us
    pallas_call x1, Pallas kernels: 1.86 us -> 0.36 us  [score(): pl.pallas_call(score_kernel, in_specs=[IN_VMEM] * 5, out_specs=IN_VMEM, o...]
    pallas_call x3, Pallas kernels: 7.24 us -> 6.23 us  [scan(): pl.pallas_call(functools.partial(scan_kernel, x_ids, ks, not state, last)...]
  transfers between devices with their start and end apart: 18 -> 18, of which waited for: 8 -> 8; matrix products, arithmetic and copies ran while one was open for 1% -> 0% of each run, Pallas kernels for 6% -> 7%
where the time goes in v3:
time: 72.7 us; the launch traced here: 71.9 us
  waiting for transfers between devices  33.5 us (46%)
  starting transfers between devices  27.1 us (37%)
  Pallas kernels  9.53 us (13%)
  local copies, waits for them, and re-layouts  1.62 us (2%)
    ppermute x18, waiting for transfers between devices, send(): return lax.ppermute(value, AXES, pairs)  33.5 us
    ppermute x18, starting transfers between devices, send(): return lax.ppermute(value, AXES, pairs)  27.1 us
    pallas_call x3, Pallas kernels, scan(): pl.pallas_call(functools.partial(scan_kernel, x_ids, ks, not state, last)...  6.23 us
    unnamed x4, local copies, waits for them, and re-layouts  1.62 us
    pallas_call x1, Pallas kernels, normalize(): pl.pallas_call(normalize_kernel, in_specs=[pl.BlockSpec(memory_space=pl.A...  1.54 us
  transfers between devices with their start and end apart: 18, of which 8 were waited for; matrix products, arithmetic and copies ran while one was open for 0% of the time, Pallas kernels for 7%

profile of v3, /device:TPU:16, one launch (start us, length us, event | category | flops | bytes accessed | tf_op | source)
XLA Modules:
  0.0 71.9 jit_solution(15595443564095487312)
XLA Ops:
  0.0 1.0 %copy-done = bf16[1,256,1024]{2,1,0:T(8,128)(2,1)S(1)} copy-done((bf16[1,256,1024]{2,1,0:T(8,128)(2,1)S(1)}, bf16[1,256,1024]{2,1,0:T(8,128)(2,1)}, u32[]{:S(2)}) %copy-start) | copy-done | bytes 524312
  1.0 1.5 %normalize.1.refs_3_ = bf16[256,1024]{1,0:T(8,128)(2,1)S(1)} custom-call(bf16[1,256,1024]{2,1,0:T(8,128)(2,1)S(1)} %copy-done), custom_call_target="tpu_custom_call" | custom-call | tf_op jit(solution)/shard_map/normalize/pallas_call | solution.py:70
  2.6 2.2 %collective-permute-start.3 = (bf16[256,1024]{1,0:T(8,128)(2,1)S(1)}, bf16[256,1024]{1,0:T(8,128)(2,1)S(1)}, u32[]{:S(2)}, u32[]{:S(2)}) collective-permute-start(bf16[256,1024]{1,0:T(8,128)(2,1)S(1)} %normalize.1.refs_3_), channel_id=1, source_target_pairs={{0,1},{1,0},{2,3},{3,2},{4,5},{5,4},{6,7},{7,6},{8,9},{9,8},{10,11... | collective-permute-start | bytes 1572872 | tf_op jit(solution)/shard_map/ppermute | solution.py:33
  4.9 6.1 %collective-permute-start.1 = (bf16[256,1024]{1,0:T(8,128)(2,1)S(1)}, bf16[256,1024]{1,0:T(8,128)(2,1)S(1)}, u32[]{:S(2)}, u32[]{:S(2)}) collective-permute-start(bf16[256,1024]{1,0:T(8,128)(2,1)S(1)} %normalize.1.refs_3_), channel_id=1, source_target_pairs={{0,248},{1,249},{2,250},{3,251},{4,252},{5,253},{6,254},{7,255},{8... | collective-permute-start | bytes 1572872 | tf_op jit(solution)/shard_map/ppermute | solution.py:33
  11.7 0.7 plan.1.refs_0_.par_ref
  12.4 5.4 %collective-permute-done.3 = bf16[256,1024]{1,0:T(8,128)(2,1)S(1)} collective-permute-done((bf16[256,1024]{1,0:T(8,128)(2,1)S(1)}, bf16[256,1024]{1,0:T(8,128)(2,1)S(1)}, u32[]{:S(2)}, u32[]{:S(2)}) %collective-permute-start.3) | collective-permute-done | bytes 524320 | tf_op jit(solution)/shard_map/ppermute | solution.py:33
  17.8 4.9 %collective-permute-done.2.refs_5_ = bf16[256,1024]{1,0:T(8,128)(2,1)S(1)} collective-permute-done((bf16[256,1024]{1,0:T(8,128)(2,1)S(1)}, bf16[256,1024]{1,0:T(8,128)(2,1)S(1)}, u32[]{:S(2)}, u32[]{:S(2)}) %collective-permute-start.2) | collective-permute-done | bytes 524320 | tf_op jit(solution)/shard_map/ppermute | solution.py:33
  22.8 5.1 %collective-permute-start.5 = (bf16[256,1024]{1,0:T(8,128)(2,1)S(1)}, bf16[256,1024]{1,0:T(8,128)(2,1)S(1)}, u32[]{:S(2)}, u32[]{:S(2)}) collective-permute-start(bf16[256,1024]{1,0:T(8,128)(2,1)S(1)} %collective-permute-done.3), channel_id=1, source_target_pairs={{0,248},{1,249},{2,250},{3,251},{4,252},{5,253},{6,254},{7,255},{8... | collective-permute-start | bytes 1572872 | tf_op jit(solution)/shard_map/ppermute | solution.py:33
  27.9 2.3 %collective-permute-start.6 = (bf16[256,1024]{1,0:T(8,128)(2,1)S(1)}, bf16[256,1024]{1,0:T(8,128)(2,1)S(1)}, u32[]{:S(2)}, u32[]{:S(2)}) collective-permute-start(bf16[256,1024]{1,0:T(8,128)(2,1)S(1)} %collective-permute-done.1.refs_1_.refs_7_.refs_3_), channel_id=1, source_target_pairs={{0,5},{1,4},{2,6},{3,7},{4,0},{5,1},{6,3},{7,2},{8,13},{9,12},{10,... | collective-permute-start | bytes 1572872 | tf_op jit(solution)/shard_map/ppermute | solution.py:33
  30.2 7.8 %collective-permute-done.5.refs_8_.refs_5_ = bf16[256,1024]{1,0:T(8,128)(2,1)S(1)} collective-permute-done((bf16[256,1024]{1,0:T(8,128)(2,1)S(1)}, bf16[256,1024]{1,0:T(8,128)(2,1)S(1)}, u32[]{:S(2)}, u32[]{:S(2)}) %collective-permute-start.5) | collective-permute-done | bytes 524320 | tf_op jit(solution)/shard_map/ppermute | solution.py:33
  38.0 5.5 %collective-permute-done.7.refs_1_ = bf16[256,1024]{1,0:T(8,128)(2,1)S(1)} collective-permute-done((bf16[256,1024]{1,0:T(8,128)(2,1)S(1)}, bf16[256,1024]{1,0:T(8,128)(2,1)S(1)}, u32[]{:S(2)}, u32[]{:S(2)}) %collective-permute-start.7) | collective-permute-done | bytes 524320 | tf_op jit(solution)/shard_map/ppermute | solution.py:33
  43.6 1.1 %scan.3 = (f32[256,128]{1,0:T(8,128)S(1)}, f32[5,8,256]{2,1,0:T(8,128)S(1)}) custom-call(s32[24,128]{1,0:T(8,128)S(1)} %plan.1.refs_0_.par_ref, bf16[256,1024]{1,0:T(8,128)(2,1)S(1)} %collective-permute-done.1.refs_1_.refs_7_.refs_3_, bf16[256,1024]{1,0:T(8,128)(2,1)S(1)} %collective-permute-done.9.refs_2_, bf16[256,1024]{1,0:T(8,128)(2,1)S(1)} %normalize.1.refs_3_, ...), custom_call_target="tpu_custom_call" | custom-call | flops 805306368 | bytes 3670016 | tf_op jit(solution)/shard_map/scan/pallas_call | solution.py:172
  44.7 3.0 %scan.4 = (f32[256,128]{1,0:T(8,128)S(1)}, f32[5,8,256]{2,1,0:T(8,128)S(1)}) custom-call(s32[24,128]{1,0:T(8,128)S(1)} %plan.1.refs_0_.par_ref, bf16[256,1024]{1,0:T(8,128)(2,1)S(1)} %collective-permute-done.1.refs_1_.refs_7_.refs_3_, bf16[256,1024]{1,0:T(8,128)(2,1)S(1)} %collective-permute-done.9.refs_2_, bf16[256,1024]{1,0:T(8,128)(2,1)S(1)} %normalize.1.refs_3_, ...), custom_call_target="tpu_custom_call" | custom-call | flops 2415919104 | bytes 4718592 | tf_op jit(solution)/shard_map/scan/pallas_call | solution.py:172
  47.7 2.1 %scan.5 = (f32[256,128]{1,0:T(8,128)}, f32[5,8,256]{2,1,0:T(8,128)S(1)}) custom-call(s32[24,128]{1,0:T(8,128)S(1)} %plan.1.refs_0_.par_ref, bf16[256,1024]{1,0:T(8,128)(2,1)S(1)} %collective-permute-done.7.refs_1_, bf16[256,1024]{1,0:T(8,128)(2,1)S(1)} %collective-permute-done.8.refs_2_, ...), custom_call_target="tpu_custom_call" | custom-call | flops 1073741824 | bytes 3145728 | tf_op jit(solution)/shard_map/scan/pallas_call | solution.py:172
  49.8 3.0 %collective-permute-start.13 = (f32[5,8,256]{2,1,0:T(8,128)S(1)}, f32[5,8,256]{2,1,0:T(8,128)S(1)}, u32[]{:S(2)}, u32[]{:S(2)}) collective-permute-start(f32[5,8,256]{2,1,0:T(8,128)S(1)} %get-tuple-element.32.own_ref), channel_id=1, source_target_pairs={{0,3},{1,2},{2,1},{3,0},{4,7},{5,6},{6,5},{7,4},{8,11},{9,10},{10,... | collective-permute-start | bytes 122888 | tf_op jit(solution)/shard_map/ppermute | solution.py:33
  52.9 0.6 collective-permute-start.11
  53.5 1.3 %collective-permute-done.13.both_ref = f32[5,8,256]{2,1,0:T(8,128)S(1)} collective-permute-done((f32[5,8,256]{2,1,0:T(8,128)S(1)}, f32[5,8,256]{2,1,0:T(8,128)S(1)}, u32[]{:S(2)}, u32[]{:S(2)}) %collective-permute-start.13) | collective-permute-done | bytes 40992 | tf_op jit(solution)/shard_map/ppermute | solution.py:33
  54.8 3.6 %collective-permute-done.11.over_ref = f32[5,8,256]{2,1,0:T(8,128)S(1)} collective-permute-done((f32[5,8,256]{2,1,0:T(8,128)S(1)}, f32[5,8,256]{2,1,0:T(8,128)S(1)}, u32[]{:S(2)}, u32[]{:S(2)}) %collective-permute-start.11) | collective-permute-done | bytes 40992 | tf_op jit(solution)/shard_map/ppermute | solution.py:33
  58.8 3.0 %collective-permute-start.16 = (f32[16,128]{1,0:T(8,128)S(1)}, f32[16,128]{1,0:T(8,128)S(1)}, u32[]{:S(2)}, u32[]{:S(2)}) collective-permute-start(f32[16,128]{1,0:T(8,128)S(1)} %score.1.own_ref), channel_id=1, source_target_pairs={{0,248},{1,249},{2,250},{3,251},{4,252},{5,253},{6,254},{7,255},{8... | collective-permute-start | bytes 24584 | tf_op jit(solution)/shard_map/ppermute | solution.py:33
  61.8 2.4 %collective-permute-start.15 = (f32[16,128]{1,0:T(8,128)S(1)}, f32[16,128]{1,0:T(8,128)S(1)}, u32[]{:S(2)}, u32[]{:S(2)}) collective-permute-start(f32[16,128]{1,0:T(8,128)S(1)} %score.1.own_ref), channel_id=1, source_target_pairs={{0,12},{1,13},{2,14},{3,15},{4,8},{5,9},{6,10},{7,11},{8,20},{9,21... | collective-permute-start | bytes 24584 | tf_op jit(solution)/shard_map/ppermute | solution.py:33
  64.2 2.0 %collective-permute-start.14 = (f32[16,128]{1,0:T(8,128)S(1)}, f32[16,128]{1,0:T(8,128)S(1)}, u32[]{:S(2)}, u32[]{:S(2)}) collective-permute-start(f32[16,128]{1,0:T(8,128)S(1)} %score.1.own_ref), channel_id=1, source_target_pairs={{0,8},{1,9},{2,10},{3,11},{4,12},{5,13},{6,14},{7,15},{8,16},{9,17... | collective-permute-start | bytes 24584 | tf_op jit(solution)/shard_map/ppermute | solution.py:33
  66.2 3.4 %collective-permute-done.15.other_ref = f32[16,128]{1,0:T(8,128)S(1)} collective-permute-done((f32[16,128]{1,0:T(8,128)S(1)}, f32[16,128]{1,0:T(8,128)S(1)}, u32[]{:S(2)}, u32[]{:S(2)}) %collective-permute-start.15) | collective-permute-done | bytes 8224 | tf_op jit(solution)/shard_map/ppermute | solution.py:33
  69.6 1.5 %collective-permute-done.14.same_ref = f32[16,128]{1,0:T(8,128)S(1)} collective-permute-done((f32[16,128]{1,0:T(8,128)S(1)}, f32[16,128]{1,0:T(8,128)S(1)}, u32[]{:S(2)}, u32[]{:S(2)}) %collective-permute-start.14) | collective-permute-done | bytes 8224 | tf_op jit(solution)/shard_map/ppermute | solution.py:33
  71.2 0.7 put.1
  (24 shorter events, 1.3 us)
Async XLA Ops:
  0.0 1.0 %copy-start = (bf16[1,256,1024]{2,1,0:T(8,128)(2,1)S(1)}, bf16[1,256,1024]{2,1,0:T(8,128)(2,1)}, u32[]{:S(2)}) copy-start(bf16[1,256,1024]{2,1,0:T(8,128)(2,1)} %emb_ref.1) | copy-start | bytes 1572868
  2.6 15.3 %collective-permute-start.3 = (bf16[256,1024]{1,0:T(8,128)(2,1)S(1)}, bf16[256,1024]{1,0:T(8,128)(2,1)S(1)}, u32[]{:S(2)}, u32[]{:S(2)}) collective-permute-start(bf16[256,1024]{1,0:T(8,128)(2,1)S(1)} %normalize.1.refs_3_), channel_id=1, source_target_pairs={{0,1},{1,0},{2,3},{3,2},{4,5},{5,4},{6,7},{7,6},{8,9},{9,8},{10,11... | collective-permute-start | bytes 1572872 | tf_op jit(solution)/shard_map/ppermute | solution.py:33
  4.8 18.0 %collective-permute-start.2 = (bf16[256,1024]{1,0:T(8,128)(2,1)S(1)}, bf16[256,1024]{1,0:T(8,128)(2,1)S(1)}, u32[]{:S(2)}, u32[]{:S(2)}) collective-permute-start(bf16[256,1024]{1,0:T(8,128)(2,1)S(1)} %normalize.1.refs_3_), channel_id=1, source_target_pairs={{0,8},{1,9},{2,10},{3,11},{4,12},{5,13},{6,14},{7,15},{8,16},{9,17... | collective-permute-start | bytes 1572872 | tf_op jit(solution)/shard_map/ppermute | solution.py:33
  4.9 17.8 %collective-permute-start.1 = (bf16[256,1024]{1,0:T(8,128)(2,1)S(1)}, bf16[256,1024]{1,0:T(8,128)(2,1)S(1)}, u32[]{:S(2)}, u32[]{:S(2)}) collective-permute-start(bf16[256,1024]{1,0:T(8,128)(2,1)S(1)} %normalize.1.refs_3_), channel_id=1, source_target_pairs={{0,248},{1,249},{2,250},{3,251},{4,252},{5,253},{6,254},{7,255},{8... | collective-permute-start | bytes 1572872 | tf_op jit(solution)/shard_map/ppermute | solution.py:33
  11.1 11.7 %collective-permute-start = (bf16[256,1024]{1,0:T(8,128)(2,1)S(1)}, bf16[256,1024]{1,0:T(8,128)(2,1)S(1)}, u32[]{:S(2)}, u32[]{:S(2)}) collective-permute-start(bf16[256,1024]{1,0:T(8,128)(2,1)S(1)} %normalize.1.refs_3_), channel_id=1, source_target_pairs={{0,2},{1,3},{2,0},{3,1},{4,6},{5,7},{6,4},{7,5},{8,10},{9,11},{10,... | collective-permute-start | bytes 1572872 | tf_op jit(solution)/shard_map/ppermute | solution.py:33
  11.1 0.7 copy-start.1
  22.8 15.3 %collective-permute-start.5 = (bf16[256,1024]{1,0:T(8,128)(2,1)S(1)}, bf16[256,1024]{1,0:T(8,128)(2,1)S(1)}, u32[]{:S(2)}, u32[]{:S(2)}) collective-permute-start(bf16[256,1024]{1,0:T(8,128)(2,1)S(1)} %collective-permute-done.3), channel_id=1, source_target_pairs={{0,248},{1,249},{2,250},{3,251},{4,252},{5,253},{6,254},{7,255},{8... | collective-permute-start | bytes 1572872 | tf_op jit(solution)/shard_map/ppermute | solution.py:33
  27.9 15.6 %collective-permute-start.7 = (bf16[256,1024]{1,0:T(8,128)(2,1)S(1)}, bf16[256,1024]{1,0:T(8,128)(2,1)S(1)}, u32[]{:S(2)}, u32[]{:S(2)}) collective-permute-start(bf16[256,1024]{1,0:T(8,128)(2,1)S(1)} %collective-permute-done.2.refs_5_), channel_id=1, source_target_pairs={{0,8},{1,9},{2,10},{3,11},{4,12},{5,13},{6,14},{7,15},{8,16},{9,17... | collective-permute-start | bytes 1572872 | tf_op jit(solution)/shard_map/ppermute | solution.py:33
  27.9 15.6 %collective-permute-start.6 = (bf16[256,1024]{1,0:T(8,128)(2,1)S(1)}, bf16[256,1024]{1,0:T(8,128)(2,1)S(1)}, u32[]{:S(2)}, u32[]{:S(2)}) collective-permute-start(bf16[256,1024]{1,0:T(8,128)(2,1)S(1)} %collective-permute-done.1.refs_1_.refs_7_.refs_3_), channel_id=1, source_target_pairs={{0,5},{1,4},{2,6},{3,7},{4,0},{5,1},{6,3},{7,2},{8,13},{9,12},{10,... | collective-permute-start | bytes 1572872 | tf_op jit(solution)/shard_map/ppermute | solution.py:33
  30.2 13.4 %collective-permute-start.4 = (bf16[256,1024]{1,0:T(8,128)(2,1)S(1)}, bf16[256,1024]{1,0:T(8,128)(2,1)S(1)}, u32[]{:S(2)}, u32[]{:S(2)}) collective-permute-start(bf16[256,1024]{1,0:T(8,128)(2,1)S(1)} %collective-permute-done.1.refs_1_.refs_7_.refs_3_), channel_id=1, source_target_pairs={{0,4},{1,5},{2,7},{3,6},{4,1},{5,0},{6,2},{7,3},{8,12},{9,13},{10,... | collective-permute-start | bytes 1572872 | tf_op jit(solution)/shard_map/ppermute | solution.py:33
  30.2 13.4 %collective-permute-start.10 = (bf16[256,1024]{1,0:T(8,128)(2,1)S(1)}, bf16[256,1024]{1,0:T(8,128)(2,1)S(1)}, u32[]{:S(2)}, u32[]{:S(2)}) collective-permute-start(bf16[256,1024]{1,0:T(8,128)(2,1)S(1)} %collective-permute-done.2.refs_5_), channel_id=1, source_target_pairs={{0,2},{1,3},{2,0},{3,1},{4,6},{5,7},{6,4},{7,5},{8,10},{9,11},{10,... | collective-permute-start | bytes 1572872 | tf_op jit(solution)/shard_map/ppermute | solution.py:33
  38.0 5.6 %collective-permute-start.9 = (bf16[256,1024]{1,0:T(8,128)(2,1)S(1)}, bf16[256,1024]{1,0:T(8,128)(2,1)S(1)}, u32[]{:S(2)}, u32[]{:S(2)}) collective-permute-start(bf16[256,1024]{1,0:T(8,128)(2,1)S(1)} %collective-permute-done.1.refs_1_.refs_7_.refs_3_), channel_id=1, source_target_pairs={{0,2},{1,3},{2,0},{3,1},{4,6},{5,7},{6,4},{7,5},{8,10},{9,11},{10,... | collective-permute-start | bytes 1572872 | tf_op jit(solution)/shard_map/ppermute | solution.py:33
  43.6 4.2 %collective-permute-start.8 = (bf16[256,1024]{1,0:T(8,128)(2,1)S(1)}, bf16[256,1024]{1,0:T(8,128)(2,1)S(1)}, u32[]{:S(2)}, u32[]{:S(2)}) collective-permute-start(bf16[256,1024]{1,0:T(8,128)(2,1)S(1)} %collective-permute-done.7.refs_1_), channel_id=1, source_target_pairs={{0,2},{1,3},{2,0},{3,1},{4,6},{5,7},{6,4},{7,5},{8,10},{9,11},{10,... | collective-permute-start | bytes 1572872 | tf_op jit(solution)/shard_map/ppermute | solution.py:33
  49.8 4.9 %collective-permute-start.13 = (f32[5,8,256]{2,1,0:T(8,128)S(1)}, f32[5,8,256]{2,1,0:T(8,128)S(1)}, u32[]{:S(2)}, u32[]{:S(2)}) collective-permute-start(f32[5,8,256]{2,1,0:T(8,128)S(1)} %get-tuple-element.32.own_ref), channel_id=1, source_target_pairs={{0,3},{1,2},{2,1},{3,0},{4,7},{5,6},{6,5},{7,4},{8,11},{9,10},{10,... | collective-permute-start | bytes 122888 | tf_op jit(solution)/shard_map/ppermute | solution.py:33
  52.9 1.9 %collective-permute-start.12 = (f32[5,8,256]{2,1,0:T(8,128)S(1)}, f32[5,8,256]{2,1,0:T(8,128)S(1)}, u32[]{:S(2)}, u32[]{:S(2)}) collective-permute-start(f32[5,8,256]{2,1,0:T(8,128)S(1)} %get-tuple-element.32.own_ref), channel_id=1, source_target_pairs={{0,2},{1,3},{2,0},{3,1},{4,6},{5,7},{6,4},{7,5},{8,10},{9,11},{10,... | collective-permute-start | bytes 122888 | tf_op jit(solution)/shard_map/ppermute | solution.py:33
  52.9 5.5 %collective-permute-start.11 = (f32[5,8,256]{2,1,0:T(8,128)S(1)}, f32[5,8,256]{2,1,0:T(8,128)S(1)}, u32[]{:S(2)}, u32[]{:S(2)}) collective-permute-start(f32[5,8,256]{2,1,0:T(8,128)S(1)} %get-tuple-element.32.own_ref), channel_id=1, source_target_pairs={{0,1},{1,0},{2,3},{3,2},{4,5},{5,4},{6,7},{7,6},{8,9},{9,8},{10,11... | collective-permute-start | bytes 122888 | tf_op jit(solution)/shard_map/ppermute | solution.py:33
  58.8 7.5 %collective-permute-start.17 = (f32[16,128]{1,0:T(8,128)S(1)}, f32[16,128]{1,0:T(8,128)S(1)}, u32[]{:S(2)}, u32[]{:S(2)}) collective-permute-start(f32[16,128]{1,0:T(8,128)S(1)} %score.1.own_ref), channel_id=1, source_target_pairs={{0,240},{1,241},{2,242},{3,243},{4,244},{5,245},{6,246},{7,247},{8... | collective-permute-start | bytes 24584 | tf_op jit(solution)/shard_map/ppermute | solution.py:33
  58.8 7.5 %collective-permute-start.16 = (f32[16,128]{1,0:T(8,128)S(1)}, f32[16,128]{1,0:T(8,128)S(1)}, u32[]{:S(2)}, u32[]{:S(2)}) collective-permute-start(f32[16,128]{1,0:T(8,128)S(1)} %score.1.own_ref), channel_id=1, source_target_pairs={{0,248},{1,249},{2,250},{3,251},{4,252},{5,253},{6,254},{7,255},{8... | collective-permute-start | bytes 24584 | tf_op jit(solution)/shard_map/ppermute | solution.py:33
  61.8 7.9 %collective-permute-start.15 = (f32[16,128]{1,0:T(8,128)S(1)}, f32[16,128]{1,0:T(8,128)S(1)}, u32[]{:S(2)}, u32[]{:S(2)}) collective-permute-start(f32[16,128]{1,0:T(8,128)S(1)} %score.1.own_ref), channel_id=1, source_target_pairs={{0,12},{1,13},{2,14},{3,15},{4,8},{5,9},{6,10},{7,11},{8,20},{9,21... | collective-permute-start | bytes 24584 | tf_op jit(solution)/shard_map/ppermute | solution.py:33
  64.2 7.0 %collective-permute-start.14 = (f32[16,128]{1,0:T(8,128)S(1)}, f32[16,128]{1,0:T(8,128)S(1)}, u32[]{:S(2)}, u32[]{:S(2)}) collective-permute-start(f32[16,128]{1,0:T(8,128)S(1)} %score.1.own_ref), channel_id=1, source_target_pairs={{0,8},{1,9},{2,10},{3,11},{4,12},{5,13},{6,14},{7,15},{8,16},{9,17... | collective-permute-start | bytes 24584 | tf_op jit(solution)/shard_map/ppermute | solution.py:33

commit v4 on v3

v4 whole, which is shorter than its diff:
```python
import functools

import jax
import jax.numpy as jnp
from jax import lax
from jax.experimental import pallas as pl
from jax.experimental.pallas import tpu as pltpu
from jax.sharding import PartitionSpec as P

STEPS = 12
WIDE = 64
AXES = ("cand", "tok")
GROUP = 4
LOW = -4.0
SMALL = pltpu.CompilerParams(vmem_limit_bytes=4 * 1024 * 1024)
LARGE = pltpu.CompilerParams(vmem_limit_bytes=8 * 1024 * 1024)
IN_VMEM = pl.BlockSpec(memory_space=pltpu.VMEM)
IN_SMEM = pl.BlockSpec(memory_space=pltpu.SMEM)
X_VALID, X_LEN, A_VALID, A_LEN, Y_LO, CORE = 0, 1, 8, 16, 24, 25


def place(flat):
    return flat // 8, (flat // 4) % 2, (flat // 2) % 2, flat % 2


def flat(group, y_lo, core, y_hi, groups):
    return (((group % groups) * 2 + y_lo) * 2 + core) * 2 + y_hi


def send(value, move):
    count = lax.axis_size(AXES)
    groups = count // 8
    pairs = [(i, flat(*move(*place(i)), groups)) for i in range(count)]
    return lax.ppermute(value, AXES, pairs)


def shift(dg=0, dl=0, dc=0, dh=0):
    return lambda g, l, c, h: (g + dg, l ^ dl, c ^ dc, h ^ dh)


def ring(way):
    def move(g, l, c, h):
        y = (2 * h + l + (way if c == 0 else -way)) % 4
        return (g, y % 2, c, y // 2)

    return move


PARTS = 4


def normalize_kernel(emb_ref, out_ref):
    step = out_ref.shape[0] // PARTS
    for i in range(PARTS):
        values = emb_ref[0, i * step : (i + 1) * step, :].astype(jnp.float32)
        factor = lax.rsqrt(jnp.sum(values * values, axis=-1, keepdims=True) + 1e-06)
        out_ref[i * step : (i + 1) * step, :] = (values * factor).astype(jnp.bfloat16)


def normalize(emb):
    _, rows, width = emb.shape
    return pl.pallas_call(
        normalize_kernel,
        in_specs=[IN_VMEM],
        out_specs=IN_VMEM,
        out_shape=jax.ShapeDtypeStruct((rows, width), jnp.bfloat16),
        compiler_params=SMALL,
        name="normalize",
    )(emb)


def plan_kernel(rows, ids_ref, len_ref, par_ref):
    group, y_lo, core, y_hi = (ids_ref[i] for i in range(4))
    cands = len_ref.shape[0]
    sub = lax.broadcasted_iota(jnp.int32, (8, 128), 0)
    lane = lax.broadcasted_iota(jnp.int32, (8, 128), 1)
    for f in range(2):
        side = core ^ f
        tile = jnp.zeros((8, 128), jnp.int32)
        for x in range(8):
            cand = GROUP * (group + 1 - x // 2) + 2 * y_lo + (side ^ (x % 2))
            length = len_ref[(cand + cands) % cands]
            tile = jnp.where((sub == x) & (lane == X_VALID), length - rows * y_hi, tile)
            tile = jnp.where((sub == x) & (lane == X_LEN), length, tile)
        for k in range(4):
            y = (2 * y_hi + y_lo + jnp.where(side == 0, 4 - k, k)) % 4
            length = len_ref[(GROUP * (group + 1) + 2 * (y % 2) + side) % cands]
            tile = jnp.where(lane == A_VALID + k, length - rows * (y // 2), tile)
            if k < 2:
                tile = jnp.where(lane == A_LEN + k, length, tile)
        tile = jnp.where(lane == Y_LO, y_lo, tile)
        tile = jnp.where(lane == CORE, side, tile)
        par_ref[8 * f : 8 * f + 8] = tile
        if f == 0:
            turned = jnp.zeros((8, 128), jnp.int32)
            for x in range(8):
                cand = GROUP * (group + 1 - x // 2) + 2 * y_lo + (core ^ (x % 2))
                length = len_ref[(cand + cands) % cands]
                turned = jnp.where(lane % 8 == x, length - rows * y_hi, turned)
            par_ref[16:24] = turned


def plan(ids, lengths, rows):
    return pl.pallas_call(
        functools.partial(plan_kernel, rows),
        in_specs=[IN_SMEM] * 2,
        out_specs=IN_VMEM,
        out_shape=jax.ShapeDtypeStruct((24, 128), jnp.int32),
        compiler_params=SMALL,
        name="plan",
    )(ids, lengths)


def scan_kernel(par_ref, *refs):
    xs, items, out_ref, best_ref = refs[:8], refs[8:12], refs[12], refs[13]
    rows = xs[0].shape[0]
    lane = lax.broadcasted_iota(jnp.int32, (1, rows), 1)
    sub = lax.broadcasted_iota(jnp.int32, (rows, 1), 0)
    lane128 = lax.broadcasted_iota(jnp.int32, (1, 128), 1)
    best_ref[...] = jnp.full(best_ref.shape, LOW, jnp.float32)
    for k in (0, 1, 3, 2):
        a_mask = lane < par_ref[0:1, A_VALID + k : A_VALID + k + 1]
        for x in range(8):
            if x == 0 and k % 2 == 0:
                out_ref[k, x : x + 1, :] = jnp.full((1, rows), LOW, jnp.float32)
                continue
            x_mask = sub < par_ref[x : x + 1, X_VALID : X_VALID + 1]
            at = slice(rows, 2 * rows) if x == 1 else slice(0, rows)
            sims = lax.dot_general(
                xs[x][at, :],
                items[k][...],
                (((1,), (1,)), ((), ())),
                preferred_element_type=jnp.float32,
            )
            best = jnp.max(jnp.where(a_mask, sims, LOW), axis=1, keepdims=True)
            best_ref[...] = jnp.where(lane128 == 8 * k + x, best, best_ref[...])
            col = jnp.max(jnp.where(x_mask, sims, LOW), axis=0, keepdims=True)
            out_ref[k, x : x + 1, :] = col
    best = best_ref[...]
    best = jnp.maximum(best, pltpu.roll(best, 128 - 16, 1))
    total = jnp.where(sub < par_ref[16:17, :], best, 0.0)
    total = jnp.sum(total, axis=0, keepdims=True)
    out_ref[4, :, 0:128] = jnp.broadcast_to(total, (8, 128))
    out_ref[4, :, 128:256] = jnp.zeros((8, 128), jnp.float32)


def scan(par, xs, items):
    rows, width = xs[0].shape
    count = len(xs) * len(items)
    return pl.pallas_call(
        scan_kernel,
        in_specs=[IN_VMEM] * (1 + len(xs) + len(items)),
        out_specs=IN_VMEM,
        out_shape=jax.ShapeDtypeStruct((5, 8, rows), jnp.float32),
        scratch_shapes=[pltpu.VMEM((rows, 128), jnp.float32)],
        compiler_params=LARGE,
        cost_estimate=pl.CostEstimate(
            flops=2 * count * rows * rows * width,
            bytes_accessed=2 * (len(xs) + len(items)) * rows * width,
            transcendentals=0,
        ),
        name="scan",
    )(par, *xs, *items)


def score_kernel(par_ref, own_ref, over_ref, out_ref, wide_ref):
    rows = own_ref.shape[2]
    lane = lax.broadcasted_iota(jnp.int32, (8, rows), 1)
    lane128 = lax.broadcasted_iota(jnp.int32, (8, 128), 1)
    sub128 = lax.broadcasted_iota(jnp.int32, (8, 128), 0)
    par = par_ref[0:8]
    x_len = par[:, X_LEN : X_LEN + 1].astype(jnp.float32)
    sums = []
    for k in range(4):
        col = jnp.maximum(own_ref[k], over_ref[k ^ 2])
        valid = lane < par[:, A_VALID + k : A_VALID + k + 1]
        sums.append(jnp.sum(jnp.where(valid, col, 0.0), axis=1, keepdims=True))
    precision = own_ref[4][:, :128] + over_ref[4][:, :128]
    tile = jnp.zeros((8, 128), jnp.float32)
    for p in range(2):
        a_len = par[:, A_LEN + p : A_LEN + p + 1].astype(jnp.float32)
        recall = (sums[p] + sums[p + 2]) / a_len
        mine = jnp.where(lane128 == 8 * p + sub128, precision, 0.0)
        mine = jnp.sum(mine, axis=1, keepdims=True) / x_len
        tile = jnp.where(lane128 == p, 0.5 * (mine + recall), tile)
    out_ref[...] = tile
    wide_ref[0:8] = tile
    wide_ref[8:] = jnp.zeros((WIDE - 8, 128), jnp.float32)


def score(par, own, over):
    return pl.pallas_call(
        score_kernel,
        in_specs=[IN_VMEM] * 3,
        out_specs=[IN_VMEM] * 2,
        out_shape=[
            jax.ShapeDtypeStruct((8, 128), jnp.float32),
            jax.ShapeDtypeStruct((WIDE, 128), jnp.float32),
        ],
        compiler_params=SMALL,
        name="score",
    )(par, own, over)


def put_kernel(par_ref, own_ref, same_ref, other_ref, one_ref, two_ref, out_ref):
    y_lo, core = par_ref[0:1, Y_LO : Y_LO + 1], par_ref[0:1, CORE : CORE + 1]
    sub = lax.broadcasted_iota(jnp.int32, (16, 128), 0)
    lane = lax.broadcasted_iota(jnp.int32, (16, 128), 1)
    f, d, e = sub // 8, (sub % 8) // 2, sub % 2
    own = 2 * y_lo + core

    def add(total, values, steps, base, used):
        n = values.shape[0]
        use = used & (steps >= 1) & (steps <= STEPS) & (lane[:n] == base + steps - 1)
        return total + jnp.where(use, values, 0.0)

    part = jnp.zeros((8, 128), jnp.float32)
    for p, ref in enumerate((same_ref, other_ref)):
        values = ref[0:8, p : p + 1]
        x = 2 * (y_lo ^ p) + (core ^ e[:8])
        steps = GROUP * d[:8] + own - x
        part = add(part, values, steps, STEPS, steps == steps)
        part = add(part, values, -steps, 0, d[:8] == 0)
    total = jnp.zeros((16, 128), jnp.float32)
    for dist, ref in enumerate((own_ref, one_ref, two_ref), 1):
        for p in range(2):
            values = ref[:, p : p + 1]
            a = 2 * (y_lo ^ p) + (core ^ f)
            total = add(total, values, GROUP * dist + a - own, 0, (d == dist) & (e == f))
    total = jnp.sum(total, axis=0, keepdims=True) + jnp.sum(part, axis=0, keepdims=True)
    out_ref[...] = total[:, : 2 * STEPS]


def put(par, own, same, other, one, two):
    return pl.pallas_call(
        put_kernel,
        in_specs=[IN_VMEM] * 6,
        out_specs=IN_VMEM,
        out_shape=jax.ShapeDtypeStruct((1, 2 * STEPS), jnp.float32),
        compiler_params=SMALL,
        name="put",
    )(par, own, same, other, one, two)


def on_device(embeddings, lengths):
    device = lax.axis_index("cand")
    rows = embeddings.shape[1]
    ids = jnp.stack(
        [device // 4, (device // 2) % 2, device % 2, lax.axis_index("tok")]
    ).astype(jnp.int32)
    par = plan(ids, lengths, rows)
    own = normalize(embeddings)

    left = send(own, shift(dg=1))
    right = send(own, shift(dg=-1))
    over = send(own, shift(dh=1))
    own_c = send(own, shift(dc=1))
    left, own_c, par = lax.optimization_barrier((left, own_c, par))
    far = send(left, shift(dg=1))
    item1 = send(right, ring(1))
    item3 = send(right, ring(-1))
    left2, right2, over = lax.optimization_barrier((left, right, over))
    pair_c = send(jnp.concatenate([left2, right2]), shift(dc=1))
    over, right = lax.optimization_barrier((over, right))
    item2 = send(over, shift(dg=-1))
    far_c = send(far, shift(dc=1))
    left_c, right_c = pair_c, pair_c
    xs = [right, right_c, own, own_c, left, left_c, far, far_c]
    message = scan(par, xs, [right, item1, item2, item3])

    tile, wide = score(par, message, send(message, shift(dh=1)))
    other = send(wide, shift(dg=1, dl=1))
    same = send(wide, shift(dg=1))
    tiles = jnp.concatenate([tile, send(tile, shift(dc=1))])
    one = send(tiles, shift(dg=-1))
    two = send(tiles, shift(dg=-2))
    return put(par, tiles, same, other, one, two)


def solution(mesh):
    in_specs = (P("cand", "tok", None), P())
    out_specs = P("cand", None)
    return jax.shard_map(
        on_device, mesh=mesh, in_specs=in_specs, out_specs=out_specs, check_vma=False
    )
```

time: 72.7 us -> 65.3 us (0.90)
  starting transfers between devices: 27.1 us -> 22.6 us
  Pallas kernels: 9.53 us -> 6.86 us
  waiting for transfers between devices: 33.5 us -> 34.4 us
    ppermute x18 -> x16, starting transfers between devices: 27.1 us -> 22.6 us  [send(): return lax.ppermute(value, AXES, pairs)]
    pallas_call x5 -> x3, Pallas kernels: 8.13 us -> 5.45 us  [the longest x1 4.98 us: scan(): pl.pallas_call(scan_kernel, in_specs=[IN_VMEM] * (1 + len(xs) + len(items...]
    ppermute x18 -> x16, waiting for transfers between devices: 33.5 us -> 34.4 us  [send(): return lax.ppermute(value, AXES, pairs)]
    unnamed x4 -> x5, local copies, waits for them, and re-layouts: 1.62 us -> 1.05 us
  transfers between devices with their start and end apart: 18 -> 16, of which waited for: 8 -> 7; matrix products, arithmetic and copies ran while one was open for 0% -> 0% of each run, Pallas kernels for 7% -> 1%
where the time goes in v4:
time: 65.3 us; the launch traced here: 65.2 us
  waiting for transfers between devices  34.4 us (53%)
  starting transfers between devices  22.6 us (35%)
  Pallas kernels  6.86 us (11%)
  local copies, waits for them, and re-layouts  1.05 us (2%)
    ppermute x16, waiting for transfers between devices, send(): return lax.ppermute(value, AXES, pairs)  34.4 us
    ppermute x16, starting transfers between devices, send(): return lax.ppermute(value, AXES, pairs)  22.6 us
    pallas_call x1, Pallas kernels, scan(): pl.pallas_call(scan_kernel, in_specs=[IN_VMEM] * (1 + len(xs) + len(items...  4.98 us
  transfers between devices with their start and end apart: 16, of which 7 were waited for; matrix products, arithmetic and copies ran while one was open for 0% of the time, Pallas kernels for 1%

profile of v4, /device:TPU:16, one launch (start us, length us, event | category | flops | bytes accessed | tf_op | source)
XLA Modules:
  0.0 65.2 jit_solution(5612105089524494873)
XLA Ops:
  0.0 1.0 %copy-done = bf16[1,256,1024]{2,1,0:T(8,128)(2,1)S(1)} copy-done((bf16[1,256,1024]{2,1,0:T(8,128)(2,1)S(1)}, bf16[1,256,1024]{2,1,0:T(8,128)(2,1)}, u32[]{:S(2)}) %copy-start) | copy-done | bytes 524312
  1.0 0.2 normalize.1.refs_2_
  1.2 2.0 %collective-permute-start = (bf16[256,1024]{1,0:T(8,128)(2,1)S(1)}, bf16[256,1024]{1,0:T(8,128)(2,1)S(1)}, u32[]{:S(2)}, u32[]{:S(2)}) collective-permute-start(bf16[256,1024]{1,0:T(8,128)(2,1)S(1)} %normalize.1.refs_2_), channel_id=1, source_target_pairs={{0,8},{1,9},{2,10},{3,11},{4,12},{5,13},{6,14},{7,15},{8,16},{9,17... | collective-permute-start | bytes 1572872 | tf_op jit(solution)/shard_map/ppermute | solution.py:34
  3.2 6.3 %collective-permute-start.2 = (bf16[256,1024]{1,0:T(8,128)(2,1)S(1)}, bf16[256,1024]{1,0:T(8,128)(2,1)S(1)}, u32[]{:S(2)}, u32[]{:S(2)}) collective-permute-start(bf16[256,1024]{1,0:T(8,128)(2,1)S(1)} %normalize.1.refs_2_), channel_id=1, source_target_pairs={{0,248},{1,249},{2,250},{3,251},{4,252},{5,253},{6,254},{7,255},{8... | collective-permute-start | bytes 1572872 | tf_op jit(solution)/shard_map/ppermute | solution.py:34
  9.6 0.3 collective-permute-start.3
  10.0 0.7 %plan.1.par_ref = s32[24,128]{1,0:T(8,128)S(1)} custom-call(s32[4]{0:T(128)S(1)} %pad_add_fusion.ids_ref, s32[128]{0:T(128)S(1)} %copy-done.1), custom_call_target="tpu_custom_call" | custom-call | tf_op jit(solution)/shard_map/plan/pallas_call | solution.py:104
  10.7 10.6 %collective-permute-done.refs_4_ = bf16[256,1024]{1,0:T(8,128)(2,1)S(1)} collective-permute-done((bf16[256,1024]{1,0:T(8,128)(2,1)S(1)}, bf16[256,1024]{1,0:T(8,128)(2,1)S(1)}, u32[]{:S(2)}, u32[]{:S(2)}) %collective-permute-start) | collective-permute-done | bytes 524320 | tf_op jit(solution)/shard_map/ppermute | solution.py:34
  21.3 3.7 %collective-permute-done.3 = bf16[256,1024]{1,0:T(8,128)(2,1)S(1)} collective-permute-done((bf16[256,1024]{1,0:T(8,128)(2,1)S(1)}, bf16[256,1024]{1,0:T(8,128)(2,1)S(1)}, u32[]{:S(2)}, u32[]{:S(2)}) %collective-permute-start.3) | collective-permute-done | bytes 524320 | tf_op jit(solution)/shard_map/ppermute | solution.py:34
  25.1 0.1 collective-permute-start.4
  25.2 2.2 %collective-permute-start.8 = (bf16[256,1024]{1,0:T(8,128)(2,1)S(1)}, bf16[256,1024]{1,0:T(8,128)(2,1)S(1)}, u32[]{:S(2)}, u32[]{:S(2)}) collective-permute-start(bf16[256,1024]{1,0:T(8,128)(2,1)S(1)} %collective-permute-done.3), channel_id=1, source_target_pairs={{0,248},{1,249},{2,250},{3,251},{4,252},{5,253},{6,254},{7,255},{8... | collective-permute-start | bytes 1572872 | tf_op jit(solution)/shard_map/ppermute | solution.py:34
  27.4 1.3 %collective-permute-start.7 = (bf16[256,1024]{1,0:T(8,128)(2,1)S(1)}, bf16[256,1024]{1,0:T(8,128)(2,1)S(1)}, u32[]{:S(2)}, u32[]{:S(2)}) collective-permute-start(bf16[256,1024]{1,0:T(8,128)(2,1)S(1)} %collective-permute-done.2.refs_0_.refs_8_), channel_id=1, source_target_pairs={{0,4},{1,5},{2,7},{3,6},{4,1},{5,0},{6,2},{7,3},{8,12},{9,13},{10,... | collective-permute-start | bytes 1572872 | tf_op jit(solution)/shard_map/ppermute | solution.py:34
  28.7 0.7 %collective-permute-start.9 = (bf16[256,1024]{1,0:T(8,128)(2,1)S(1)}, bf16[256,1024]{1,0:T(8,128)(2,1)S(1)}, u32[]{:S(2)}, u32[]{:S(2)}) collective-permute-start(bf16[256,1024]{1,0:T(8,128)(2,1)S(1)} %collective-permute-done.2.refs_0_.refs_8_), channel_id=1, source_target_pairs={{0,5},{1,4},{2,6},{3,7},{4,0},{5,1},{6,3},{7,2},{8,13},{9,12},{10,... | collective-permute-start | bytes 1572872 | tf_op jit(solution)/shard_map/ppermute | solution.py:34
  29.4 8.3 %collective-permute-done.5.refs_6_ = bf16[256,1024]{1,0:T(8,128)(2,1)S(1)} collective-permute-done((bf16[256,1024]{1,0:T(8,128)(2,1)S(1)}, bf16[256,1024]{1,0:T(8,128)(2,1)S(1)}, u32[]{:S(2)}, u32[]{:S(2)}) %collective-permute-start.5) | collective-permute-done | bytes 524320 | tf_op jit(solution)/shard_map/ppermute | solution.py:34
  37.7 1.8 %collective-permute-done.8.refs_10_ = bf16[256,1024]{1,0:T(8,128)(2,1)S(1)} collective-permute-done((bf16[256,1024]{1,0:T(8,128)(2,1)S(1)}, bf16[256,1024]{1,0:T(8,128)(2,1)S(1)}, u32[]{:S(2)}, u32[]{:S(2)}) %collective-permute-start.8) | collective-permute-done | bytes 524320 | tf_op jit(solution)/shard_map/ppermute | solution.py:34
  39.6 2.0 %collective-permute-done.7.refs_9_ = bf16[256,1024]{1,0:T(8,128)(2,1)S(1)} collective-permute-done((bf16[256,1024]{1,0:T(8,128)(2,1)S(1)}, bf16[256,1024]{1,0:T(8,128)(2,1)S(1)}, u32[]{:S(2)}, u32[]{:S(2)}) %collective-permute-start.7) | collective-permute-done | bytes 524320 | tf_op jit(solution)/shard_map/ppermute | solution.py:34
  41.6 5.0 %scan.1.own_ref = f32[5,8,256]{2,1,0:T(8,128)S(1)} custom-call(s32[24,128]{1,0:T(8,128)S(1)} %plan.1.par_ref, bf16[256,1024]{1,0:T(8,128)(2,1)S(1)} %collective-permute-done.2.refs_0_.refs_8_, bf16[512,1024]{1,0:T(8,128)(2,1)S(1)} %collective-permute-done.4.refs_1_.refs_5_, bf16[256,1024]{1,0:T(8,128)(2,1)S(1)} %normalize.1.refs_2_, ...), custom_call_target="tpu_custom_call" | custom-call | flops 4294967296 | bytes 6291456 | tf_op jit(solution)/shard_map/scan/pallas_call | solution.py:150
  46.5 1.0 %collective-permute-start.10 = (f32[5,8,256]{2,1,0:T(8,128)S(1)}, f32[5,8,256]{2,1,0:T(8,128)S(1)}, u32[]{:S(2)}, u32[]{:S(2)}) collective-permute-start(f32[5,8,256]{2,1,0:T(8,128)S(1)} %scan.1.own_ref), channel_id=1, source_target_pairs={{0,1},{1,0},{2,3},{3,2},{4,5},{5,4},{6,7},{7,6},{8,9},{9,8},{10,11... | collective-permute-start | bytes 122888 | tf_op jit(solution)/shard_map/ppermute | solution.py:34
  47.5 4.8 %collective-permute-done.10.over_ref = f32[5,8,256]{2,1,0:T(8,128)S(1)} collective-permute-done((f32[5,8,256]{2,1,0:T(8,128)S(1)}, f32[5,8,256]{2,1,0:T(8,128)S(1)}, u32[]{:S(2)}, u32[]{:S(2)}) %collective-permute-start.10) | collective-permute-done | bytes 40992 | tf_op jit(solution)/shard_map/ppermute | solution.py:34
  52.3 0.3 score.1
  52.7 1.8 %collective-permute-start.13 = (f32[64,128]{1,0:T(8,128)S(1)}, f32[64,128]{1,0:T(8,128)S(1)}, u32[]{:S(2)}, u32[]{:S(2)}) collective-permute-start(f32[64,128]{1,0:T(8,128)S(1)} %get-tuple-element.24), channel_id=1, source_target_pairs={{0,12},{1,13},{2,14},{3,15},{4,8},{5,9},{6,10},{7,11},{8,20},{9,21... | collective-permute-start | bytes 98312 | tf_op jit(solution)/shard_map/ppermute | solution.py:34
  54.5 5.4 %collective-permute-start.14 = (f32[16,128]{1,0:T(8,128)S(1)}, f32[16,128]{1,0:T(8,128)S(1)}, u32[]{:S(2)}, u32[]{:S(2)}) collective-permute-start(f32[16,128]{1,0:T(8,128)S(1)} %constant_dynamic-update-slice_fusion.own_ref), channel_id=1, source_target_pairs={{0,248},{1,249},{2,250},{3,251},{4,252},{5,253},{6,254},{7,255},{8... | collective-permute-start | bytes 24584 | tf_op jit(solution)/shard_map/ppermute | solution.py:34
  59.9 1.4 %collective-permute-start.15 = (f32[16,128]{1,0:T(8,128)S(1)}, f32[16,128]{1,0:T(8,128)S(1)}, u32[]{:S(2)}, u32[]{:S(2)}) collective-permute-start(f32[16,128]{1,0:T(8,128)S(1)} %constant_dynamic-update-slice_fusion.own_ref), channel_id=1, source_target_pairs={{0,240},{1,241},{2,242},{3,243},{4,244},{5,245},{6,246},{7,247},{8... | collective-permute-start | bytes 24584 | tf_op jit(solution)/shard_map/ppermute | solution.py:34
  61.3 3.1 %collective-permute-done.15.two_ref = f32[16,128]{1,0:T(8,128)S(1)} collective-permute-done((f32[16,128]{1,0:T(8,128)S(1)}, f32[16,128]{1,0:T(8,128)S(1)}, u32[]{:S(2)}, u32[]{:S(2)}) %collective-permute-start.15) | collective-permute-done | bytes 8224 | tf_op jit(solution)/shard_map/ppermute | solution.py:34
  64.4 0.7 %put.1 = f32[1,24]{1,0:T(1,128)} custom-call(s32[24,128]{1,0:T(8,128)S(1)} %plan.1.par_ref, f32[16,128]{1,0:T(8,128)S(1)} %constant_dynamic-update-slice_fusion.own_ref, f32[64,128]{1,0:T(8,128)S(1)} %collective-permute-done.12.same_ref, f32[64,128]{1,0:T(8,128)S(1)} %collective-permute-done.13.other_ref, f32[16,128]{1,0:T(8,128)S(1)} %collective-permute-done.14.one_ref, ...), custom_call_target="tpu_custom_call" | custom-call | tf_op jit(solution)/shard_map/put/pallas_call | solution.py:235
  (21 shorter events, 0.3 us)
Async XLA Ops:
  0.0 1.0 %copy-start = (bf16[1,256,1024]{2,1,0:T(8,128)(2,1)S(1)}, bf16[1,256,1024]{2,1,0:T(8,128)(2,1)}, u32[]{:S(2)}) copy-start(bf16[1,256,1024]{2,1,0:T(8,128)(2,1)} %emb_ref.1) | copy-start | bytes 1572868
  1.0 8.9 %copy-start.1 = (s32[128]{0:T(128)S(1)}, s32[128]{0:T(128)}, u32[]{:S(2)}) copy-start(s32[128]{0:T(128)} %len_ref.1) | copy-start | bytes 1540
  1.2 20.1 %collective-permute-start = (bf16[256,1024]{1,0:T(8,128)(2,1)S(1)}, bf16[256,1024]{1,0:T(8,128)(2,1)S(1)}, u32[]{:S(2)}, u32[]{:S(2)}) collective-permute-start(bf16[256,1024]{1,0:T(8,128)(2,1)S(1)} %normalize.1.refs_2_), channel_id=1, source_target_pairs={{0,8},{1,9},{2,10},{3,11},{4,12},{5,13},{6,14},{7,15},{8,16},{9,17... | collective-permute-start | bytes 1572872 | tf_op jit(solution)/shard_map/ppermute | solution.py:34
  3.2 18.1 %collective-permute-start.1 = (bf16[256,1024]{1,0:T(8,128)(2,1)S(1)}, bf16[256,1024]{1,0:T(8,128)(2,1)S(1)}, u32[]{:S(2)}, u32[]{:S(2)}) collective-permute-start(bf16[256,1024]{1,0:T(8,128)(2,1)S(1)} %normalize.1.refs_2_), channel_id=1, source_target_pairs={{0,2},{1,3},{2,0},{3,1},{4,6},{5,7},{6,4},{7,5},{8,10},{9,11},{10,... | collective-permute-start | bytes 1572872 | tf_op jit(solution)/shard_map/ppermute | solution.py:34
  3.2 18.1 %collective-permute-start.2 = (bf16[256,1024]{1,0:T(8,128)(2,1)S(1)}, bf16[256,1024]{1,0:T(8,128)(2,1)S(1)}, u32[]{:S(2)}, u32[]{:S(2)}) collective-permute-start(bf16[256,1024]{1,0:T(8,128)(2,1)S(1)} %normalize.1.refs_2_), channel_id=1, source_target_pairs={{0,248},{1,249},{2,250},{3,251},{4,252},{5,253},{6,254},{7,255},{8... | collective-permute-start | bytes 1572872 | tf_op jit(solution)/shard_map/ppermute | solution.py:34
  9.6 15.5 %collective-permute-start.3 = (bf16[256,1024]{1,0:T(8,128)(2,1)S(1)}, bf16[256,1024]{1,0:T(8,128)(2,1)S(1)}, u32[]{:S(2)}, u32[]{:S(2)}) collective-permute-start(bf16[256,1024]{1,0:T(8,128)(2,1)S(1)} %normalize.1.refs_2_), channel_id=1, source_target_pairs={{0,1},{1,0},{2,3},{3,2},{4,5},{5,4},{6,7},{7,6},{8,9},{9,8},{10,11... | collective-permute-start | bytes 1572872 | tf_op jit(solution)/shard_map/ppermute | solution.py:34
  21.3 16.4 %collective-permute-start.5 = (bf16[256,1024]{1,0:T(8,128)(2,1)S(1)}, bf16[256,1024]{1,0:T(8,128)(2,1)S(1)}, u32[]{:S(2)}, u32[]{:S(2)}) collective-permute-start(bf16[256,1024]{1,0:T(8,128)(2,1)S(1)} %collective-permute-done.refs_4_), channel_id=1, source_target_pairs={{0,8},{1,9},{2,10},{3,11},{4,12},{5,13},{6,14},{7,15},{8,16},{9,17... | collective-permute-start | bytes 1572872 | tf_op jit(solution)/shard_map/ppermute | solution.py:34
  25.1 16.4 %collective-permute-start.4 = (bf16[512,1024]{1,0:T(8,128)(2,1)S(1)}, bf16[512,1024]{1,0:T(8,128)(2,1)S(1)}, u32[]{:S(2)}, u32[]{:S(2)}) collective-permute-start(bf16[512,1024]{1,0:T(8,128)(2,1)S(1)} %pad_maximum_fusion), channel_id=1, source_target_pairs={{0,2},{1,3},{2,0},{3,1},{4,6},{5,7},{6,4},{7,5},{8,10},{9,11},{10,... | collective-permute-start | bytes 3145736 | tf_op jit(solution)/shard_map/ppermute | solution.py:34
  25.2 14.3 %collective-permute-start.8 = (bf16[256,1024]{1,0:T(8,128)(2,1)S(1)}, bf16[256,1024]{1,0:T(8,128)(2,1)S(1)}, u32[]{:S(2)}, u32[]{:S(2)}) collective-permute-start(bf16[256,1024]{1,0:T(8,128)(2,1)S(1)} %collective-permute-done.3), channel_id=1, source_target_pairs={{0,248},{1,249},{2,250},{3,251},{4,252},{5,253},{6,254},{7,255},{8... | collective-permute-start | bytes 1572872 | tf_op jit(solution)/shard_map/ppermute | solution.py:34
  27.4 14.2 %collective-permute-start.7 = (bf16[256,1024]{1,0:T(8,128)(2,1)S(1)}, bf16[256,1024]{1,0:T(8,128)(2,1)S(1)}, u32[]{:S(2)}, u32[]{:S(2)}) collective-permute-start(bf16[256,1024]{1,0:T(8,128)(2,1)S(1)} %collective-permute-done.2.refs_0_.refs_8_), channel_id=1, source_target_pairs={{0,4},{1,5},{2,7},{3,6},{4,1},{5,0},{6,2},{7,3},{8,12},{9,13},{10,... | collective-permute-start | bytes 1572872 | tf_op jit(solution)/shard_map/ppermute | solution.py:34
  28.7 12.9 %collective-permute-start.9 = (bf16[256,1024]{1,0:T(8,128)(2,1)S(1)}, bf16[256,1024]{1,0:T(8,128)(2,1)S(1)}, u32[]{:S(2)}, u32[]{:S(2)}) collective-permute-start(bf16[256,1024]{1,0:T(8,128)(2,1)S(1)} %collective-permute-done.2.refs_0_.refs_8_), channel_id=1, source_target_pairs={{0,5},{1,4},{2,6},{3,7},{4,0},{5,1},{6,3},{7,2},{8,13},{9,12},{10,... | collective-permute-start | bytes 1572872 | tf_op jit(solution)/shard_map/ppermute | solution.py:34
  37.7 3.8 %collective-permute-start.6 = (bf16[256,1024]{1,0:T(8,128)(2,1)S(1)}, bf16[256,1024]{1,0:T(8,128)(2,1)S(1)}, u32[]{:S(2)}, u32[]{:S(2)}) collective-permute-start(bf16[256,1024]{1,0:T(8,128)(2,1)S(1)} %collective-permute-done.5.refs_6_), channel_id=1, source_target_pairs={{0,2},{1,3},{2,0},{3,1},{4,6},{5,7},{6,4},{7,5},{8,10},{9,11},{10,... | collective-permute-start | bytes 1572872 | tf_op jit(solution)/shard_map/ppermute | solution.py:34
  46.5 5.8 %collective-permute-start.10 = (f32[5,8,256]{2,1,0:T(8,128)S(1)}, f32[5,8,256]{2,1,0:T(8,128)S(1)}, u32[]{:S(2)}, u32[]{:S(2)}) collective-permute-start(f32[5,8,256]{2,1,0:T(8,128)S(1)} %scan.1.own_ref), channel_id=1, source_target_pairs={{0,1},{1,0},{2,3},{3,2},{4,5},{5,4},{6,7},{7,6},{8,9},{9,8},{10,11... | collective-permute-start | bytes 122888 | tf_op jit(solution)/shard_map/ppermute | solution.py:34
  52.6 1.9 %collective-permute-start.11 = (f32[8,128]{1,0:T(8,128)S(1)}, f32[8,128]{1,0:T(8,128)S(1)}, u32[]{:S(2)}, u32[]{:S(2)}) collective-permute-start(f32[8,128]{1,0:T(8,128)S(1)} %get-tuple-element.23), channel_id=1, source_target_pairs={{0,2},{1,3},{2,0},{3,1},{4,6},{5,7},{6,4},{7,5},{8,10},{9,11},{10,... | collective-permute-start | bytes 12296 | tf_op jit(solution)/shard_map/ppermute | solution.py:34
  52.6 11.8 %collective-permute-start.12 = (f32[64,128]{1,0:T(8,128)S(1)}, f32[64,128]{1,0:T(8,128)S(1)}, u32[]{:S(2)}, u32[]{:S(2)}) collective-permute-start(f32[64,128]{1,0:T(8,128)S(1)} %get-tuple-element.24), channel_id=1, source_target_pairs={{0,8},{1,9},{2,10},{3,11},{4,12},{5,13},{6,14},{7,15},{8,16},{9,17... | collective-permute-start | bytes 98312 | tf_op jit(solution)/shard_map/ppermute | solution.py:34
  52.7 11.8 %collective-permute-start.13 = (f32[64,128]{1,0:T(8,128)S(1)}, f32[64,128]{1,0:T(8,128)S(1)}, u32[]{:S(2)}, u32[]{:S(2)}) collective-permute-start(f32[64,128]{1,0:T(8,128)S(1)} %get-tuple-element.24), channel_id=1, source_target_pairs={{0,12},{1,13},{2,14},{3,15},{4,8},{5,9},{6,10},{7,11},{8,20},{9,21... | collective-permute-start | bytes 98312 | tf_op jit(solution)/shard_map/ppermute | solution.py:34
  54.5 6.9 %collective-permute-start.14 = (f32[16,128]{1,0:T(8,128)S(1)}, f32[16,128]{1,0:T(8,128)S(1)}, u32[]{:S(2)}, u32[]{:S(2)}) collective-permute-start(f32[16,128]{1,0:T(8,128)S(1)} %constant_dynamic-update-slice_fusion.own_ref), channel_id=1, source_target_pairs={{0,248},{1,249},{2,250},{3,251},{4,252},{5,253},{6,254},{7,255},{8... | collective-permute-start | bytes 24584 | tf_op jit(solution)/shard_map/ppermute | solution.py:34
  59.9 4.5 %collective-permute-start.15 = (f32[16,128]{1,0:T(8,128)S(1)}, f32[16,128]{1,0:T(8,128)S(1)}, u32[]{:S(2)}, u32[]{:S(2)}) collective-permute-start(f32[16,128]{1,0:T(8,128)S(1)} %constant_dynamic-update-slice_fusion.own_ref), channel_id=1, source_target_pairs={{0,240},{1,241},{2,242},{3,243},{4,244},{5,245},{6,246},{7,247},{8... | collective-permute-start | bytes 24584 | tf_op jit(solution)/shard_map/ppermute | solution.py:34

commit v5 on v4

--- a/solution.py
+++ b/solution.py
@@ -52,13 +52,13 @@
 def normalize_kernel(emb_ref, out_ref):
     step = out_ref.shape[0] // PARTS
     for i in range(PARTS):
-        values = emb_ref[0, i * step : (i + 1) * step, :].astype(jnp.float32)
+        values = emb_ref[i * step : (i + 1) * step, :].astype(jnp.float32)
         factor = lax.rsqrt(jnp.sum(values * values, axis=-1, keepdims=True) + 1e-06)
         out_ref[i * step : (i + 1) * step, :] = (values * factor).astype(jnp.bfloat16)
 
 
 def normalize(emb):
-    _, rows, width = emb.shape
+    rows, width = emb.shape
     return pl.pallas_call(
         normalize_kernel,
         in_specs=[IN_VMEM],
@@ -249,20 +249,21 @@
         [device // 4, (device // 2) % 2, device % 2, lax.axis_index("tok")]
     ).astype(jnp.int32)
     par = plan(ids, lengths, rows)
-    own = normalize(embeddings)
-
-    left = send(own, shift(dg=1))
-    right = send(own, shift(dg=-1))
-    over = send(own, shift(dh=1))
+    raw = embeddings[0]
+    left_raw = send(raw, shift(dg=1))
+    right = normalize(send(raw, shift(dg=-1)))
+    over = send(raw, shift(dh=1))
+    own = normalize(raw)
     own_c = send(own, shift(dc=1))
-    left, own_c, par = lax.optimization_barrier((left, own_c, par))
-    far = send(left, shift(dg=1))
+    left_raw, par = lax.optimization_barrier((left_raw, par))
+    far = normalize(send(left_raw, shift(dg=1)))
+    left = normalize(left_raw)
     item1 = send(right, ring(1))
     item3 = send(right, ring(-1))
     left2, right2, over = lax.optimization_barrier((left, right, over))
     pair_c = send(jnp.concatenate([left2, right2]), shift(dc=1))
-    over, right = lax.optimization_barrier((over, right))
-    item2 = send(over, shift(dg=-1))
+    over, right, own_c = lax.optimization_barrier((over, right, own_c))
+    item2 = normalize(send(over, shift(dg=-1)))
     far_c = send(far, shift(dc=1))
     left_c, right_c = pair_c, pair_c
     xs = [right, right_c, own, own_c, left, left_c, far, far_c]

time: 65.3 us -> 63.8 us (0.977)
  waiting for transfers between devices: 34.4 us -> 31.5 us
  starting transfers between devices: 22.6 us -> 23.4 us
    ppermute x16, waiting for transfers between devices: 34.4 us -> 31.5 us  [send(): return lax.ppermute(value, AXES, pairs)]
    ppermute x16, starting transfers between devices: 22.6 us -> 23.4 us  [send(): return lax.ppermute(value, AXES, pairs)]
    pallas_call x1 -> x5, Pallas kernels: 0.19 us -> 0.95 us  [normalize(): pl.pallas_call(normalize_kernel, in_specs=[IN_VMEM], out_specs=IN_VMEM, o...]
  transfers between devices with their start and end apart: 16 -> 16, of which waited for: 7 -> 7; matrix products, arithmetic and copies ran while one was open for 0% -> 0% of each run, Pallas kernels for 1% -> 3%
where the time goes in v5:
time: 63.8 us; the launch traced here: 63.7 us
  waiting for transfers between devices  31.5 us (49%)
  starting transfers between devices  23.4 us (37%)
  Pallas kernels  7.47 us (12%)
  local copies, waits for them, and re-layouts  1.08 us (2%)
    ppermute x16, waiting for transfers between devices, send(): return lax.ppermute(value, AXES, pairs)  31.5 us
    ppermute x16, starting transfers between devices, send(): return lax.ppermute(value, AXES, pairs)  23.4 us
    pallas_call x1, Pallas kernels, scan(): pl.pallas_call(scan_kernel, in_specs=[IN_VMEM] * (1 + len(xs) + len(items...  4.83 us
  transfers between devices with their start and end apart: 16, of which 7 were waited for; matrix products, arithmetic and copies ran while one was open for 0% of the time, Pallas kernels for 3%

profile of v5, /device:TPU:16, one launch (start us, length us, event | category | flops | bytes accessed | tf_op | source)
XLA Modules:
  0.0 63.7 jit_solution(15637264557007505451)
XLA Ops:
  0.0 1.9 %collective-permute-start = (bf16[256,1024]{1,0:T(8,128)(2,1)}, bf16[256,1024]{1,0:T(8,128)(2,1)S(1)}, u32[]{:S(2)}, u32[]{:S(2)}) collective-permute-start(bf16[256,1024]{1,0:T(8,128)(2,1)} %bitcast.5), channel_id=1, source_target_pairs={{0,8},{1,9},{2,10},{3,11},{4,12},{5,13},{6,14},{7,15},{8,16},{9,17... | collective-permute-start | bytes 1572872 | tf_op jit(solution)/shard_map/ppermute | solution.py:34
  1.9 6.2 %collective-permute-start.1 = (bf16[256,1024]{1,0:T(8,128)(2,1)}, bf16[256,1024]{1,0:T(8,128)(2,1)S(1)}, u32[]{:S(2)}, u32[]{:S(2)}) collective-permute-start(bf16[256,1024]{1,0:T(8,128)(2,1)} %bitcast.6), channel_id=1, source_target_pairs={{0,248},{1,249},{2,250},{3,251},{4,252},{5,253},{6,254},{7,255},{8... | collective-permute-start | bytes 1572872 | tf_op jit(solution)/shard_map/ppermute | solution.py:34
  8.1 0.3 collective-permute-start.2
  8.5 1.1 %copy-done = bf16[1,256,1024]{2,1,0:T(8,128)(2,1)S(1)} copy-done((bf16[1,256,1024]{2,1,0:T(8,128)(2,1)S(1)}, bf16[1,256,1024]{2,1,0:T(8,128)(2,1)}, u32[]{:S(2)}) %copy-start) | copy-done | bytes 524312
  10.0 0.7 %plan.1.par_ref = s32[24,128]{1,0:T(8,128)S(1)} custom-call(s32[4]{0:T(128)S(1)} %pad_add_fusion.ids_ref, s32[128]{0:T(128)S(1)} %copy-done.1), custom_call_target="tpu_custom_call" | custom-call | tf_op jit(solution)/shard_map/plan/pallas_call | solution.py:104
  10.7 9.5 %collective-permute-done.emb_ref = bf16[256,1024]{1,0:T(8,128)(2,1)S(1)} collective-permute-done((bf16[256,1024]{1,0:T(8,128)(2,1)}, bf16[256,1024]{1,0:T(8,128)(2,1)S(1)}, u32[]{:S(2)}, u32[]{:S(2)}) %collective-permute-start) | collective-permute-done | bytes 524320 | tf_op jit(solution)/shard_map/ppermute | solution.py:34
  20.5 0.2 normalize.6.refs_0_.refs_8_
  20.7 2.6 %collective-permute-done.2 = bf16[256,1024]{1,0:T(8,128)(2,1)S(1)} collective-permute-done((bf16[256,1024]{1,0:T(8,128)(2,1)}, bf16[256,1024]{1,0:T(8,128)(2,1)S(1)}, u32[]{:S(2)}, u32[]{:S(2)}) %collective-permute-start.2) | collective-permute-done | bytes 524320 | tf_op jit(solution)/shard_map/ppermute | solution.py:34
  23.4 2.9 %collective-permute-start.8 = (bf16[256,1024]{1,0:T(8,128)(2,1)S(1)}, bf16[256,1024]{1,0:T(8,128)(2,1)S(1)}, u32[]{:S(2)}, u32[]{:S(2)}) collective-permute-start(bf16[256,1024]{1,0:T(8,128)(2,1)S(1)} %collective-permute-done.2), channel_id=1, source_target_pairs={{0,248},{1,249},{2,250},{3,251},{4,252},{5,253},{6,254},{7,255},{8... | collective-permute-start | bytes 1572872 | tf_op jit(solution)/shard_map/ppermute | solution.py:34
  26.3 1.3 %collective-permute-start.7 = (bf16[256,1024]{1,0:T(8,128)(2,1)S(1)}, bf16[256,1024]{1,0:T(8,128)(2,1)S(1)}, u32[]{:S(2)}, u32[]{:S(2)}) collective-permute-start(bf16[256,1024]{1,0:T(8,128)(2,1)S(1)} %normalize.6.refs_0_.refs_8_), channel_id=1, source_target_pairs={{0,4},{1,5},{2,7},{3,6},{4,1},{5,0},{6,2},{7,3},{8,12},{9,13},{10,... | collective-permute-start | bytes 1572872 | tf_op jit(solution)/shard_map/ppermute | solution.py:34
  27.6 0.7 %collective-permute-start.9 = (bf16[256,1024]{1,0:T(8,128)(2,1)S(1)}, bf16[256,1024]{1,0:T(8,128)(2,1)S(1)}, u32[]{:S(2)}, u32[]{:S(2)}) collective-permute-start(bf16[256,1024]{1,0:T(8,128)(2,1)S(1)} %normalize.6.refs_0_.refs_8_), channel_id=1, source_target_pairs={{0,5},{1,4},{2,6},{3,7},{4,0},{5,1},{6,3},{7,2},{8,13},{9,12},{10,... | collective-permute-start | bytes 1572872 | tf_op jit(solution)/shard_map/ppermute | solution.py:34
  28.3 8.6 %collective-permute-done.5.emb_ref = bf16[256,1024]{1,0:T(8,128)(2,1)S(1)} collective-permute-done((bf16[256,1024]{1,0:T(8,128)(2,1)S(1)}, bf16[256,1024]{1,0:T(8,128)(2,1)S(1)}, u32[]{:S(2)}, u32[]{:S(2)}) %collective-permute-start.5) | collective-permute-done | bytes 524320 | tf_op jit(solution)/shard_map/ppermute | solution.py:34
  37.1 0.3 collective-permute-start.6
  37.4 0.7 %collective-permute-done.8.emb_ref = bf16[256,1024]{1,0:T(8,128)(2,1)S(1)} collective-permute-done((bf16[256,1024]{1,0:T(8,128)(2,1)S(1)}, bf16[256,1024]{1,0:T(8,128)(2,1)S(1)}, u32[]{:S(2)}, u32[]{:S(2)}) %collective-permute-start.8) | collective-permute-done | bytes 524320 | tf_op jit(solution)/shard_map/ppermute | solution.py:34
  38.2 2.2 %collective-permute-done.7.refs_9_ = bf16[256,1024]{1,0:T(8,128)(2,1)S(1)} collective-permute-done((bf16[256,1024]{1,0:T(8,128)(2,1)S(1)}, bf16[256,1024]{1,0:T(8,128)(2,1)S(1)}, u32[]{:S(2)}, u32[]{:S(2)}) %collective-permute-start.7) | collective-permute-done | bytes 524320 | tf_op jit(solution)/shard_map/ppermute | solution.py:34
  40.4 4.8 %scan.1.own_ref = f32[5,8,256]{2,1,0:T(8,128)S(1)} custom-call(s32[24,128]{1,0:T(8,128)S(1)} %plan.1.par_ref, bf16[256,1024]{1,0:T(8,128)(2,1)S(1)} %normalize.6.refs_0_.refs_8_, bf16[512,1024]{1,0:T(8,128)(2,1)S(1)} %collective-permute-done.4.refs_1_.refs_5_, bf16[256,1024]{1,0:T(8,128)(2,1)S(1)} %normalize.7.refs_2_, ...), custom_call_target="tpu_custom_call" | custom-call | flops 4294967296 | bytes 6291456 | tf_op jit(solution)/shard_map/scan/pallas_call | solution.py:150
  45.3 0.8 %collective-permute-start.10 = (f32[5,8,256]{2,1,0:T(8,128)S(1)}, f32[5,8,256]{2,1,0:T(8,128)S(1)}, u32[]{:S(2)}, u32[]{:S(2)}) collective-permute-start(f32[5,8,256]{2,1,0:T(8,128)S(1)} %scan.1.own_ref), channel_id=1, source_target_pairs={{0,1},{1,0},{2,3},{3,2},{4,5},{5,4},{6,7},{7,6},{8,9},{9,8},{10,11... | collective-permute-start | bytes 122888 | tf_op jit(solution)/shard_map/ppermute | solution.py:34
  46.1 4.8 %collective-permute-done.10.over_ref = f32[5,8,256]{2,1,0:T(8,128)S(1)} collective-permute-done((f32[5,8,256]{2,1,0:T(8,128)S(1)}, f32[5,8,256]{2,1,0:T(8,128)S(1)}, u32[]{:S(2)}, u32[]{:S(2)}) %collective-permute-start.10) | collective-permute-done | bytes 40992 | tf_op jit(solution)/shard_map/ppermute | solution.py:34
  50.9 0.3 score.1
  51.2 1.1 %collective-permute-start.13 = (f32[64,128]{1,0:T(8,128)S(1)}, f32[64,128]{1,0:T(8,128)S(1)}, u32[]{:S(2)}, u32[]{:S(2)}) collective-permute-start(f32[64,128]{1,0:T(8,128)S(1)} %get-tuple-element.24), channel_id=1, source_target_pairs={{0,12},{1,13},{2,14},{3,15},{4,8},{5,9},{6,10},{7,11},{8,20},{9,21... | collective-permute-start | bytes 98312 | tf_op jit(solution)/shard_map/ppermute | solution.py:34
  52.3 6.1 %collective-permute-start.14 = (f32[16,128]{1,0:T(8,128)S(1)}, f32[16,128]{1,0:T(8,128)S(1)}, u32[]{:S(2)}, u32[]{:S(2)}) collective-permute-start(f32[16,128]{1,0:T(8,128)S(1)} %constant_dynamic-update-slice_fusion.own_ref), channel_id=1, source_target_pairs={{0,248},{1,249},{2,250},{3,251},{4,252},{5,253},{6,254},{7,255},{8... | collective-permute-start | bytes 24584 | tf_op jit(solution)/shard_map/ppermute | solution.py:34
  58.4 1.4 %collective-permute-start.15 = (f32[16,128]{1,0:T(8,128)S(1)}, f32[16,128]{1,0:T(8,128)S(1)}, u32[]{:S(2)}, u32[]{:S(2)}) collective-permute-start(f32[16,128]{1,0:T(8,128)S(1)} %constant_dynamic-update-slice_fusion.own_ref), channel_id=1, source_target_pairs={{0,240},{1,241},{2,242},{3,243},{4,244},{5,245},{6,246},{7,247},{8... | collective-permute-start | bytes 24584 | tf_op jit(solution)/shard_map/ppermute | solution.py:34
  59.9 3.1 %collective-permute-done.15.two_ref = f32[16,128]{1,0:T(8,128)S(1)} collective-permute-done((f32[16,128]{1,0:T(8,128)S(1)}, f32[16,128]{1,0:T(8,128)S(1)}, u32[]{:S(2)}, u32[]{:S(2)}) %collective-permute-start.15) | collective-permute-done | bytes 8224 | tf_op jit(solution)/shard_map/ppermute | solution.py:34
  63.0 0.7 %put.1 = f32[1,24]{1,0:T(1,128)} custom-call(s32[24,128]{1,0:T(8,128)S(1)} %plan.1.par_ref, f32[16,128]{1,0:T(8,128)S(1)} %constant_dynamic-update-slice_fusion.own_ref, f32[64,128]{1,0:T(8,128)S(1)} %collective-permute-done.12.same_ref, f32[64,128]{1,0:T(8,128)S(1)} %collective-permute-done.13.other_ref, f32[16,128]{1,0:T(8,128)S(1)} %collective-permute-done.14.one_ref, ...), custom_call_target="tpu_custom_call" | custom-call | tf_op jit(solution)/shard_map/put/pallas_call | solution.py:235
  (25 shorter events, 1.3 us)
Async XLA Ops:
  0.0 10.0 %copy-start.1 = (s32[128]{0:T(128)S(1)}, s32[128]{0:T(128)}, u32[]{:S(2)}) copy-start(s32[128]{0:T(128)} %len_ref.1) | copy-start | bytes 1540
  0.0 20.2 %collective-permute-start = (bf16[256,1024]{1,0:T(8,128)(2,1)}, bf16[256,1024]{1,0:T(8,128)(2,1)S(1)}, u32[]{:S(2)}, u32[]{:S(2)}) collective-permute-start(bf16[256,1024]{1,0:T(8,128)(2,1)} %bitcast.5), channel_id=1, source_target_pairs={{0,8},{1,9},{2,10},{3,11},{4,12},{5,13},{6,14},{7,15},{8,16},{9,17... | collective-permute-start | bytes 1572872 | tf_op jit(solution)/shard_map/ppermute | solution.py:34
  1.9 18.6 %collective-permute-start.1 = (bf16[256,1024]{1,0:T(8,128)(2,1)}, bf16[256,1024]{1,0:T(8,128)(2,1)S(1)}, u32[]{:S(2)}, u32[]{:S(2)}) collective-permute-start(bf16[256,1024]{1,0:T(8,128)(2,1)} %bitcast.6), channel_id=1, source_target_pairs={{0,248},{1,249},{2,250},{3,251},{4,252},{5,253},{6,254},{7,255},{8... | collective-permute-start | bytes 1572872 | tf_op jit(solution)/shard_map/ppermute | solution.py:34
  8.1 15.1 %collective-permute-start.2 = (bf16[256,1024]{1,0:T(8,128)(2,1)}, bf16[256,1024]{1,0:T(8,128)(2,1)S(1)}, u32[]{:S(2)}, u32[]{:S(2)}) collective-permute-start(bf16[256,1024]{1,0:T(8,128)(2,1)} %bitcast.7), channel_id=1, source_target_pairs={{0,1},{1,0},{2,3},{3,2},{4,5},{5,4},{6,7},{7,6},{8,9},{9,8},{10,11... | collective-permute-start | bytes 1572872 | tf_op jit(solution)/shard_map/ppermute | solution.py:34
  8.5 1.1 %copy-start = (bf16[1,256,1024]{2,1,0:T(8,128)(2,1)S(1)}, bf16[1,256,1024]{2,1,0:T(8,128)(2,1)}, u32[]{:S(2)}) copy-start(bf16[1,256,1024]{2,1,0:T(8,128)(2,1)} %param.2) | copy-start | bytes 1572868
  9.7 13.7 %collective-permute-start.3 = (bf16[256,1024]{1,0:T(8,128)(2,1)S(1)}, bf16[256,1024]{1,0:T(8,128)(2,1)S(1)}, u32[]{:S(2)}, u32[]{:S(2)}) collective-permute-start(bf16[256,1024]{1,0:T(8,128)(2,1)S(1)} %normalize.7.refs_2_), channel_id=1, source_target_pairs={{0,2},{1,3},{2,0},{3,1},{4,6},{5,7},{6,4},{7,5},{8,10},{9,11},{10,... | collective-permute-start | bytes 1572872 | tf_op jit(solution)/shard_map/ppermute | solution.py:34
  20.4 16.5 %collective-permute-start.5 = (bf16[256,1024]{1,0:T(8,128)(2,1)S(1)}, bf16[256,1024]{1,0:T(8,128)(2,1)S(1)}, u32[]{:S(2)}, u32[]{:S(2)}) collective-permute-start(bf16[256,1024]{1,0:T(8,128)(2,1)S(1)} %collective-permute-done.emb_ref), channel_id=1, source_target_pairs={{0,8},{1,9},{2,10},{3,11},{4,12},{5,13},{6,14},{7,15},{8,16},{9,17... | collective-permute-start | bytes 1572872 | tf_op jit(solution)/shard_map/ppermute | solution.py:34
  23.3 17.1 %collective-permute-start.4 = (bf16[512,1024]{1,0:T(8,128)(2,1)S(1)}, bf16[512,1024]{1,0:T(8,128)(2,1)S(1)}, u32[]{:S(2)}, u32[]{:S(2)}) collective-permute-start(bf16[512,1024]{1,0:T(8,128)(2,1)S(1)} %pad_maximum_fusion), channel_id=1, source_target_pairs={{0,2},{1,3},{2,0},{3,1},{4,6},{5,7},{6,4},{7,5},{8,10},{9,11},{10,... | collective-permute-start | bytes 3145736 | tf_op jit(solution)/shard_map/ppermute | solution.py:34
  23.4 14.6 %collective-permute-start.8 = (bf16[256,1024]{1,0:T(8,128)(2,1)S(1)}, bf16[256,1024]{1,0:T(8,128)(2,1)S(1)}, u32[]{:S(2)}, u32[]{:S(2)}) collective-permute-start(bf16[256,1024]{1,0:T(8,128)(2,1)S(1)} %collective-permute-done.2), channel_id=1, source_target_pairs={{0,248},{1,249},{2,250},{3,251},{4,252},{5,253},{6,254},{7,255},{8... | collective-permute-start | bytes 1572872 | tf_op jit(solution)/shard_map/ppermute | solution.py:34
  26.3 14.1 %collective-permute-start.7 = (bf16[256,1024]{1,0:T(8,128)(2,1)S(1)}, bf16[256,1024]{1,0:T(8,128)(2,1)S(1)}, u32[]{:S(2)}, u32[]{:S(2)}) collective-permute-start(bf16[256,1024]{1,0:T(8,128)(2,1)S(1)} %normalize.6.refs_0_.refs_8_), channel_id=1, source_target_pairs={{0,4},{1,5},{2,7},{3,6},{4,1},{5,0},{6,2},{7,3},{8,12},{9,13},{10,... | collective-permute-start | bytes 1572872 | tf_op jit(solution)/shard_map/ppermute | solution.py:34
  27.6 12.9 %collective-permute-start.9 = (bf16[256,1024]{1,0:T(8,128)(2,1)S(1)}, bf16[256,1024]{1,0:T(8,128)(2,1)S(1)}, u32[]{:S(2)}, u32[]{:S(2)}) collective-permute-start(bf16[256,1024]{1,0:T(8,128)(2,1)S(1)} %normalize.6.refs_0_.refs_8_), channel_id=1, source_target_pairs={{0,5},{1,4},{2,6},{3,7},{4,0},{5,1},{6,3},{7,2},{8,13},{9,12},{10,... | collective-permute-start | bytes 1572872 | tf_op jit(solution)/shard_map/ppermute | solution.py:34
  37.1 3.4 %collective-permute-start.6 = (bf16[256,1024]{1,0:T(8,128)(2,1)S(1)}, bf16[256,1024]{1,0:T(8,128)(2,1)S(1)}, u32[]{:S(2)}, u32[]{:S(2)}) collective-permute-start(bf16[256,1024]{1,0:T(8,128)(2,1)S(1)} %normalize.8.refs_6_), channel_id=1, source_target_pairs={{0,2},{1,3},{2,0},{3,1},{4,6},{5,7},{6,4},{7,5},{8,10},{9,11},{10,... | collective-permute-start | bytes 1572872 | tf_op jit(solution)/shard_map/ppermute | solution.py:34
  45.3 5.6 %collective-permute-start.10 = (f32[5,8,256]{2,1,0:T(8,128)S(1)}, f32[5,8,256]{2,1,0:T(8,128)S(1)}, u32[]{:S(2)}, u32[]{:S(2)}) collective-permute-start(f32[5,8,256]{2,1,0:T(8,128)S(1)} %scan.1.own_ref), channel_id=1, source_target_pairs={{0,1},{1,0},{2,3},{3,2},{4,5},{5,4},{6,7},{7,6},{8,9},{9,8},{10,11... | collective-permute-start | bytes 122888 | tf_op jit(solution)/shard_map/ppermute | solution.py:34
  51.2 1.2 %collective-permute-start.11 = (f32[8,128]{1,0:T(8,128)S(1)}, f32[8,128]{1,0:T(8,128)S(1)}, u32[]{:S(2)}, u32[]{:S(2)}) collective-permute-start(f32[8,128]{1,0:T(8,128)S(1)} %get-tuple-element.23), channel_id=1, source_target_pairs={{0,2},{1,3},{2,0},{3,1},{4,6},{5,7},{6,4},{7,5},{8,10},{9,11},{10,... | collective-permute-start | bytes 12296 | tf_op jit(solution)/shard_map/ppermute | solution.py:34
  51.2 11.8 %collective-permute-start.12 = (f32[64,128]{1,0:T(8,128)S(1)}, f32[64,128]{1,0:T(8,128)S(1)}, u32[]{:S(2)}, u32[]{:S(2)}) collective-permute-start(f32[64,128]{1,0:T(8,128)S(1)} %get-tuple-element.24), channel_id=1, source_target_pairs={{0,8},{1,9},{2,10},{3,11},{4,12},{5,13},{6,14},{7,15},{8,16},{9,17... | collective-permute-start | bytes 98312 | tf_op jit(solution)/shard_map/ppermute | solution.py:34
  51.2 11.8 %collective-permute-start.13 = (f32[64,128]{1,0:T(8,128)S(1)}, f32[64,128]{1,0:T(8,128)S(1)}, u32[]{:S(2)}, u32[]{:S(2)}) collective-permute-start(f32[64,128]{1,0:T(8,128)S(1)} %get-tuple-element.24), channel_id=1, source_target_pairs={{0,12},{1,13},{2,14},{3,15},{4,8},{5,9},{6,10},{7,11},{8,20},{9,21... | collective-permute-start | bytes 98312 | tf_op jit(solution)/shard_map/ppermute | solution.py:34
  52.3 7.6 %collective-permute-start.14 = (f32[16,128]{1,0:T(8,128)S(1)}, f32[16,128]{1,0:T(8,128)S(1)}, u32[]{:S(2)}, u32[]{:S(2)}) collective-permute-start(f32[16,128]{1,0:T(8,128)S(1)} %constant_dynamic-update-slice_fusion.own_ref), channel_id=1, source_target_pairs={{0,248},{1,249},{2,250},{3,251},{4,252},{5,253},{6,254},{7,255},{8... | collective-permute-start | bytes 24584 | tf_op jit(solution)/shard_map/ppermute | solution.py:34
  58.4 4.5 %collective-permute-start.15 = (f32[16,128]{1,0:T(8,128)S(1)}, f32[16,128]{1,0:T(8,128)S(1)}, u32[]{:S(2)}, u32[]{:S(2)}) collective-permute-start(f32[16,128]{1,0:T(8,128)S(1)} %constant_dynamic-update-slice_fusion.own_ref), channel_id=1, source_target_pairs={{0,240},{1,241},{2,242},{3,243},{4,244},{5,245},{6,246},{7,247},{8... | collective-permute-start | bytes 24584 | tf_op jit(solution)/shard_map/ppermute | solution.py:34

commit v6 on v5

--- a/solution.py
+++ b/solution.py
@@ -8,7 +8,7 @@
 from jax.sharding import PartitionSpec as P
 
 STEPS = 12
-WIDE = 64
+WIDE = 24
 AXES = ("cand", "tok")
 GROUP = 4
 LOW = -4.0
@@ -120,6 +120,7 @@
     best_ref[...] = jnp.full(best_ref.shape, LOW, jnp.float32)
     for k in (0, 1, 3, 2):
         a_mask = lane < par_ref[0:1, A_VALID + k : A_VALID + k + 1]
+        held = best_ref[...]
         for x in range(8):
             if x == 0 and k % 2 == 0:
                 out_ref[k, x : x + 1, :] = jnp.full((1, rows), LOW, jnp.float32)
@@ -133,9 +134,10 @@
                 preferred_element_type=jnp.float32,
             )
             best = jnp.max(jnp.where(a_mask, sims, LOW), axis=1, keepdims=True)
-            best_ref[...] = jnp.where(lane128 == 8 * k + x, best, best_ref[...])
+            held = jnp.where(lane128 == 8 * k + x, best, held)
             col = jnp.max(jnp.where(x_mask, sims, LOW), axis=0, keepdims=True)
             out_ref[k, x : x + 1, :] = col
+        best_ref[...] = held
     best = best_ref[...]
     best = jnp.maximum(best, pltpu.roll(best, 128 - 16, 1))
     total = jnp.where(sub < par_ref[16:17, :], best, 0.0)
@@ -258,11 +260,10 @@
     left_raw, par = lax.optimization_barrier((left_raw, par))
     far = normalize(send(left_raw, shift(dg=1)))
     left = normalize(left_raw)
+    over, right, own_c = lax.optimization_barrier((over, right, own_c))
     item1 = send(right, ring(1))
     item3 = send(right, ring(-1))
-    left2, right2, over = lax.optimization_barrier((left, right, over))
-    pair_c = send(jnp.concatenate([left2, right2]), shift(dc=1))
-    over, right, own_c = lax.optimization_barrier((over, right, own_c))
+    pair_c = send(jnp.concatenate([left, right]), shift(dc=1))
     item2 = normalize(send(over, shift(dg=-1)))
     far_c = send(far, shift(dc=1))
     left_c, right_c = pair_c, pair_c

time: 63.8 us -> 63.8 us (level)
  no operation moved by 1% of the time
where the time goes in v6:
time: 63.8 us; the launch traced here: 63.7 us
  waiting for transfers between devices  31.5 us (49%)
  starting transfers between devices  23.3 us (37%)
  Pallas kernels  7.49 us (12%)
  local copies, waits for them, and re-layouts  1.08 us (2%)
    ppermute x16, waiting for transfers between devices, send(): return lax.ppermute(value, AXES, pairs)  31.5 us
    ppermute x16, starting transfers between devices, send(): return lax.ppermute(value, AXES, pairs)  23.3 us
    pallas_call x1, Pallas kernels, scan(): pl.pallas_call(scan_kernel, in_specs=[IN_VMEM] * (1 + len(xs) + len(items...  4.85 us
  transfers between devices with their start and end apart: 16, of which 7 were waited for; matrix products, arithmetic and copies ran while one was open for 0% of the time, Pallas kernels for 3%

profile of v6, /device:TPU:16, one launch (start us, length us, event | category | flops | bytes accessed | tf_op | source)
XLA Modules:
  0.0 63.7 jit_solution(14755011847477405536)
XLA Ops:
  0.0 1.9 %collective-permute-start = (bf16[256,1024]{1,0:T(8,128)(2,1)}, bf16[256,1024]{1,0:T(8,128)(2,1)S(1)}, u32[]{:S(2)}, u32[]{:S(2)}) collective-permute-start(bf16[256,1024]{1,0:T(8,128)(2,1)} %bitcast.5), channel_id=1, source_target_pairs={{0,8},{1,9},{2,10},{3,11},{4,12},{5,13},{6,14},{7,15},{8,16},{9,17... | collective-permute-start | bytes 1572872 | tf_op jit(solution)/shard_map/ppermute | solution.py:34
  1.9 6.2 %collective-permute-start.2 = (bf16[256,1024]{1,0:T(8,128)(2,1)}, bf16[256,1024]{1,0:T(8,128)(2,1)S(1)}, u32[]{:S(2)}, u32[]{:S(2)}) collective-permute-start(bf16[256,1024]{1,0:T(8,128)(2,1)} %bitcast.6), channel_id=1, source_target_pairs={{0,248},{1,249},{2,250},{3,251},{4,252},{5,253},{6,254},{7,255},{8... | collective-permute-start | bytes 1572872 | tf_op jit(solution)/shard_map/ppermute | solution.py:34
  8.1 0.3 collective-permute-start.1
  8.5 1.1 %copy-done = bf16[1,256,1024]{2,1,0:T(8,128)(2,1)S(1)} copy-done((bf16[1,256,1024]{2,1,0:T(8,128)(2,1)S(1)}, bf16[1,256,1024]{2,1,0:T(8,128)(2,1)}, u32[]{:S(2)}) %copy-start) | copy-done | bytes 524312
  10.0 0.7 %plan.1.par_ref = s32[24,128]{1,0:T(8,128)S(1)} custom-call(s32[4]{0:T(128)S(1)} %pad_add_fusion.ids_ref, s32[128]{0:T(128)S(1)} %copy-done.1), custom_call_target="tpu_custom_call" | custom-call | tf_op jit(solution)/shard_map/plan/pallas_call | solution.py:104
  10.7 9.5 %collective-permute-done.emb_ref = bf16[256,1024]{1,0:T(8,128)(2,1)S(1)} collective-permute-done((bf16[256,1024]{1,0:T(8,128)(2,1)}, bf16[256,1024]{1,0:T(8,128)(2,1)S(1)}, u32[]{:S(2)}, u32[]{:S(2)}) %collective-permute-start) | collective-permute-done | bytes 524320 | tf_op jit(solution)/shard_map/ppermute | solution.py:34
  20.5 0.2 normalize.5.refs_0_.refs_8_
  20.7 2.6 %collective-permute-done.1 = bf16[256,1024]{1,0:T(8,128)(2,1)S(1)} collective-permute-done((bf16[256,1024]{1,0:T(8,128)(2,1)}, bf16[256,1024]{1,0:T(8,128)(2,1)S(1)}, u32[]{:S(2)}, u32[]{:S(2)}) %collective-permute-start.1) | collective-permute-done | bytes 524320 | tf_op jit(solution)/shard_map/ppermute | solution.py:34
  23.4 2.9 %collective-permute-start.8 = (bf16[256,1024]{1,0:T(8,128)(2,1)S(1)}, bf16[256,1024]{1,0:T(8,128)(2,1)S(1)}, u32[]{:S(2)}, u32[]{:S(2)}) collective-permute-start(bf16[256,1024]{1,0:T(8,128)(2,1)S(1)} %collective-permute-done.1), channel_id=1, source_target_pairs={{0,248},{1,249},{2,250},{3,251},{4,252},{5,253},{6,254},{7,255},{8... | collective-permute-start | bytes 1572872 | tf_op jit(solution)/shard_map/ppermute | solution.py:34
  26.3 1.3 %collective-permute-start.7 = (bf16[256,1024]{1,0:T(8,128)(2,1)S(1)}, bf16[256,1024]{1,0:T(8,128)(2,1)S(1)}, u32[]{:S(2)}, u32[]{:S(2)}) collective-permute-start(bf16[256,1024]{1,0:T(8,128)(2,1)S(1)} %normalize.5.refs_0_.refs_8_), channel_id=1, source_target_pairs={{0,4},{1,5},{2,7},{3,6},{4,1},{5,0},{6,2},{7,3},{8,12},{9,13},{10,... | collective-permute-start | bytes 1572872 | tf_op jit(solution)/shard_map/ppermute | solution.py:34
  27.6 0.7 %collective-permute-start.9 = (bf16[256,1024]{1,0:T(8,128)(2,1)S(1)}, bf16[256,1024]{1,0:T(8,128)(2,1)S(1)}, u32[]{:S(2)}, u32[]{:S(2)}) collective-permute-start(bf16[256,1024]{1,0:T(8,128)(2,1)S(1)} %normalize.5.refs_0_.refs_8_), channel_id=1, source_target_pairs={{0,5},{1,4},{2,6},{3,7},{4,0},{5,1},{6,3},{7,2},{8,13},{9,12},{10,... | collective-permute-start | bytes 1572872 | tf_op jit(solution)/shard_map/ppermute | solution.py:34
  28.3 8.6 %collective-permute-done.5.emb_ref = bf16[256,1024]{1,0:T(8,128)(2,1)S(1)} collective-permute-done((bf16[256,1024]{1,0:T(8,128)(2,1)S(1)}, bf16[256,1024]{1,0:T(8,128)(2,1)S(1)}, u32[]{:S(2)}, u32[]{:S(2)}) %collective-permute-start.5) | collective-permute-done | bytes 524320 | tf_op jit(solution)/shard_map/ppermute | solution.py:34
  37.1 0.3 collective-permute-start.6
  37.4 0.7 %collective-permute-done.8.emb_ref = bf16[256,1024]{1,0:T(8,128)(2,1)S(1)} collective-permute-done((bf16[256,1024]{1,0:T(8,128)(2,1)S(1)}, bf16[256,1024]{1,0:T(8,128)(2,1)S(1)}, u32[]{:S(2)}, u32[]{:S(2)}) %collective-permute-start.8) | collective-permute-done | bytes 524320 | tf_op jit(solution)/shard_map/ppermute | solution.py:34
  38.2 2.2 %collective-permute-done.7.refs_9_ = bf16[256,1024]{1,0:T(8,128)(2,1)S(1)} collective-permute-done((bf16[256,1024]{1,0:T(8,128)(2,1)S(1)}, bf16[256,1024]{1,0:T(8,128)(2,1)S(1)}, u32[]{:S(2)}, u32[]{:S(2)}) %collective-permute-start.7) | collective-permute-done | bytes 524320 | tf_op jit(solution)/shard_map/ppermute | solution.py:34
  40.4 4.8 %scan.1.own_ref = f32[5,8,256]{2,1,0:T(8,128)S(1)} custom-call(s32[24,128]{1,0:T(8,128)S(1)} %plan.1.par_ref, bf16[256,1024]{1,0:T(8,128)(2,1)S(1)} %normalize.5.refs_0_.refs_8_, bf16[512,1024]{1,0:T(8,128)(2,1)S(1)} %collective-permute-done.4.refs_1_.refs_5_, bf16[256,1024]{1,0:T(8,128)(2,1)S(1)} %normalize.6.refs_2_, ...), custom_call_target="tpu_custom_call" | custom-call | flops 4294967296 | bytes 6291456 | tf_op jit(solution)/shard_map/scan/pallas_call | solution.py:152
  45.3 0.8 %collective-permute-start.10 = (f32[5,8,256]{2,1,0:T(8,128)S(1)}, f32[5,8,256]{2,1,0:T(8,128)S(1)}, u32[]{:S(2)}, u32[]{:S(2)}) collective-permute-start(f32[5,8,256]{2,1,0:T(8,128)S(1)} %scan.1.own_ref), channel_id=1, source_target_pairs={{0,1},{1,0},{2,3},{3,2},{4,5},{5,4},{6,7},{7,6},{8,9},{9,8},{10,11... | collective-permute-start | bytes 122888 | tf_op jit(solution)/shard_map/ppermute | solution.py:34
  46.1 4.8 %collective-permute-done.10.over_ref = f32[5,8,256]{2,1,0:T(8,128)S(1)} collective-permute-done((f32[5,8,256]{2,1,0:T(8,128)S(1)}, f32[5,8,256]{2,1,0:T(8,128)S(1)}, u32[]{:S(2)}, u32[]{:S(2)}) %collective-permute-start.10) | collective-permute-done | bytes 40992 | tf_op jit(solution)/shard_map/ppermute | solution.py:34
  50.9 0.3 score.1
  51.3 1.1 %collective-permute-start.13 = (f32[24,128]{1,0:T(8,128)S(1)}, f32[24,128]{1,0:T(8,128)S(1)}, u32[]{:S(2)}, u32[]{:S(2)}) collective-permute-start(f32[24,128]{1,0:T(8,128)S(1)} %get-tuple-element.18), channel_id=1, source_target_pairs={{0,12},{1,13},{2,14},{3,15},{4,8},{5,9},{6,10},{7,11},{8,20},{9,21... | collective-permute-start | bytes 36872 | tf_op jit(solution)/shard_map/ppermute | solution.py:34
  52.3 6.1 %collective-permute-start.14 = (f32[16,128]{1,0:T(8,128)S(1)}, f32[16,128]{1,0:T(8,128)S(1)}, u32[]{:S(2)}, u32[]{:S(2)}) collective-permute-start(f32[16,128]{1,0:T(8,128)S(1)} %constant_dynamic-update-slice_fusion.own_ref), channel_id=1, source_target_pairs={{0,248},{1,249},{2,250},{3,251},{4,252},{5,253},{6,254},{7,255},{8... | collective-permute-start | bytes 24584 | tf_op jit(solution)/shard_map/ppermute | solution.py:34
  58.4 1.4 %collective-permute-start.15 = (f32[16,128]{1,0:T(8,128)S(1)}, f32[16,128]{1,0:T(8,128)S(1)}, u32[]{:S(2)}, u32[]{:S(2)}) collective-permute-start(f32[16,128]{1,0:T(8,128)S(1)} %constant_dynamic-update-slice_fusion.own_ref), channel_id=1, source_target_pairs={{0,240},{1,241},{2,242},{3,243},{4,244},{5,245},{6,246},{7,247},{8... | collective-permute-start | bytes 24584 | tf_op jit(solution)/shard_map/ppermute | solution.py:34
  59.9 3.1 %collective-permute-done.15.two_ref = f32[16,128]{1,0:T(8,128)S(1)} collective-permute-done((f32[16,128]{1,0:T(8,128)S(1)}, f32[16,128]{1,0:T(8,128)S(1)}, u32[]{:S(2)}, u32[]{:S(2)}) %collective-permute-start.15) | collective-permute-done | bytes 8224 | tf_op jit(solution)/shard_map/ppermute | solution.py:34
  63.0 0.7 %put.1 = f32[1,24]{1,0:T(1,128)} custom-call(s32[24,128]{1,0:T(8,128)S(1)} %plan.1.par_ref, f32[16,128]{1,0:T(8,128)S(1)} %constant_dynamic-update-slice_fusion.own_ref, f32[24,128]{1,0:T(8,128)S(1)} %collective-permute-done.12.same_ref, f32[24,128]{1,0:T(8,128)S(1)} %collective-permute-done.13.other_ref, f32[16,128]{1,0:T(8,128)S(1)} %collective-permute-done.14.one_ref, ...), custom_call_target="tpu_custom_call" | custom-call | tf_op jit(solution)/shard_map/put/pallas_call | solution.py:237
  (25 shorter events, 1.3 us)
Async XLA Ops:
  0.0 10.0 %copy-start.1 = (s32[128]{0:T(128)S(1)}, s32[128]{0:T(128)}, u32[]{:S(2)}) copy-start(s32[128]{0:T(128)} %len_ref.1) | copy-start | bytes 1540
  0.0 20.2 %collective-permute-start = (bf16[256,1024]{1,0:T(8,128)(2,1)}, bf16[256,1024]{1,0:T(8,128)(2,1)S(1)}, u32[]{:S(2)}, u32[]{:S(2)}) collective-permute-start(bf16[256,1024]{1,0:T(8,128)(2,1)} %bitcast.5), channel_id=1, source_target_pairs={{0,8},{1,9},{2,10},{3,11},{4,12},{5,13},{6,14},{7,15},{8,16},{9,17... | collective-permute-start | bytes 1572872 | tf_op jit(solution)/shard_map/ppermute | solution.py:34
  1.9 18.6 %collective-permute-start.2 = (bf16[256,1024]{1,0:T(8,128)(2,1)}, bf16[256,1024]{1,0:T(8,128)(2,1)S(1)}, u32[]{:S(2)}, u32[]{:S(2)}) collective-permute-start(bf16[256,1024]{1,0:T(8,128)(2,1)} %bitcast.6), channel_id=1, source_target_pairs={{0,248},{1,249},{2,250},{3,251},{4,252},{5,253},{6,254},{7,255},{8... | collective-permute-start | bytes 1572872 | tf_op jit(solution)/shard_map/ppermute | solution.py:34
  8.1 15.1 %collective-permute-start.1 = (bf16[256,1024]{1,0:T(8,128)(2,1)}, bf16[256,1024]{1,0:T(8,128)(2,1)S(1)}, u32[]{:S(2)}, u32[]{:S(2)}) collective-permute-start(bf16[256,1024]{1,0:T(8,128)(2,1)} %bitcast.7), channel_id=1, source_target_pairs={{0,1},{1,0},{2,3},{3,2},{4,5},{5,4},{6,7},{7,6},{8,9},{9,8},{10,11... | collective-permute-start | bytes 1572872 | tf_op jit(solution)/shard_map/ppermute | solution.py:34
  8.5 1.1 %copy-start = (bf16[1,256,1024]{2,1,0:T(8,128)(2,1)S(1)}, bf16[1,256,1024]{2,1,0:T(8,128)(2,1)}, u32[]{:S(2)}) copy-start(bf16[1,256,1024]{2,1,0:T(8,128)(2,1)} %param.2) | copy-start | bytes 1572868
  9.7 13.5 %collective-permute-start.3 = (bf16[256,1024]{1,0:T(8,128)(2,1)S(1)}, bf16[256,1024]{1,0:T(8,128)(2,1)S(1)}, u32[]{:S(2)}, u32[]{:S(2)}) collective-permute-start(bf16[256,1024]{1,0:T(8,128)(2,1)S(1)} %normalize.6.refs_2_), channel_id=1, source_target_pairs={{0,2},{1,3},{2,0},{3,1},{4,6},{5,7},{6,4},{7,5},{8,10},{9,11},{10,... | collective-permute-start | bytes 1572872 | tf_op jit(solution)/shard_map/ppermute | solution.py:34
  20.4 16.5 %collective-permute-start.5 = (bf16[256,1024]{1,0:T(8,128)(2,1)S(1)}, bf16[256,1024]{1,0:T(8,128)(2,1)S(1)}, u32[]{:S(2)}, u32[]{:S(2)}) collective-permute-start(bf16[256,1024]{1,0:T(8,128)(2,1)S(1)} %collective-permute-done.emb_ref), channel_id=1, source_target_pairs={{0,8},{1,9},{2,10},{3,11},{4,12},{5,13},{6,14},{7,15},{8,16},{9,17... | collective-permute-start | bytes 1572872 | tf_op jit(solution)/shard_map/ppermute | solution.py:34
  23.3 17.1 %collective-permute-start.4 = (bf16[512,1024]{1,0:T(8,128)(2,1)S(1)}, bf16[512,1024]{1,0:T(8,128)(2,1)S(1)}, u32[]{:S(2)}, u32[]{:S(2)}) collective-permute-start(bf16[512,1024]{1,0:T(8,128)(2,1)S(1)} %pad_maximum_fusion), channel_id=1, source_target_pairs={{0,2},{1,3},{2,0},{3,1},{4,6},{5,7},{6,4},{7,5},{8,10},{9,11},{10,... | collective-permute-start | bytes 3145736 | tf_op jit(solution)/shard_map/ppermute | solution.py:34
  23.4 14.7 %collective-permute-start.8 = (bf16[256,1024]{1,0:T(8,128)(2,1)S(1)}, bf16[256,1024]{1,0:T(8,128)(2,1)S(1)}, u32[]{:S(2)}, u32[]{:S(2)}) collective-permute-start(bf16[256,1024]{1,0:T(8,128)(2,1)S(1)} %collective-permute-done.1), channel_id=1, source_target_pairs={{0,248},{1,249},{2,250},{3,251},{4,252},{5,253},{6,254},{7,255},{8... | collective-permute-start | bytes 1572872 | tf_op jit(solution)/shard_map/ppermute | solution.py:34
  26.3 14.2 %collective-permute-start.7 = (bf16[256,1024]{1,0:T(8,128)(2,1)S(1)}, bf16[256,1024]{1,0:T(8,128)(2,1)S(1)}, u32[]{:S(2)}, u32[]{:S(2)}) collective-permute-start(bf16[256,1024]{1,0:T(8,128)(2,1)S(1)} %normalize.5.refs_0_.refs_8_), channel_id=1, source_target_pairs={{0,4},{1,5},{2,7},{3,6},{4,1},{5,0},{6,2},{7,3},{8,12},{9,13},{10,... | collective-permute-start | bytes 1572872 | tf_op jit(solution)/shard_map/ppermute | solution.py:34
  27.6 12.9 %collective-permute-start.9 = (bf16[256,1024]{1,0:T(8,128)(2,1)S(1)}, bf16[256,1024]{1,0:T(8,128)(2,1)S(1)}, u32[]{:S(2)}, u32[]{:S(2)}) collective-permute-start(bf16[256,1024]{1,0:T(8,128)(2,1)S(1)} %normalize.5.refs_0_.refs_8_), channel_id=1, source_target_pairs={{0,5},{1,4},{2,6},{3,7},{4,0},{5,1},{6,3},{7,2},{8,13},{9,12},{10,... | collective-permute-start | bytes 1572872 | tf_op jit(solution)/shard_map/ppermute | solution.py:34
  37.1 3.4 %collective-permute-start.6 = (bf16[256,1024]{1,0:T(8,128)(2,1)S(1)}, bf16[256,1024]{1,0:T(8,128)(2,1)S(1)}, u32[]{:S(2)}, u32[]{:S(2)}) collective-permute-start(bf16[256,1024]{1,0:T(8,128)(2,1)S(1)} %normalize.8.refs_6_), channel_id=1, source_target_pairs={{0,2},{1,3},{2,0},{3,1},{4,6},{5,7},{6,4},{7,5},{8,10},{9,11},{10,... | collective-permute-start | bytes 1572872 | tf_op jit(solution)/shard_map/ppermute | solution.py:34
  45.3 5.6 %collective-permute-start.10 = (f32[5,8,256]{2,1,0:T(8,128)S(1)}, f32[5,8,256]{2,1,0:T(8,128)S(1)}, u32[]{:S(2)}, u32[]{:S(2)}) collective-permute-start(f32[5,8,256]{2,1,0:T(8,128)S(1)} %scan.1.own_ref), channel_id=1, source_target_pairs={{0,1},{1,0},{2,3},{3,2},{4,5},{5,4},{6,7},{7,6},{8,9},{9,8},{10,11... | collective-permute-start | bytes 122888 | tf_op jit(solution)/shard_map/ppermute | solution.py:34
  51.2 1.2 %collective-permute-start.11 = (f32[8,128]{1,0:T(8,128)S(1)}, f32[8,128]{1,0:T(8,128)S(1)}, u32[]{:S(2)}, u32[]{:S(2)}) collective-permute-start(f32[8,128]{1,0:T(8,128)S(1)} %get-tuple-element.17), channel_id=1, source_target_pairs={{0,2},{1,3},{2,0},{3,1},{4,6},{5,7},{6,4},{7,5},{8,10},{9,11},{10,... | collective-permute-start | bytes 12296 | tf_op jit(solution)/shard_map/ppermute | solution.py:34
  51.2 11.8 %collective-permute-start.12 = (f32[24,128]{1,0:T(8,128)S(1)}, f32[24,128]{1,0:T(8,128)S(1)}, u32[]{:S(2)}, u32[]{:S(2)}) collective-permute-start(f32[24,128]{1,0:T(8,128)S(1)} %get-tuple-element.18), channel_id=1, source_target_pairs={{0,8},{1,9},{2,10},{3,11},{4,12},{5,13},{6,14},{7,15},{8,16},{9,17... | collective-permute-start | bytes 36872 | tf_op jit(solution)/shard_map/ppermute | solution.py:34
  51.3 11.7 %collective-permute-start.13 = (f32[24,128]{1,0:T(8,128)S(1)}, f32[24,128]{1,0:T(8,128)S(1)}, u32[]{:S(2)}, u32[]{:S(2)}) collective-permute-start(f32[24,128]{1,0:T(8,128)S(1)} %get-tuple-element.18), channel_id=1, source_target_pairs={{0,12},{1,13},{2,14},{3,15},{4,8},{5,9},{6,10},{7,11},{8,20},{9,21... | collective-permute-start | bytes 36872 | tf_op jit(solution)/shard_map/ppermute | solution.py:34
  52.3 7.5 %collective-permute-start.14 = (f32[16,128]{1,0:T(8,128)S(1)}, f32[16,128]{1,0:T(8,128)S(1)}, u32[]{:S(2)}, u32[]{:S(2)}) collective-permute-start(f32[16,128]{1,0:T(8,128)S(1)} %constant_dynamic-update-slice_fusion.own_ref), channel_id=1, source_target_pairs={{0,248},{1,249},{2,250},{3,251},{4,252},{5,253},{6,254},{7,255},{8... | collective-permute-start | bytes 24584 | tf_op jit(solution)/shard_map/ppermute | solution.py:34
  58.4 4.5 %collective-permute-start.15 = (f32[16,128]{1,0:T(8,128)S(1)}, f32[16,128]{1,0:T(8,128)S(1)}, u32[]{:S(2)}, u32[]{:S(2)}) collective-permute-start(f32[16,128]{1,0:T(8,128)S(1)} %constant_dynamic-update-slice_fusion.own_ref), channel_id=1, source_target_pairs={{0,240},{1,241},{2,242},{3,243},{4,244},{5,245},{6,246},{7,247},{8... | collective-permute-start | bytes 24584 | tf_op jit(solution)/shard_map/ppermute | solution.py:34

commit v7 on v6

--- a/solution.py
+++ b/solution.py
@@ -259,7 +259,8 @@
     own_c = send(own, shift(dc=1))
     left_raw, par = lax.optimization_barrier((left_raw, par))
     far = normalize(send(left_raw, shift(dg=1)))
-    left = normalize(left_raw)
+    left_late, right = lax.optimization_barrier((left_raw, right))
+    left = normalize(left_late)
     over, right, own_c = lax.optimization_barrier((over, right, own_c))
     item1 = send(right, ring(1))
     item3 = send(right, ring(-1))

time: 63.8 us -> 65.5 us (1.027)
  waiting for transfers between devices: 31.5 us -> 34 us
  local copies, waits for them, and re-layouts: 1.08 us -> 0.01 us
  Pallas kernels: 7.49 us -> 8.55 us
  starting transfers between devices: 23.3 us -> 22.6 us
    ppermute x16, waiting for transfers between devices: 31.5 us -> 34 us  [send(): return lax.ppermute(value, AXES, pairs)]
    unnamed x5 -> x3, local copies, waits for them, and re-layouts: 1.08 us -> 0.01 us
    pallas_call x5, Pallas kernels: 0.95 us -> 2.02 us  [normalize(): pl.pallas_call(normalize_kernel, in_specs=[IN_VMEM], out_specs=IN_VMEM, o...]
    ppermute x16, starting transfers between devices: 23.3 us -> 22.6 us  [send(): return lax.ppermute(value, AXES, pairs)]
  transfers between devices with their start and end apart: 16 -> 16, of which waited for: 7 -> 7; matrix products, arithmetic and copies ran while one was open for 0% -> 0% of each run, Pallas kernels for 3% -> 4%
where the time goes in v7:
time: 65.5 us; the launch traced here: 65.4 us
  waiting for transfers between devices  34 us (52%)
  starting transfers between devices  22.6 us (35%)
  Pallas kernels  8.55 us (13%)
    ppermute x16, waiting for transfers between devices, send(): return lax.ppermute(value, AXES, pairs)  34 us
    ppermute x16, starting transfers between devices, send(): return lax.ppermute(value, AXES, pairs)  22.6 us
    pallas_call x1, Pallas kernels, scan(): pl.pallas_call(scan_kernel, in_specs=[IN_VMEM] * (1 + len(xs) + len(items...  4.83 us
    pallas_call x5, Pallas kernels, normalize(): pl.pallas_call(normalize_kernel, in_specs=[IN_VMEM], out_specs=IN_VMEM, o...  2.02 us
  transfers between devices with their start and end apart: 16, of which 7 were waited for; matrix products, arithmetic and copies ran while one was open for 0% of the time, Pallas kernels for 4%

profile of v7, /device:TPU:16, one launch (start us, length us, event | category | flops | bytes accessed | tf_op | source)
XLA Modules:
  0.0 65.4 jit_solution(9150035659018465240)
XLA Ops:
  0.0 1.9 %collective-permute-start = (bf16[256,1024]{1,0:T(8,128)(2,1)}, bf16[256,1024]{1,0:T(8,128)(2,1)S(1)}, u32[]{:S(2)}, u32[]{:S(2)}) collective-permute-start(bf16[256,1024]{1,0:T(8,128)(2,1)} %bitcast.emb_ref), channel_id=1, source_target_pairs={{0,8},{1,9},{2,10},{3,11},{4,12},{5,13},{6,14},{7,15},{8,16},{9,17... | collective-permute-start | bytes 1572872 | tf_op jit(solution)/shard_map/ppermute | solution.py:34
  1.9 6.2 %collective-permute-start.2 = (bf16[256,1024]{1,0:T(8,128)(2,1)}, bf16[256,1024]{1,0:T(8,128)(2,1)S(1)}, u32[]{:S(2)}, u32[]{:S(2)}) collective-permute-start(bf16[256,1024]{1,0:T(8,128)(2,1)} %bitcast.emb_ref), channel_id=1, source_target_pairs={{0,248},{1,249},{2,250},{3,251},{4,252},{5,253},{6,254},{7,255},{8... | collective-permute-start | bytes 1572872 | tf_op jit(solution)/shard_map/ppermute | solution.py:34
  8.1 1.3 %normalize.6.refs_2_ = bf16[256,1024]{1,0:T(8,128)(2,1)S(1)} custom-call(bf16[256,1024]{1,0:T(8,128)(2,1)} %bitcast.emb_ref), custom_call_target="tpu_custom_call" | custom-call | tf_op jit(solution)/shard_map/normalize/pallas_call | solution.py:62
  9.5 0.4 collective-permute-start.1
  10.0 0.7 %plan.1.par_ref = s32[24,128]{1,0:T(8,128)S(1)} custom-call(s32[4]{0:T(128)S(1)} %pad_add_fusion.ids_ref, s32[128]{0:T(128)S(1)} %copy-done), custom_call_target="tpu_custom_call" | custom-call | tf_op jit(solution)/shard_map/plan/pallas_call | solution.py:104
  10.7 9.5 %collective-permute-done.emb_ref = bf16[256,1024]{1,0:T(8,128)(2,1)S(1)} collective-permute-done((bf16[256,1024]{1,0:T(8,128)(2,1)}, bf16[256,1024]{1,0:T(8,128)(2,1)S(1)}, u32[]{:S(2)}, u32[]{:S(2)}) %collective-permute-start) | collective-permute-done | bytes 524320 | tf_op jit(solution)/shard_map/ppermute | solution.py:34
  20.4 5.2 %collective-permute-done.1 = bf16[256,1024]{1,0:T(8,128)(2,1)S(1)} collective-permute-done((bf16[256,1024]{1,0:T(8,128)(2,1)}, bf16[256,1024]{1,0:T(8,128)(2,1)S(1)}, u32[]{:S(2)}, u32[]{:S(2)}) %collective-permute-start.1) | collective-permute-done | bytes 524320 | tf_op jit(solution)/shard_map/ppermute | solution.py:34
  25.6 0.2 normalize.7.refs_4_
  25.9 2.0 %collective-permute-start.8 = (bf16[256,1024]{1,0:T(8,128)(2,1)S(1)}, bf16[256,1024]{1,0:T(8,128)(2,1)S(1)}, u32[]{:S(2)}, u32[]{:S(2)}) collective-permute-start(bf16[256,1024]{1,0:T(8,128)(2,1)S(1)} %collective-permute-done.1), channel_id=1, source_target_pairs={{0,248},{1,249},{2,250},{3,251},{4,252},{5,253},{6,254},{7,255},{8... | collective-permute-start | bytes 1572872 | tf_op jit(solution)/shard_map/ppermute | solution.py:34
  28.0 1.3 %collective-permute-start.7 = (bf16[256,1024]{1,0:T(8,128)(2,1)S(1)}, bf16[256,1024]{1,0:T(8,128)(2,1)S(1)}, u32[]{:S(2)}, u32[]{:S(2)}) collective-permute-start(bf16[256,1024]{1,0:T(8,128)(2,1)S(1)} %normalize.5.refs_0_.refs_8_), channel_id=1, source_target_pairs={{0,4},{1,5},{2,7},{3,6},{4,1},{5,0},{6,2},{7,3},{8,12},{9,13},{10,... | collective-permute-start | bytes 1572872 | tf_op jit(solution)/shard_map/ppermute | solution.py:34
  29.2 0.7 %collective-permute-start.9 = (bf16[256,1024]{1,0:T(8,128)(2,1)S(1)}, bf16[256,1024]{1,0:T(8,128)(2,1)S(1)}, u32[]{:S(2)}, u32[]{:S(2)}) collective-permute-start(bf16[256,1024]{1,0:T(8,128)(2,1)S(1)} %normalize.5.refs_0_.refs_8_), channel_id=1, source_target_pairs={{0,5},{1,4},{2,6},{3,7},{4,0},{5,1},{6,3},{7,2},{8,13},{9,12},{10,... | collective-permute-start | bytes 1572872 | tf_op jit(solution)/shard_map/ppermute | solution.py:34
  30.0 6.6 %collective-permute-done.5.emb_ref = bf16[256,1024]{1,0:T(8,128)(2,1)S(1)} collective-permute-done((bf16[256,1024]{1,0:T(8,128)(2,1)S(1)}, bf16[256,1024]{1,0:T(8,128)(2,1)S(1)}, u32[]{:S(2)}, u32[]{:S(2)}) %collective-permute-start.5) | collective-permute-done | bytes 524320 | tf_op jit(solution)/shard_map/ppermute | solution.py:34
  36.8 0.3 collective-permute-start.6
  37.1 3.2 %collective-permute-done.8.emb_ref = bf16[256,1024]{1,0:T(8,128)(2,1)S(1)} collective-permute-done((bf16[256,1024]{1,0:T(8,128)(2,1)S(1)}, bf16[256,1024]{1,0:T(8,128)(2,1)S(1)}, u32[]{:S(2)}, u32[]{:S(2)}) %collective-permute-start.8) | collective-permute-done | bytes 524320 | tf_op jit(solution)/shard_map/ppermute | solution.py:34
  40.5 1.6 %collective-permute-done.7.refs_9_ = bf16[256,1024]{1,0:T(8,128)(2,1)S(1)} collective-permute-done((bf16[256,1024]{1,0:T(8,128)(2,1)S(1)}, bf16[256,1024]{1,0:T(8,128)(2,1)S(1)}, u32[]{:S(2)}, u32[]{:S(2)}) %collective-permute-start.7) | collective-permute-done | bytes 524320 | tf_op jit(solution)/shard_map/ppermute | solution.py:34
  42.1 4.8 %scan.1.own_ref = f32[5,8,256]{2,1,0:T(8,128)S(1)} custom-call(s32[24,128]{1,0:T(8,128)S(1)} %plan.1.par_ref, bf16[256,1024]{1,0:T(8,128)(2,1)S(1)} %normalize.5.refs_0_.refs_8_, bf16[512,1024]{1,0:T(8,128)(2,1)S(1)} %collective-permute-done.4.refs_1_.refs_5_, bf16[256,1024]{1,0:T(8,128)(2,1)S(1)} %normalize.6.refs_2_, ...), custom_call_target="tpu_custom_call" | custom-call | flops 4294967296 | bytes 6291456 | tf_op jit(solution)/shard_map/scan/pallas_call | solution.py:152
  47.0 0.8 %collective-permute-start.10 = (f32[5,8,256]{2,1,0:T(8,128)S(1)}, f32[5,8,256]{2,1,0:T(8,128)S(1)}, u32[]{:S(2)}, u32[]{:S(2)}) collective-permute-start(f32[5,8,256]{2,1,0:T(8,128)S(1)} %scan.1.own_ref), channel_id=1, source_target_pairs={{0,1},{1,0},{2,3},{3,2},{4,5},{5,4},{6,7},{7,6},{8,9},{9,8},{10,11... | collective-permute-start | bytes 122888 | tf_op jit(solution)/shard_map/ppermute | solution.py:34
  47.8 4.8 %collective-permute-done.10.over_ref = f32[5,8,256]{2,1,0:T(8,128)S(1)} collective-permute-done((f32[5,8,256]{2,1,0:T(8,128)S(1)}, f32[5,8,256]{2,1,0:T(8,128)S(1)}, u32[]{:S(2)}, u32[]{:S(2)}) %collective-permute-start.10) | collective-permute-done | bytes 40992 | tf_op jit(solution)/shard_map/ppermute | solution.py:34
  52.5 0.3 score.1
  53.0 1.9 %collective-permute-start.13 = (f32[24,128]{1,0:T(8,128)S(1)}, f32[24,128]{1,0:T(8,128)S(1)}, u32[]{:S(2)}, u32[]{:S(2)}) collective-permute-start(f32[24,128]{1,0:T(8,128)S(1)} %get-tuple-element.22), channel_id=1, source_target_pairs={{0,12},{1,13},{2,14},{3,15},{4,8},{5,9},{6,10},{7,11},{8,20},{9,21... | collective-permute-start | bytes 36872 | tf_op jit(solution)/shard_map/ppermute | solution.py:34
  54.9 5.3 %collective-permute-start.14 = (f32[16,128]{1,0:T(8,128)S(1)}, f32[16,128]{1,0:T(8,128)S(1)}, u32[]{:S(2)}, u32[]{:S(2)}) collective-permute-start(f32[16,128]{1,0:T(8,128)S(1)} %constant_dynamic-update-slice_fusion.own_ref), channel_id=1, source_target_pairs={{0,248},{1,249},{2,250},{3,251},{4,252},{5,253},{6,254},{7,255},{8... | collective-permute-start | bytes 24584 | tf_op jit(solution)/shard_map/ppermute | solution.py:34
  60.1 1.4 %collective-permute-start.15 = (f32[16,128]{1,0:T(8,128)S(1)}, f32[16,128]{1,0:T(8,128)S(1)}, u32[]{:S(2)}, u32[]{:S(2)}) collective-permute-start(f32[16,128]{1,0:T(8,128)S(1)} %constant_dynamic-update-slice_fusion.own_ref), channel_id=1, source_target_pairs={{0,240},{1,241},{2,242},{3,243},{4,244},{5,245},{6,246},{7,247},{8... | collective-permute-start | bytes 24584 | tf_op jit(solution)/shard_map/ppermute | solution.py:34
  61.6 3.1 %collective-permute-done.15.two_ref = f32[16,128]{1,0:T(8,128)S(1)} collective-permute-done((f32[16,128]{1,0:T(8,128)S(1)}, f32[16,128]{1,0:T(8,128)S(1)}, u32[]{:S(2)}, u32[]{:S(2)}) %collective-permute-start.15) | collective-permute-done | bytes 8224 | tf_op jit(solution)/shard_map/ppermute | solution.py:34
  64.7 0.7 %put.1 = f32[1,24]{1,0:T(1,128)} custom-call(s32[24,128]{1,0:T(8,128)S(1)} %plan.1.par_ref, f32[16,128]{1,0:T(8,128)S(1)} %constant_dynamic-update-slice_fusion.own_ref, f32[24,128]{1,0:T(8,128)S(1)} %collective-permute-done.12.same_ref, f32[24,128]{1,0:T(8,128)S(1)} %collective-permute-done.13.other_ref, f32[16,128]{1,0:T(8,128)S(1)} %collective-permute-done.14.one_ref, ...), custom_call_target="tpu_custom_call" | custom-call | tf_op jit(solution)/shard_map/put/pallas_call | solution.py:237
  (23 shorter events, 1.1 us)
Async XLA Ops:
  0.0 10.0 %copy-start = (s32[128]{0:T(128)S(1)}, s32[128]{0:T(128)}, u32[]{:S(2)}) copy-start(s32[128]{0:T(128)} %len_ref.1) | copy-start | bytes 1540
  0.0 20.2 %collective-permute-start = (bf16[256,1024]{1,0:T(8,128)(2,1)}, bf16[256,1024]{1,0:T(8,128)(2,1)S(1)}, u32[]{:S(2)}, u32[]{:S(2)}) collective-permute-start(bf16[256,1024]{1,0:T(8,128)(2,1)} %bitcast.emb_ref), channel_id=1, source_target_pairs={{0,8},{1,9},{2,10},{3,11},{4,12},{5,13},{6,14},{7,15},{8,16},{9,17... | collective-permute-start | bytes 1572872 | tf_op jit(solution)/shard_map/ppermute | solution.py:34
  1.9 18.3 %collective-permute-start.2 = (bf16[256,1024]{1,0:T(8,128)(2,1)}, bf16[256,1024]{1,0:T(8,128)(2,1)S(1)}, u32[]{:S(2)}, u32[]{:S(2)}) collective-permute-start(bf16[256,1024]{1,0:T(8,128)(2,1)} %bitcast.emb_ref), channel_id=1, source_target_pairs={{0,248},{1,249},{2,250},{3,251},{4,252},{5,253},{6,254},{7,255},{8... | collective-permute-start | bytes 1572872 | tf_op jit(solution)/shard_map/ppermute | solution.py:34
  9.4 11.0 %collective-permute-start.3 = (bf16[256,1024]{1,0:T(8,128)(2,1)S(1)}, bf16[256,1024]{1,0:T(8,128)(2,1)S(1)}, u32[]{:S(2)}, u32[]{:S(2)}) collective-permute-start(bf16[256,1024]{1,0:T(8,128)(2,1)S(1)} %normalize.6.refs_2_), channel_id=1, source_target_pairs={{0,2},{1,3},{2,0},{3,1},{4,6},{5,7},{6,4},{7,5},{8,10},{9,11},{10,... | collective-permute-start | bytes 1572872 | tf_op jit(solution)/shard_map/ppermute | solution.py:34
  9.5 16.1 %collective-permute-start.1 = (bf16[256,1024]{1,0:T(8,128)(2,1)}, bf16[256,1024]{1,0:T(8,128)(2,1)S(1)}, u32[]{:S(2)}, u32[]{:S(2)}) collective-permute-start(bf16[256,1024]{1,0:T(8,128)(2,1)} %bitcast.emb_ref), channel_id=1, source_target_pairs={{0,1},{1,0},{2,3},{3,2},{4,5},{5,4},{6,7},{7,6},{8,9},{9,8},{10,11... | collective-permute-start | bytes 1572872 | tf_op jit(solution)/shard_map/ppermute | solution.py:34
  20.2 16.4 %collective-permute-start.5 = (bf16[256,1024]{1,0:T(8,128)(2,1)S(1)}, bf16[256,1024]{1,0:T(8,128)(2,1)S(1)}, u32[]{:S(2)}, u32[]{:S(2)}) collective-permute-start(bf16[256,1024]{1,0:T(8,128)(2,1)S(1)} %collective-permute-done.emb_ref), channel_id=1, source_target_pairs={{0,8},{1,9},{2,10},{3,11},{4,12},{5,13},{6,14},{7,15},{8,16},{9,17... | collective-permute-start | bytes 1572872 | tf_op jit(solution)/shard_map/ppermute | solution.py:34
  25.8 16.3 %collective-permute-start.4 = (bf16[512,1024]{1,0:T(8,128)(2,1)S(1)}, bf16[512,1024]{1,0:T(8,128)(2,1)S(1)}, u32[]{:S(2)}, u32[]{:S(2)}) collective-permute-start(bf16[512,1024]{1,0:T(8,128)(2,1)S(1)} %pad_maximum_fusion), channel_id=1, source_target_pairs={{0,2},{1,3},{2,0},{3,1},{4,6},{5,7},{6,4},{7,5},{8,10},{9,11},{10,... | collective-permute-start | bytes 3145736 | tf_op jit(solution)/shard_map/ppermute | solution.py:34
  25.9 14.3 %collective-permute-start.8 = (bf16[256,1024]{1,0:T(8,128)(2,1)S(1)}, bf16[256,1024]{1,0:T(8,128)(2,1)S(1)}, u32[]{:S(2)}, u32[]{:S(2)}) collective-permute-start(bf16[256,1024]{1,0:T(8,128)(2,1)S(1)} %collective-permute-done.1), channel_id=1, source_target_pairs={{0,248},{1,249},{2,250},{3,251},{4,252},{5,253},{6,254},{7,255},{8... | collective-permute-start | bytes 1572872 | tf_op jit(solution)/shard_map/ppermute | solution.py:34
  28.0 14.2 %collective-permute-start.7 = (bf16[256,1024]{1,0:T(8,128)(2,1)S(1)}, bf16[256,1024]{1,0:T(8,128)(2,1)S(1)}, u32[]{:S(2)}, u32[]{:S(2)}) collective-permute-start(bf16[256,1024]{1,0:T(8,128)(2,1)S(1)} %normalize.5.refs_0_.refs_8_), channel_id=1, source_target_pairs={{0,4},{1,5},{2,7},{3,6},{4,1},{5,0},{6,2},{7,3},{8,12},{9,13},{10,... | collective-permute-start | bytes 1572872 | tf_op jit(solution)/shard_map/ppermute | solution.py:34
  29.2 12.9 %collective-permute-start.9 = (bf16[256,1024]{1,0:T(8,128)(2,1)S(1)}, bf16[256,1024]{1,0:T(8,128)(2,1)S(1)}, u32[]{:S(2)}, u32[]{:S(2)}) collective-permute-start(bf16[256,1024]{1,0:T(8,128)(2,1)S(1)} %normalize.5.refs_0_.refs_8_), channel_id=1, source_target_pairs={{0,5},{1,4},{2,6},{3,7},{4,0},{5,1},{6,3},{7,2},{8,13},{9,12},{10,... | collective-permute-start | bytes 1572872 | tf_op jit(solution)/shard_map/ppermute | solution.py:34
  36.8 5.3 %collective-permute-start.6 = (bf16[256,1024]{1,0:T(8,128)(2,1)S(1)}, bf16[256,1024]{1,0:T(8,128)(2,1)S(1)}, u32[]{:S(2)}, u32[]{:S(2)}) collective-permute-start(bf16[256,1024]{1,0:T(8,128)(2,1)S(1)} %normalize.8.refs_6_), channel_id=1, source_target_pairs={{0,2},{1,3},{2,0},{3,1},{4,6},{5,7},{6,4},{7,5},{8,10},{9,11},{10,... | collective-permute-start | bytes 1572872 | tf_op jit(solution)/shard_map/ppermute | solution.py:34
  47.0 5.6 %collective-permute-start.10 = (f32[5,8,256]{2,1,0:T(8,128)S(1)}, f32[5,8,256]{2,1,0:T(8,128)S(1)}, u32[]{:S(2)}, u32[]{:S(2)}) collective-permute-start(f32[5,8,256]{2,1,0:T(8,128)S(1)} %scan.1.own_ref), channel_id=1, source_target_pairs={{0,1},{1,0},{2,3},{3,2},{4,5},{5,4},{6,7},{7,6},{8,9},{9,8},{10,11... | collective-permute-start | bytes 122888 | tf_op jit(solution)/shard_map/ppermute | solution.py:34
  52.8 2.0 %collective-permute-start.11 = (f32[8,128]{1,0:T(8,128)S(1)}, f32[8,128]{1,0:T(8,128)S(1)}, u32[]{:S(2)}, u32[]{:S(2)}) collective-permute-start(f32[8,128]{1,0:T(8,128)S(1)} %get-tuple-element.21), channel_id=1, source_target_pairs={{0,2},{1,3},{2,0},{3,1},{4,6},{5,7},{6,4},{7,5},{8,10},{9,11},{10,... | collective-permute-start | bytes 12296 | tf_op jit(solution)/shard_map/ppermute | solution.py:34
  52.8 11.8 %collective-permute-start.12 = (f32[24,128]{1,0:T(8,128)S(1)}, f32[24,128]{1,0:T(8,128)S(1)}, u32[]{:S(2)}, u32[]{:S(2)}) collective-permute-start(f32[24,128]{1,0:T(8,128)S(1)} %get-tuple-element.22), channel_id=1, source_target_pairs={{0,8},{1,9},{2,10},{3,11},{4,12},{5,13},{6,14},{7,15},{8,16},{9,17... | collective-permute-start | bytes 36872 | tf_op jit(solution)/shard_map/ppermute | solution.py:34
  53.0 11.7 %collective-permute-start.13 = (f32[24,128]{1,0:T(8,128)S(1)}, f32[24,128]{1,0:T(8,128)S(1)}, u32[]{:S(2)}, u32[]{:S(2)}) collective-permute-start(f32[24,128]{1,0:T(8,128)S(1)} %get-tuple-element.22), channel_id=1, source_target_pairs={{0,12},{1,13},{2,14},{3,15},{4,8},{5,9},{6,10},{7,11},{8,20},{9,21... | collective-permute-start | bytes 36872 | tf_op jit(solution)/shard_map/ppermute | solution.py:34
  54.9 6.7 %collective-permute-start.14 = (f32[16,128]{1,0:T(8,128)S(1)}, f32[16,128]{1,0:T(8,128)S(1)}, u32[]{:S(2)}, u32[]{:S(2)}) collective-permute-start(f32[16,128]{1,0:T(8,128)S(1)} %constant_dynamic-update-slice_fusion.own_ref), channel_id=1, source_target_pairs={{0,248},{1,249},{2,250},{3,251},{4,252},{5,253},{6,254},{7,255},{8... | collective-permute-start | bytes 24584 | tf_op jit(solution)/shard_map/ppermute | solution.py:34
  60.1 4.5 %collective-permute-start.15 = (f32[16,128]{1,0:T(8,128)S(1)}, f32[16,128]{1,0:T(8,128)S(1)}, u32[]{:S(2)}, u32[]{:S(2)}) collective-permute-start(f32[16,128]{1,0:T(8,128)S(1)} %constant_dynamic-update-slice_fusion.own_ref), channel_id=1, source_target_pairs={{0,240},{1,241},{2,242},{3,243},{4,244},{5,245},{6,246},{7,247},{8... | collective-permute-start | bytes 24584 | tf_op jit(solution)/shard_map/ppermute | solution.py:34
